TPU v7x, 32 devices: a whole 2x2x4 slice. The times are simulated.
32 devices in a mesh: dp: 8 (over z, y), seq: 4 (over x, core).
Axes of the slice: x: 2, y: 2, z: 4, core: 2. Of those that a mesh axis runs over, the one named last changes fastest.
Arguments:
- layer_input: bfloat16 [8, 2048, 1024], P('dp', 'seq'), may hold values from -6 to 6
- segment_length: int32 [8], P('dp'), may hold values from 1434 to 2048, as said below
- output_gradient: bfloat16 [8, 2048, 1024], P('dp', 'seq'), may hold values from -6 to 6
- state_cotangent: float32 [8, 512, 1024], P('dp'), may hold values from -6 to 6
- query_key_value_weight: bfloat16 [1024, 3072], P(('dp', 'seq')), may hold values from -0.1875 to 0.1875
- state_key_value_weight: bfloat16 [1024, 2048], P(('dp', 'seq')), may hold values from -0.1875 to 0.1875
- state_query_weight: bfloat16 [1024, 1024], P(('dp', 'seq')), may hold values from -0.1875 to 0.1875
- output_weight: bfloat16 [1024, 1024], P(('dp', 'seq')), may hold values from -0.75 to 0.75
- merge_weight: bfloat16 [1024, 1024], P(('dp', 'seq')), may hold values from -0.375 to 0.375
- up_weight: bfloat16 [1024, 4096], P(('dp', 'seq')), may hold values from -0.1875 to 0.1875
- down_weight: bfloat16 [4096, 1024], P(('dp', 'seq')), may hold values from -0.09375 to 0.09375
- initial_state_learned: bfloat16 [512, 1024], P(None, ('dp', 'seq')), may hold values from -6 to 6
- attention_norm_gain: bfloat16 [1024], P(('dp', 'seq')), may hold values from 0.5 to 1.5
- feedforward_norm_gain: bfloat16 [1024], P(('dp', 'seq')), may hold values from 0.5 to 1.5
- state_norm_gain: bfloat16 [1024], P(('dp', 'seq')), may hold values from 0.5 to 1.5
- state_gate_logits: bfloat16 [1024], P(('dp', 'seq')), may hold values from -2 to 3
- relative_position_bias: bfloat16 [256], P(('dp', 'seq')), may hold values from -5 to 5
Outputs:
- layer_out: bfloat16 [8, 2048, 1024], P('dp', 'seq')
- state_out: float32 [8, 512, 1024], P('dp', 'seq')
- x_grad: float32 [8, 2048, 1024], P('dp', 'seq')
- w_qkv_grad: float32 [1024, 3072], P(('dp', 'seq'))
- w_skv_grad: float32 [1024, 2048], P(('dp', 'seq'))
- w_query_grad: float32 [1024, 1024], P(('dp', 'seq'))
- w_out_grad: float32 [1024, 1024], P(('dp', 'seq'))
- w_merge_grad: float32 [1024, 1024], P(('dp', 'seq'))
- w_up_grad: float32 [1024, 4096], P(('dp', 'seq'))
- w_down_grad: float32 [4096, 1024], P(('dp', 'seq'))
- state_init_grad: float32 [512, 1024], P(None, ('dp', 'seq'))
- gain_attn_grad: float32 [1024], P(('dp', 'seq'))
- gain_mlp_grad: float32 [1024], P(('dp', 'seq'))
- gain_state_grad: float32 [1024], P(('dp', 'seq'))
- gate_logit_grad: float32 [1024], P(('dp', 'seq'))
- rel_bias_grad: float32 [256], P(('dp', 'seq'))
Inputs may be any that keep to these rules, and one draw needn't show every extreme that they name: A segment's first segment_length tokens are valid and the rest are padding at its end. In every draw some segment is full and some has the fewest valid tokens.
All inputs are finite; a program needn't handle non-finite values.
Results may differ from a plain program's by a relative error of at most 0.025.
Values may be sent and summed in bfloat16 or wider, within the bound.
No kernel may reach another device: no remote copies, remote signals or barrier semaphores. Data moves between devices by JAX's collectives and lax.ppermute only.
A program may use at most 384 MiB of HBM per device.

v0:
```python
from functools import partial

import jax
import jax.numpy as jnp
import numpy as np
from jax import lax
from jax.sharding import PartitionSpec as P

HEADS = 8
HEAD = 128
BUCKETS = 32
MAX_DIST = 128


EPS = 1e-05
NEG = -1e30
HIGH = lax.Precision.HIGHEST


def shortened(shard):
    return jax.tree.map(lambda a: a.astype(jnp.bfloat16) if a.dtype == jnp.float32 else a, shard)


def from_behind(block, axis, distance):
    devices = range(lax.axis_size(axis))
    route = [(i - distance, i) for i in devices if i - distance in devices]
    return lax.ppermute(block, axis, route)


def from_root(shard, axis, root):
    mine = lax.axis_index(axis) == root
    return lax.psum(jnp.where(mine, shard, jnp.zeros_like(shard)), axis)


def bucket_ids(length, buckets, max_dist):
    dist = np.arange(length)[:, None] - np.arange(length)[None, :]
    dist = np.maximum(dist, 0)
    exact = buckets // 2
    scaled = np.log(np.maximum(dist, exact) / exact) / np.log(max_dist / exact) * (buckets - exact)
    far = np.minimum(exact + np.floor(scaled).astype(np.int32), buckets - 1)
    return np.where(dist < exact, dist, far).astype(np.int32)


def layer_norm(value, gain):
    mean = jnp.mean(value, axis=-1, keepdims=True)
    centered = value - mean
    spread = jnp.mean(centered * centered, axis=-1, keepdims=True)
    return centered * lax.rsqrt(spread + EPS) * gain


def hold(kept, value):
    return kept


def bias_grid(table, bucket):
    rows = bucket.shape[0]
    block_rows = min(128, rows)
    ids = jnp.asarray(bucket).reshape(rows // block_rows, block_rows, rows)

    def one_block(block_ids):
        onehot = (block_ids[..., None] == jnp.arange(table.shape[1], dtype=jnp.int32)).astype(
            jnp.float32
        )
        return jnp.einsum("hb,rnb->hrn", table, onehot, precision=HIGH)

    grid = lax.map(one_block, ids)
    return jnp.transpose(grid, (1, 0, 2, 3)).reshape(table.shape[0], rows, rows)


def bias_grad(grid_grad, bucket, buckets):
    heads, rows, _ = grid_grad.shape
    block_rows = min(128, rows)
    blocks = rows // block_rows
    ids = jnp.asarray(bucket).reshape(blocks, block_rows, rows)
    pieces = jnp.transpose(grid_grad.reshape(heads, blocks, block_rows, rows), (1, 0, 2, 3))

    def one_block(total, pair):
        block_ids, block_grad = pair
        onehot = (block_ids[..., None] == jnp.arange(buckets, dtype=jnp.int32)).astype(jnp.float32)
        return (total + jnp.einsum("hrn,rnb->hb", block_grad, onehot, precision=HIGH), None)

    total, _ = lax.scan(one_block, jnp.zeros((heads, buckets), jnp.float32), (ids, pieces))
    return total


def attend_scores(query, first_keys, second_keys, first_add, first_allow, second_allow):
    first = (
        jnp.einsum("lhe,nhe->hln", query, first_keys, preferred_element_type=jnp.float32)
        + first_add
    )
    first = jnp.where(first_allow, first, NEG)
    second = jnp.einsum("lhe,nhe->hln", query, second_keys, preferred_element_type=jnp.float32)
    second = jnp.where(second_allow, second, NEG)
    return (first, second)


def attend_forward(
    query,
    first_keys,
    first_values,
    second_keys,
    second_values,
    first_add,
    first_allow,
    second_allow,
):
    first, second = attend_scores(
        query, first_keys, second_keys, first_add, first_allow, second_allow
    )
    top = jnp.maximum(
        jnp.max(first, axis=-1, keepdims=True), jnp.max(second, axis=-1, keepdims=True)
    )
    total = jnp.sum(jnp.exp(first - top), axis=-1, keepdims=True) + jnp.sum(
        jnp.exp(second - top), axis=-1, keepdims=True
    )
    lse = top + jnp.log(total)
    first_prob = jnp.exp(first - lse).astype(jnp.bfloat16)
    second_prob = jnp.exp(second - lse).astype(jnp.bfloat16)
    mixed = jnp.einsum("hln,nhe->lhe", first_prob, first_values, preferred_element_type=jnp.float32)
    mixed = mixed + jnp.einsum(
        "hln,nhe->lhe", second_prob, second_values, preferred_element_type=jnp.float32
    )
    return (mixed.reshape(mixed.shape[0], -1).astype(jnp.bfloat16), lse)


def attend_backward(
    query,
    first_keys,
    first_values,
    second_keys,
    second_values,
    first_add,
    first_allow,
    second_allow,
    lse,
    grad_mixed,
):
    first, second = attend_scores(
        query, first_keys, second_keys, first_add, first_allow, second_allow
    )
    first_prob = jnp.exp(first - lse)
    second_prob = jnp.exp(second - lse)
    grad_first = jnp.einsum(
        "lhe,nhe->hln", grad_mixed, first_values, preferred_element_type=jnp.float32
    )
    grad_second = jnp.einsum(
        "lhe,nhe->hln", grad_mixed, second_values, preferred_element_type=jnp.float32
    )
    first_vgrad = jnp.einsum(
        "hln,lhe->nhe",
        first_prob.astype(jnp.bfloat16),
        grad_mixed,
        preferred_element_type=jnp.float32,
    )
    second_vgrad = jnp.einsum(
        "hln,lhe->nhe",
        second_prob.astype(jnp.bfloat16),
        grad_mixed,
        preferred_element_type=jnp.float32,
    )
    inner = jnp.sum(first_prob * grad_first, axis=-1, keepdims=True) + jnp.sum(
        second_prob * grad_second, axis=-1, keepdims=True
    )
    first_score = first_prob * (grad_first - inner)
    second_score = second_prob * (grad_second - inner)
    first_low = first_score.astype(jnp.bfloat16)
    second_low = second_score.astype(jnp.bfloat16)
    query_grad = jnp.einsum(
        "hln,nhe->lhe", first_low, first_keys, preferred_element_type=jnp.float32
    )
    query_grad = query_grad + jnp.einsum(
        "hln,nhe->lhe", second_low, second_keys, preferred_element_type=jnp.float32
    )
    first_kgrad = jnp.einsum("hln,lhe->nhe", first_low, query, preferred_element_type=jnp.float32)
    second_kgrad = jnp.einsum("hln,lhe->nhe", second_low, query, preferred_element_type=jnp.float32)
    return (query_grad, first_kgrad, first_vgrad, second_kgrad, second_vgrad, first_score)


def fetch_forward(
    query_key_value_weight,
    state_key_value_weight,
    state_query_weight,
    output_weight,
    merge_weight,
    up_weight,
    down_weight,
    initial_state_learned,
    attention_norm_gain,
    feedforward_norm_gain,
    state_norm_gain,
    state_gate_logits,
    relative_position_bias,
):
    return (
        lax.all_gather(query_key_value_weight, ("dp", "seq"), axis=0, tiled=True),
        lax.all_gather(state_key_value_weight, ("dp", "seq"), axis=0, tiled=True),
        lax.all_gather(state_query_weight, ("dp", "seq"), axis=0, tiled=True),
        lax.all_gather(output_weight, ("dp", "seq"), axis=0, tiled=True),
        lax.all_gather(merge_weight, ("dp", "seq"), axis=0, tiled=True),
        lax.all_gather(up_weight, ("dp", "seq"), axis=0, tiled=True),
        lax.all_gather(down_weight, ("dp", "seq"), axis=0, tiled=True),
        lax.all_gather(initial_state_learned, ("dp", "seq"), axis=1, tiled=True),
        lax.all_gather(attention_norm_gain, ("dp", "seq"), axis=0, tiled=True),
        lax.all_gather(feedforward_norm_gain, ("dp", "seq"), axis=0, tiled=True),
        lax.all_gather(state_norm_gain, ("dp", "seq"), axis=0, tiled=True),
        lax.all_gather(state_gate_logits, ("dp", "seq"), axis=0, tiled=True),
        lax.all_gather(relative_position_bias, ("dp", "seq"), axis=0, tiled=True),
    )


def fetch_backward(
    query_key_value_weight,
    state_key_value_weight,
    state_query_weight,
    output_weight,
    merge_weight,
    up_weight,
    down_weight,
    initial_state_learned,
    attention_norm_gain,
    feedforward_norm_gain,
    state_norm_gain,
    state_gate_logits,
    relative_position_bias,
):
    return (
        lax.all_gather(query_key_value_weight, ("dp", "seq"), axis=0, tiled=True),
        lax.all_gather(state_key_value_weight, ("dp", "seq"), axis=0, tiled=True),
        lax.all_gather(state_query_weight, ("dp", "seq"), axis=0, tiled=True),
        lax.all_gather(output_weight, ("dp", "seq"), axis=0, tiled=True),
        lax.all_gather(merge_weight, ("dp", "seq"), axis=0, tiled=True),
        lax.all_gather(up_weight, ("dp", "seq"), axis=0, tiled=True),
        lax.all_gather(down_weight, ("dp", "seq"), axis=0, tiled=True),
        lax.all_gather(initial_state_learned, ("dp", "seq"), axis=1, tiled=True),
        lax.all_gather(attention_norm_gain, ("dp", "seq"), axis=0, tiled=True),
        lax.all_gather(feedforward_norm_gain, ("dp", "seq"), axis=0, tiled=True),
        lax.all_gather(state_norm_gain, ("dp", "seq"), axis=0, tiled=True),
        lax.all_gather(state_gate_logits, ("dp", "seq"), axis=0, tiled=True),
        lax.all_gather(relative_position_bias, ("dp", "seq"), axis=0, tiled=True),
    )


def reduce_grads(
    qkv_grad,
    state_key_value_gradient,
    query_grad,
    output_gradient,
    merge_grad,
    up_grad,
    down_grad,
    init_grad,
    attn_gain_grad,
    mlp_gain_grad,
    state_gain_grad,
    gate_grad,
    table_grad,
):
    return (
        lax.psum_scatter(qkv_grad, ("dp", "seq"), scatter_dimension=0, tiled=True),
        lax.psum_scatter(state_key_value_gradient, ("dp", "seq"), scatter_dimension=0, tiled=True),
        lax.psum_scatter(query_grad, ("dp", "seq"), scatter_dimension=0, tiled=True),
        lax.psum_scatter(output_gradient, ("dp", "seq"), scatter_dimension=0, tiled=True),
        lax.psum_scatter(merge_grad, ("dp", "seq"), scatter_dimension=0, tiled=True),
        lax.psum_scatter(up_grad, ("dp", "seq"), scatter_dimension=0, tiled=True),
        lax.psum_scatter(down_grad, ("dp", "seq"), scatter_dimension=0, tiled=True),
        lax.psum_scatter(init_grad, ("dp", "seq"), scatter_dimension=1, tiled=True),
        lax.psum_scatter(attn_gain_grad, ("dp", "seq"), scatter_dimension=0, tiled=True),
        lax.psum_scatter(mlp_gain_grad, ("dp", "seq"), scatter_dimension=0, tiled=True),
        lax.psum_scatter(state_gain_grad, ("dp", "seq"), scatter_dimension=0, tiled=True),
        lax.psum_scatter(gate_grad, ("dp", "seq"), scatter_dimension=0, tiled=True),
        lax.psum_scatter(table_grad, ("dp", "seq"), scatter_dimension=0, tiled=True),
    )


def body(
    layer_input,
    segment_length,
    output_gradient,
    state_cotangent,
    query_key_value_weight,
    state_key_value_weight,
    state_query_weight,
    output_weight,
    merge_weight,
    up_weight,
    down_weight,
    initial_state_learned,
    attention_norm_gain,
    feedforward_norm_gain,
    state_norm_gain,
    state_gate_logits,
    relative_position_bias,
):
    weights_fwd = fetch_forward(
        query_key_value_weight,
        state_key_value_weight,
        state_query_weight,
        output_weight,
        merge_weight,
        up_weight,
        down_weight,
        initial_state_learned,
        attention_norm_gain,
        feedforward_norm_gain,
        state_norm_gain,
        state_gate_logits,
        relative_position_bias,
    )
    (
        qkv_full,
        state_key_value_gathered,
        query_full,
        out_full,
        merge_full,
        up_full,
        down_full,
        init_full,
        attn_gain,
        mlp_gain,
        state_gain,
        gate_raw,
        bias_flat,
    ) = weights_fwd
    segs, rows, width = layer_input.shape
    states = init_full.shape[0]
    place = lax.axis_index("seq")
    count = lax.axis_size("seq")
    scale = HEAD ** (-0.5)
    single_float = jnp.float32
    bf16 = jnp.bfloat16
    attn_g = attn_gain.astype(single_float)
    mlp_g = mlp_gain.astype(single_float)
    state_g = state_gain.astype(single_float)
    gate = jax.nn.sigmoid(gate_raw.astype(single_float))
    init_f = init_full.astype(single_float)
    table = bias_flat.astype(single_float).reshape(HEADS, -1)
    bucket = bucket_ids(rows, BUCKETS, MAX_DIST)
    causal = jnp.asarray(np.tril(np.ones((rows, rows), dtype=bool)))
    bias = bias_grid(table, bucket)
    all_allowed = jnp.ones((1, 1, 1), dtype=bool)
    valid = (place * rows + jnp.arange(rows, dtype=jnp.int32))[None, :] < segment_length[:, None]
    tokens = layer_input.astype(single_float).reshape(segs * rows, width)
    normed = layer_norm(tokens, attn_g).astype(bf16)
    qkv = jnp.dot(normed, qkv_full, preferred_element_type=single_float)
    query = (qkv[:, :width] * scale).astype(bf16).reshape(segs, rows, HEADS, HEAD)
    keys = qkv[:, width : 2 * width].astype(bf16).reshape(segs, rows, HEADS, HEAD)
    values = qkv[:, 2 * width :].astype(bf16).reshape(segs, rows, HEADS, HEAD)

    def advance(carry):
        carried_norm = layer_norm(carry, state_g).astype(bf16)
        carried_state_flat = carried_norm.reshape(segs * states, width)
        carried_key_value = jnp.dot(
            carried_state_flat, state_key_value_gathered, preferred_element_type=single_float
        )
        carried_keys = carried_key_value[:, :width].astype(bf16).reshape(segs, states, HEADS, HEAD)
        carried_values = (
            carried_key_value[:, width:].astype(bf16).reshape(segs, states, HEADS, HEAD)
        )
        state_query = (
            (jnp.dot(carried_state_flat, query_full, preferred_element_type=single_float) * scale)
            .astype(bf16)
            .reshape(segs, states, HEADS, HEAD)
        )

        def update_one(pair):
            seg_squery, seg_ckeys, seg_cvalues, seg_keys, seg_values, seg_valid = pair
            return attend_forward(
                seg_squery,
                seg_ckeys,
                seg_cvalues,
                seg_keys,
                seg_values,
                0.0,
                all_allowed,
                seg_valid[None, None, :],
            )

        update, update_lse = lax.map(
            update_one, (state_query, carried_keys, carried_values, keys, values, valid)
        )
        candidate = jnp.dot(
            update.reshape(segs * states, width), merge_full, preferred_element_type=single_float
        ).reshape(segs, states, width)
        new_state = gate * carry + (1.0 - gate) * candidate
        return (
            new_state,
            carried_norm,
            carried_keys,
            carried_values,
            state_query,
            update,
            update_lse,
            candidate,
        )

    zero_state = jnp.zeros((segs, states, width), single_float)
    zero_low = jnp.zeros((segs, states, width), bf16)
    zero_heads = jnp.zeros((segs, states, HEADS, HEAD), bf16)
    zero_lse = jnp.zeros((segs, HEADS, states, 1), single_float)
    stash = (
        zero_state,
        zero_low,
        zero_heads,
        zero_heads,
        zero_heads,
        zero_low,
        zero_lse,
        zero_state,
    )
    carry = jnp.broadcast_to(init_f, (segs, states, width))
    for section in range(count):
        stash = lax.cond(place == section, advance, partial(hold, stash), carry)
        if section + 1 < count:
            moved = from_behind(shortened(stash[0]), "seq", 1)
            carry = jnp.where(place == section + 1, moved, carry)
    (
        final,
        carried_norm,
        carried_keys,
        carried_values,
        state_query,
        update,
        update_lse,
        candidate,
    ) = stash
    carried_state_flat = carried_norm.reshape(segs * states, width)
    update_flat = update.reshape(segs * states, width)
    everyone = from_root(shortened(final), "seq", count - 1).astype(final.dtype)
    share = states // count
    state_out = lax.dynamic_slice_in_dim(everyone, place * share, share, 1)

    def token_one(pair):
        seg_query, seg_keys, seg_values, seg_ckeys, seg_cvalues, seg_valid = pair
        allow_own = jnp.logical_and(causal, seg_valid[None, :])[None]
        return attend_forward(
            seg_query, seg_keys, seg_values, seg_ckeys, seg_cvalues, bias, allow_own, all_allowed
        )

    mixed, token_lse = lax.map(
        token_one, (query, keys, values, carried_keys, carried_values, valid)
    )
    mixed_flat = mixed.reshape(segs * rows, width)
    attn = jnp.dot(mixed_flat, out_full, preferred_element_type=single_float)
    resid = tokens + attn
    hidden = layer_norm(resid, mlp_g).astype(bf16)
    up = jnp.dot(hidden, up_full, preferred_element_type=single_float)
    act = jax.nn.gelu(up, approximate=True).astype(bf16)
    result = resid + jnp.dot(act, down_full, preferred_element_type=single_float)
    layer_out = result.astype(bf16).reshape(segs, rows, width)
    layer_weights_backward = fetch_backward(
        query_key_value_weight,
        state_key_value_weight,
        state_query_weight,
        output_weight,
        merge_weight,
        up_weight,
        down_weight,
        initial_state_learned,
        attention_norm_gain,
        feedforward_norm_gain,
        state_norm_gain,
        state_gate_logits,
        relative_position_bias,
    )
    (
        query_key_value_backward,
        state_key_value_backward,
        state_query_backward,
        output_weight_backward,
        merge_weight_backward,
        up_weight_backward,
        down_weight_backward,
    ) = layer_weights_backward[:7]
    grad_result = output_gradient.reshape(segs * rows, width)
    down_grad = jnp.einsum("rf,rd->fd", act, grad_result, preferred_element_type=single_float)
    grad_act = jnp.einsum(
        "rd,fd->rf", grad_result, down_weight_backward, preferred_element_type=single_float
    )
    _, gelu_back = jax.vjp(partial(jax.nn.gelu, approximate=True), up)
    grad_up = gelu_back(grad_act)[0].astype(bf16)
    up_grad = jnp.einsum("rd,rf->df", hidden, grad_up, preferred_element_type=single_float)
    grad_hidden = jnp.einsum(
        "rf,df->rd", grad_up, up_weight_backward, preferred_element_type=single_float
    )
    _, mlp_norm_back = jax.vjp(layer_norm, resid, mlp_g)
    resid_part, mlp_gain_grad = mlp_norm_back(grad_hidden)
    grad_resid = output_gradient.astype(single_float).reshape(segs * rows, width) + resid_part
    grad_attn = grad_resid.astype(bf16)
    out_weight_grad = jnp.einsum(
        "rd,re->de", mixed_flat, grad_attn, preferred_element_type=single_float
    )
    grad_mixed = (
        jnp.einsum(
            "re,de->rd", grad_attn, output_weight_backward, preferred_element_type=single_float
        )
        .astype(bf16)
        .reshape(segs, rows, HEADS, HEAD)
    )

    def token_back(total, pair):
        seg_query, seg_keys, seg_values, seg_ckeys, seg_cvalues, seg_valid, seg_lse, seg_grad = pair
        allow_own = jnp.logical_and(causal, seg_valid[None, :])[None]
        grads = attend_backward(
            seg_query,
            seg_keys,
            seg_values,
            seg_ckeys,
            seg_cvalues,
            bias,
            allow_own,
            all_allowed,
            seg_lse,
            seg_grad,
        )
        return (total + grads[5], grads[:5])

    bias_total, (grad_query, grad_keys, grad_values, grad_ckeys, grad_cvalues) = lax.scan(
        token_back,
        jnp.zeros_like(bias),
        (query, keys, values, carried_keys, carried_values, valid, token_lse, grad_mixed),
    )
    _, carry_norm_back = jax.vjp(layer_norm, carry, state_g)

    def retreat(adjoint):
        grad_cand = ((1.0 - gate) * adjoint).astype(bf16).reshape(segs * states, width)
        merge_term = jnp.einsum(
            "rd,re->de", update_flat, grad_cand, preferred_element_type=single_float
        )
        grad_update = (
            jnp.einsum(
                "re,de->rd", grad_cand, merge_weight_backward, preferred_element_type=single_float
            )
            .astype(bf16)
            .reshape(segs, states, HEADS, HEAD)
        )

        def state_one(pair):
            (
                seg_squery,
                seg_ckeys,
                seg_cvalues,
                seg_keys,
                seg_values,
                seg_valid,
                seg_lse,
                seg_grad,
            ) = pair
            grads = attend_backward(
                seg_squery,
                seg_ckeys,
                seg_cvalues,
                seg_keys,
                seg_values,
                0.0,
                all_allowed,
                seg_valid[None, None, :],
                seg_lse,
                seg_grad,
            )
            return grads[:5]

        grad_squery, grad_ck_two, grad_cv_two, grad_k_two, grad_v_two = lax.map(
            state_one,
            (
                state_query,
                carried_keys,
                carried_values,
                keys,
                values,
                valid,
                update_lse,
                grad_update,
            ),
        )
        carried_key_value_gradient = jnp.concatenate(
            [
                (grad_ckeys + grad_ck_two).reshape(segs * states, width),
                (grad_cvalues + grad_cv_two).reshape(segs * states, width),
            ],
            axis=1,
        ).astype(bf16)
        squery_low = (grad_squery * scale).reshape(segs * states, width).astype(bf16)
        state_key_value_summand = jnp.einsum(
            "bp,bx->px",
            carried_state_flat,
            carried_key_value_gradient,
            preferred_element_type=single_float,
        )
        query_term = jnp.einsum(
            "bp,bx->px", carried_state_flat, squery_low, preferred_element_type=single_float
        )
        carried_norm_gradient = jnp.einsum(
            "qh,ch->qc",
            carried_key_value_gradient,
            state_key_value_backward,
            preferred_element_type=single_float,
        )
        carried_norm_gradient = carried_norm_gradient + jnp.einsum(
            "qh,ch->qc", squery_low, state_query_backward, preferred_element_type=single_float
        )
        grad_carried, gain_term = carry_norm_back(
            carried_norm_gradient.reshape(segs, states, width)
        )
        grad_before = grad_carried + gate * adjoint
        gate_sum = jnp.sum(adjoint * (carry - candidate), axis=(0, 1))
        return (
            grad_before,
            merge_term,
            state_key_value_summand,
            query_term,
            gain_term,
            gate_sum,
            grad_k_two,
            grad_v_two,
        )

    zero_rows = jnp.zeros((segs, rows, HEADS, HEAD), single_float)
    back_stash = (
        zero_state,
        jnp.zeros((width, width), single_float),
        jnp.zeros((width, 2 * width), single_float),
        jnp.zeros((width, width), single_float),
        jnp.zeros((width,), single_float),
        jnp.zeros((width,), single_float),
        zero_rows,
        zero_rows,
    )
    adjoint = jnp.where(place == count - 1, state_cotangent, 0.0)
    for section in reversed(range(count)):
        back_stash = lax.cond(place == section, retreat, partial(hold, back_stash), adjoint)
        if section > 0:
            moved_back = from_behind(shortened(back_stash[0]), "seq", -1)
            adjoint = jnp.where(place == section - 1, moved_back, adjoint)
    (
        grad_first_state,
        merge_grad,
        state_key_value_gradient,
        query_grad,
        state_gain_grad,
        gate_sum,
        grad_keys_two,
        grad_values_two,
    ) = back_stash
    gate_grad = gate_sum * gate * (1.0 - gate)
    init_grad = jnp.where(place == 0, jnp.sum(grad_first_state, axis=0), 0.0)
    grad_qkv = jnp.concatenate(
        [
            (grad_query * scale).reshape(segs * rows, width),
            (grad_keys + grad_keys_two).reshape(segs * rows, width),
            (grad_values + grad_values_two).reshape(segs * rows, width),
        ],
        axis=1,
    ).astype(bf16)
    qkv_grad = jnp.einsum("bp,bx->px", normed, grad_qkv, preferred_element_type=single_float)
    grad_normed = jnp.einsum(
        "qh,ch->qc", grad_qkv, query_key_value_backward, preferred_element_type=single_float
    )
    _, token_norm_back = jax.vjp(layer_norm, tokens, attn_g)
    token_part, attn_gain_grad = token_norm_back(grad_normed)
    x_grad = (grad_resid + token_part).reshape(segs, rows, width)
    table_grad = bias_grad(bias_total, bucket, table.shape[1]).reshape(-1)
    shards = reduce_grads(
        qkv_grad,
        state_key_value_gradient,
        query_grad,
        out_weight_grad,
        merge_grad,
        up_grad,
        down_grad,
        init_grad,
        attn_gain_grad,
        mlp_gain_grad,
        state_gain_grad,
        gate_grad,
        table_grad,
    )
    return (layer_out, state_out, x_grad) + tuple(shards)


def solution(mesh):
    return jax.shard_map(
        body,
        mesh=mesh,
        in_specs=(
            P("dp", "seq", None),
            P("dp"),
            P("dp", "seq", None),
            P("dp", None, None),
            P(("dp", "seq"), None),
            P(("dp", "seq"), None),
            P(("dp", "seq"), None),
            P(("dp", "seq"), None),
            P(("dp", "seq"), None),
            P(("dp", "seq"), None),
            P(("dp", "seq"), None),
            P(None, ("dp", "seq")),
            P(("dp", "seq")),
            P(("dp", "seq")),
            P(("dp", "seq")),
            P(("dp", "seq")),
            P(("dp", "seq")),
        ),
        out_specs=(
            P("dp", "seq", None),
            P("dp", "seq", None),
            P("dp", "seq", None),
            P(("dp", "seq"), None),
            P(("dp", "seq"), None),
            P(("dp", "seq"), None),
            P(("dp", "seq"), None),
            P(("dp", "seq"), None),
            P(("dp", "seq"), None),
            P(("dp", "seq"), None),
            P(None, ("dp", "seq")),
            P(("dp", "seq")),
            P(("dp", "seq")),
            P(("dp", "seq")),
            P(("dp", "seq")),
            P(("dp", "seq")),
        ),
        check_vma=False,
    )
```

profile of v0, /device:TPU:0, one launch (start us, length us, event | category | flops | bytes accessed | tf_op | source)
XLA Modules:
  0.0 2366.7 jit_solution(9065032464817926133)
XLA Ops:
  17.6 42.2 %all-reduce.11 = (bf16[256]{0:T(256)(128)(2,1)S(1)}, bf16[1024]{0:T(1024)(128)(2,1)S(1)}, bf16[1024]{0:T(1024)(128)(2,1)S(1)}, bf16[1024]{0:T(1024)(128)(2,1)S(1)}, bf16[1024]{0:T(1024)(128)(2,1)S(1)}) all-reduce(bf16[256]{0:T(256)(128)(2,1)S(1)} %dynamic-update-slice.1, ...), channel_id=1, replica_groups=mesh['dp'=8,'seq'=4] {'dp','seq'}, use_global_device_ids=true, to_apply=%add.1 | all-reduce | flops 4352 | bytes 17408
  70.3 68.6 %all-gather.9.cloned.1.call-done = bf16[1024,3072]{1,0:T(8,128)(2,1)} async-done(((bf16[32,3072]{1,0:T(8,128)(2,1)}), bf16[1024,3072]{1,0:T(8,128)(2,1)}) %all-gather.9.cloned.1.call-update) | async-done | bytes 6291472 | tf_op jit(solution)/shard_map/all_gather | solution.py:195
  150.8 45.9 %all-gather.15.cloned.1.call-done = bf16[1024,1024]{1,0:T(8,128)(2,1)} async-done(((bf16[32,1024]{1,0:T(8,128)(2,1)}), bf16[1024,1024]{1,0:T(8,128)(2,1)}) %all-gather.15.cloned.1.call-update) | async-done | bytes 2097168 | tf_op jit(solution)/shard_map/all_gather | solution.py:197
  196.7 58.0 %all-gather.17.cloned.1.call-done = bf16[1024,1024]{1,0:T(8,128)(2,1)} async-done(((bf16[32,1024]{1,0:T(8,128)(2,1)}), bf16[1024,1024]{1,0:T(8,128)(2,1)}) %all-gather.17.cloned.1.call-update) | async-done | bytes 2097168 | tf_op jit(solution)/shard_map/all_gather | solution.py:199
  254.6 63.6 %all-gather.13.cloned.1.call-done = bf16[1024,2048]{1,0:T(8,128)(2,1)} async-done(((bf16[32,2048]{1,0:T(8,128)(2,1)}), bf16[1024,2048]{1,0:T(8,128)(2,1)}) %all-gather.13.cloned.1.call-update) | async-done | bytes 4194320 | tf_op jit(solution)/shard_map/all_gather | solution.py:196
  318.3 44.1 %conditional.8 = (f32[1,512,1024]{2,1,0:T(8,128)}, bf16[1,512,1024]{2,1,0:T(8,128)(2,1)}, bf16[1,512,8,128]{3,2,1,0:T(8,128)(2,1)S(1)}, bf16[1,512,8,128]{3,2,1,...) conditional(s32[]{:T(128)} %convert_element_type.404, ...), branch_computations={%region_5.6_spmd, %region_6.13_spmd} | conditional | flops 6478624256 | bytes 170206080 | solution.py:412
  380.6 41.3 %collective-permute-start.1 = (bf16[1,512,1024]{1,2,0:T(8,128)(2,1)}, bf16[1,512,1024]{1,2,0:T(8,128)(2,1)}, u32[]{:S(2)}, u32[]{:S(2)}) collective-permute-start(bf16[1,512,1024]{1,2,0:T(8,128)(2,1)} %copy.282), channel_id=1, source_target_pairs={{0,1},{1,2},{2,3},{4,5},{5,6},{6,7},{8,9},{9,10},{10,11},{12,13},{... | collective-permute-start | bytes 3145736 | tf_op jit(solution)/shard_map/ppermute | solution.py:27
  421.9 19.8 while.18
  612.6 15.7 subtract_multiply_fusion
  632.4 22.6 conditional.12
  659.0 42.0 %collective-permute-done.3 = bf16[1,512,1024]{1,2,0:T(8,128)(2,1)S(1)} collective-permute-done((bf16[1,512,1024]{1,2,0:T(8,128)(2,1)}, bf16[1,512,1024]{1,2,0:T(8,128)(2,1)S(1)}, u32[]{:S(2)}, u32[]{:S(2)}) %collective-permute-start.3) | collective-permute-done | bytes 1048608 | tf_op jit(solution)/shard_map/ppermute | solution.py:27
  715.1 15.0 collective-permute-done.4
  749.5 274.8 %collective-permute-done.5 = bf16[1,512,1024]{2,1,0:T(8,128)(2,1)} collective-permute-done((bf16[1,512,1024]{2,1,0:T(8,128)(2,1)}, bf16[1,512,1024]{2,1,0:T(8,128)(2,1)}, u32[]{:S(2)}, u32[]{:S(2)}) %collective-permute-start.5) | collective-permute-done | bytes 1048608 | tf_op jit(solution)/shard_map/ppermute | solution.py:27
  1027.2 99.3 %conditional.15 = (f32[1024,1024]{0,1:T(8,128)}, f32[1024,2048]{0,1:T(8,128)}, f32[1024,1024]{0,1:T(8,128)}, f32[1024]{0:T(1024)S(1)}, f32[1024]{0:T(1024)S(1)},...) conditional(s32[]{:T(128)} %convert_element_type.404, ...), branch_computations={%region_73.74_spmd, %region_74.81_spmd} | conditional | flops 14029943808 | bytes 450071616 | solution.py:630
  1080.2 15.5 multiply_convert_fusion.20
  1231.4 27.9 %while.24 = (s32[]{:T(128)}, f32[8,32]{1,0:T(8,128)S(1)}, f32[4,8,128,512]{2,1,3,0:T(8,128)}, s32[4,128,512]{1,2,0:T(8,128)}, s32[]{:T(128)}, /*index=5*/s32[]{:T(128)}) while((s32[]{:T(128)}, f32[8,32]{1,0:T(8,128)S(1)}, f32[4,8,128,512]{2,1,3,0:T(8,128)}, s32[4,128,512]{1,2,0:T(8,128)}, s32[]{:T(128)}, ...), condition=%wide.region_98.99_spmd.clone, body=%wide.region_97.98_spmd.clone.sunk | while | flops 203424256 | bytes 2885727 | solution.py:82
  1281.1 38.3 %all-reduce.10 = (f32[1024]{0:T(1024)S(1)}, f32[1024]{0:T(1024)S(1)}, f32[1024]{0:T(1024)S(1)}, f32[1024]{0:T(1024)S(1)}, f32[256]{0:T(256)S(1)}) all-reduce(f32[1024]{0:T(1024)S(1)} %get-tuple-element.1401, f32[1024]{0:T(1024)S(1)} %copy-done.155, ...), channel_id=10, replica_groups=mesh['dp'=8,'seq'=4] {'dp','seq'}, use_global_device_ids=true, to_apply=%region_92.93.clone | all-reduce | flops 4352 | bytes 34816
  1326.7 76.2 %reduce-scatter.15.cloned.1.call-done = f32[32,1024]{1,0:T(8,128)} async-done(((f32[1024,1024]{1,0:T(8,128)}), f32[32,1024]{1,0:T(8,128)}) %reduce-scatter.15.cloned.1.call-update) | async-done | bytes 131088 | tf_op jit(solution)/shard_map/reduce_scatter | solution.py:262
  1402.9 139.6 %reduce-scatter.13.cloned.1.call-done = f32[32,1024]{1,0:T(8,128)} async-done(((f32[1024,1024]{1,0:T(8,128)}), f32[32,1024]{1,0:T(8,128)}) %reduce-scatter.13.cloned.1.call-update) | async-done | bytes 131088 | tf_op jit(solution)/shard_map/reduce_scatter | solution.py:261
  1542.5 140.0 %reduce-scatter.17.cloned.1.call-done = f32[32,1024]{1,0:T(8,128)} async-done(((f32[1024,1024]{1,0:T(8,128)}), f32[32,1024]{1,0:T(8,128)}) %reduce-scatter.17.cloned.1.call-update) | async-done | bytes 131088 | tf_op jit(solution)/shard_map/reduce_scatter | solution.py:263
  1682.5 147.4 %reduce-scatter.11.cloned.1.call-done = f32[32,2048]{1,0:T(8,128)} async-done(((f32[1024,2048]{1,0:T(8,128)}), f32[32,2048]{1,0:T(8,128)}) %reduce-scatter.11.cloned.1.call-update) | async-done | bytes 262160 | tf_op jit(solution)/shard_map/reduce_scatter | solution.py:260
  1829.9 157.8 %reduce-scatter.9.cloned.1.call-done = f32[32,3072]{1,0:T(8,128)} async-done(((f32[1024,3072]{1,0:T(8,128)}), f32[32,3072]{1,0:T(8,128)}) %reduce-scatter.9.cloned.1.call-update) | async-done | bytes 393232 | tf_op jit(solution)/shard_map/reduce_scatter | solution.py:259
  1987.7 184.8 %reduce-scatter.21.cloned.1.call-done = f32[128,1024]{1,0:T(8,128)} async-done(((f32[4096,1024]{1,0:T(8,128)}), f32[128,1024]{1,0:T(8,128)}) %reduce-scatter.21.cloned.1.call-update) | async-done | bytes 524304 | tf_op jit(solution)/shard_map/reduce_scatter | solution.py:265
  2172.5 187.4 %reduce-scatter.19.cloned.1.call-done = f32[32,4096]{1,0:T(8,128)} async-done(((f32[1024,4096]{1,0:T(8,128)}), f32[32,4096]{1,0:T(8,128)}) %reduce-scatter.19.cloned.1.call-update) | async-done | bytes 524304 | tf_op jit(solution)/shard_map/reduce_scatter | solution.py:264
  (439 shorter events, 590.4 us)
Async XLA Ops:
  7.2 60.3 %all-gather.11.cloned.1.call-start = ((), (), s32[]{:S(2)}) async-start(), calls=%async_computation.9 | async-start | bytes 1081344 | tf_op jit(solution)/shard_map/all_gather | solution.py:202
  7.9 131.0 %all-gather.9.cloned.1.call-start = ((), (), s32[]{:S(2)}) async-start(), calls=%async_computation.8 | async-start | bytes 6488064 | tf_op jit(solution)/shard_map/all_gather | solution.py:195
  8.7 188.0 %all-gather.15.cloned.1.call-start = ((), (), s32[]{:S(2)}) async-start(), calls=%async_computation.11 | async-start | bytes 2162688 | tf_op jit(solution)/shard_map/all_gather | solution.py:197
  9.4 245.2 %all-gather.17.cloned.1.call-start = ((), (), s32[]{:S(2)}) async-start(), calls=%async_computation.12 | async-start | bytes 2162688 | tf_op jit(solution)/shard_map/all_gather | solution.py:199
  10.0 308.3 %all-gather.13.cloned.1.call-start = ((), (), s32[]{:S(2)}) async-start(), calls=%async_computation.10 | async-start | bytes 4325376 | tf_op jit(solution)/shard_map/all_gather | solution.py:196
  10.6 530.3 %all-gather.19.cloned.1.call-start = ((), (), s32[]{:S(2)}) async-start(), calls=%async_computation.13 | async-start | bytes 2162688 | tf_op jit(solution)/shard_map/all_gather | solution.py:198
  11.1 538.8 %all-gather.21.cloned.1.call-start = ((), (), s32[]{:S(2)}) async-start(), calls=%async_computation.14 | async-start | bytes 8650752 | tf_op jit(solution)/shard_map/all_gather | solution.py:200
  11.9 550.0 %all-gather.23.cloned.1.call-start = ((), (), s32[]{:S(2)}) async-start(), calls=%async_computation.15 | async-start | bytes 8650752 | tf_op jit(solution)/shard_map/all_gather | solution.py:201
  12.6 1206.8 %all-reduce.14.cloned.1.call-start = ((), (), s32[]{:S(2)}) async-start(), calls=%async_computation.16 | async-start | bytes 2097152 | tf_op jit(solution)/shard_map/psum | solution.py:32
  364.9 6.8 collective-permute-start
  380.6 61.1 %collective-permute-start.1 = (bf16[1,512,1024]{1,2,0:T(8,128)(2,1)}, bf16[1,512,1024]{1,2,0:T(8,128)(2,1)}, u32[]{:S(2)}, u32[]{:S(2)}) collective-permute-start(bf16[1,512,1024]{1,2,0:T(8,128)(2,1)} %copy.282), channel_id=1, source_target_pairs={{0,1},{1,2},{2,3},{4,5},{5,6},{6,7},{8,9},{9,10},{10,11},{12,13},{... | collective-permute-start | bytes 3145736 | tf_op jit(solution)/shard_map/ppermute | solution.py:27
  454.4 37.5 %collective-permute-start.2 = (bf16[1,512,1024]{1,2,0:T(8,128)(2,1)}, bf16[1,512,1024]{1,2,0:T(8,128)(2,1)}, u32[]{:S(2)}, u32[]{:S(2)}) collective-permute-start(bf16[1,512,1024]{1,2,0:T(8,128)(2,1)} %copy.286), channel_id=1, source_target_pairs={{0,1},{1,2},{2,3},{4,5},{5,6},{6,7},{8,9},{9,10},{10,11},{12,13},{... | collective-permute-start | bytes 3145736 | tf_op jit(solution)/shard_map/ppermute | solution.py:27
  657.5 43.5 %collective-permute-start.3 = (bf16[1,512,1024]{1,2,0:T(8,128)(2,1)}, bf16[1,512,1024]{1,2,0:T(8,128)(2,1)S(1)}, u32[]{:S(2)}, u32[]{:S(2)}) collective-permute-start(bf16[1,512,1024]{1,2,0:T(8,128)(2,1)} %copy.319), channel_id=1, source_target_pairs={{1,0},{2,1},{3,2},{5,4},{6,5},{7,6},{9,8},{10,9},{11,10},{13,12},{... | collective-permute-start | bytes 3145736 | tf_op jit(solution)/shard_map/ppermute | solution.py:27
  713.7 16.4 collective-permute-start.4
  745.3 279.0 %collective-permute-start.5 = (bf16[1,512,1024]{2,1,0:T(8,128)(2,1)}, bf16[1,512,1024]{2,1,0:T(8,128)(2,1)}, u32[]{:S(2)}, u32[]{:S(2)}) collective-permute-start(bf16[1,512,1024]{2,1,0:T(8,128)(2,1)} %convert_element_type.433), channel_id=1, source_target_pairs={{1,0},{2,1},{3,2},{5,4},{6,5},{7,6},{9,8},{10,9},{11,10},{13,12},{... | collective-permute-start | bytes 3145736 | tf_op jit(solution)/shard_map/ppermute | solution.py:27
  749.4 277.7 %copy-start.15 = (bf16[1,512,8,128]{3,2,1,0:T(8,128)(2,1)S(1)}, bf16[1,512,8,128]{3,2,1,0:T(8,128)(2,1)}, u32[]{:S(2)}) copy-start(bf16[1,512,8,128]{3,2,1,0:T(8,128)(2,1)} %copy-done.12) | copy-start | bytes 3145732
  749.5 577.2 %reduce-scatter.23.cloned.1.call-start = ((), (), s32[]{:S(2)}) async-start(), calls=%async_computation.24 | async-start | bytes 2162688 | tf_op jit(solution)/shard_map/reduce_scatter | solution.py:266
  1130.0 272.9 %reduce-scatter.15.cloned.1.call-start = ((), (), s32[]{:S(2)}) async-start(), calls=%async_computation.20 | async-start | bytes 4325376 | tf_op jit(solution)/shard_map/reduce_scatter | solution.py:262
  1134.8 407.7 %reduce-scatter.13.cloned.1.call-start = ((), (), s32[]{:S(2)}) async-start(), calls=%async_computation.19 | async-start | bytes 4325376 | tf_op jit(solution)/shard_map/reduce_scatter | solution.py:261
  1140.2 542.3 %reduce-scatter.17.cloned.1.call-start = ((), (), s32[]{:S(2)}) async-start(), calls=%async_computation.21 | async-start | bytes 4325376 | tf_op jit(solution)/shard_map/reduce_scatter | solution.py:263
  1145.6 684.3 %reduce-scatter.11.cloned.1.call-start = ((), (), s32[]{:S(2)}) async-start(), calls=%async_computation.18 | async-start | bytes 8650752 | tf_op jit(solution)/shard_map/reduce_scatter | solution.py:260
  1154.9 832.8 %reduce-scatter.9.cloned.1.call-start = ((), (), s32[]{:S(2)}) async-start(), calls=%async_computation.17 | async-start | bytes 12976128 | tf_op jit(solution)/shard_map/reduce_scatter | solution.py:259
  1189.1 983.5 %reduce-scatter.21.cloned.1.call-start = ((), (), s32[]{:S(2)}) async-start(), calls=%async_computation.23 | async-start | bytes 17301504 | tf_op jit(solution)/shard_map/reduce_scatter | solution.py:265
  1205.3 1154.6 %reduce-scatter.19.cloned.1.call-start = ((), (), s32[]{:S(2)}) async-start(), calls=%async_computation.22 | async-start | bytes 17301504 | tf_op jit(solution)/shard_map/reduce_scatter | solution.py:264
  (94 other events, 1254.3 us)
Sparse Core Ops, SparseCore 0:
  10.9 56.5 all-gather.10
  70.3 68.4 all-gather.8
  141.7 54.8 all-gather.14
  199.4 55.2 all-gather.16
  257.3 60.8 all-gather.12
  321.0 55.4 all-gather.18
  379.3 76.3 all-gather.20
  458.5 83.0 all-gather.22
  749.6 310.6 all-reduce.13
  1130.1 132.9 reduce-scatter.22
  1265.9 136.9 reduce-scatter.14
  1405.6 136.8 reduce-scatter.12
  1545.4 137.0 reduce-scatter.16
  1685.3 144.5 reduce-scatter.10
  1836.3 151.3 reduce-scatter.8
  1990.5 181.9 reduce-scatter.20
  2175.4 184.5 reduce-scatter.18
where the time goes:
time: 2380 us; the launch traced here: 2370 us
  waiting for transfers between devices  1610 us (68%)
  matrix products  288 us (12%)
  local copies, waits for them, and re-layouts  170 us (7%)
  other arithmetic  98.8 us (4%)
  blocking collectives  80.5 us (3%)
  starting transfers between devices  56.6 us (2%)
  loops' own time  45.3 us (2%)
    ppermute x6, waiting for transfers between devices, from_behind(): return lax.ppermute(block, axis, route)  332 us
    reduce_scatter x1, waiting for transfers between devices, reduce_grads(): lax.psum_scatter(up_grad, ('dp', 'seq'), scatter_dimension=0, tiled=True)  187 us
    reduce_scatter x1, waiting for transfers between devices, reduce_grads(): lax.psum_scatter(down_grad, ('dp', 'seq'), scatter_dimension=0, tiled=True)  185 us
    reduce_scatter x1, waiting for transfers between devices, reduce_grads(): lax.psum_scatter(qkv_grad, ('dp', 'seq'), scatter_dimension=0, tiled=True)  158 us
    reduce_scatter x1, waiting for transfers between devices, reduce_grads(): lax.psum_scatter(state_key_value_gradient, ('dp', 'seq'), scatter_dimensi...  147 us
    reduce_scatter x1, waiting for transfers between devices, reduce_grads(): lax.psum_scatter(merge_grad, ('dp', 'seq'), scatter_dimension=0, tiled=True)  140 us
    reduce_scatter x1, waiting for transfers between devices, reduce_grads(): lax.psum_scatter(query_grad, ('dp', 'seq'), scatter_dimension=0, tiled=True)  140 us
    unnamed x2, blocking collectives  80.5 us
  transfers between devices with their start and end apart: 23, of which 15 were waited for; matrix products, arithmetic and copies ran while one was open for 19% of the time, Pallas kernels for 0%

commit v1 on v0

v1 whole, which is shorter than its diff:
```python
from functools import partial

import jax
import jax.numpy as jnp
import numpy as np
from jax import lax
from jax.experimental import pallas as pl
from jax.experimental.pallas import tpu as pltpu
from jax.sharding import PartitionSpec as P

HEADS = 8
HEAD = 128
BUCKETS = 32
MAX_DIST = 128
EPS = 1e-05
NEG = -1e30
SCALE = HEAD ** (-0.5)
AXES = ("dp", "seq")
F32 = jnp.float32
BF16 = jnp.bfloat16
MIB = 1 << 20


def bucket_of(length):
    dist = np.arange(length)
    exact = BUCKETS // 2
    scaled = np.log(np.maximum(dist, exact) / exact) / np.log(MAX_DIST / exact) * (BUCKETS - exact)
    far = np.minimum(exact + np.floor(scaled).astype(np.int32), BUCKETS - 1)
    return np.where(dist < exact, dist, far).astype(np.int32)


def dot_nn(a, b):
    return jnp.dot(a, b, preferred_element_type=F32)


def dot_nt(a, b):
    return lax.dot_general(a, b, (((1,), (1,)), ((), ())), preferred_element_type=F32)


def norm_parts(x):
    mean = jnp.mean(x, axis=-1, keepdims=True)
    centered = x - mean
    spread = jnp.mean(centered * centered, axis=-1, keepdims=True)
    rstd = lax.rsqrt(spread + EPS)
    return centered * rstd, rstd


def norm_back(x, gain, dy):
    xhat, rstd = norm_parts(x)
    dyg = dy * gain
    mean_one = jnp.mean(dyg, axis=-1, keepdims=True)
    mean_two = jnp.mean(dyg * xhat, axis=-1, keepdims=True)
    return rstd * (dyg - mean_one - xhat * mean_two), dy * xhat


def row_iota(rows, cols):
    return lax.broadcasted_iota(jnp.int32, (rows, cols), 0)


def row_chunks(rows, chunk, body):
    def step(i, carry):
        body(pl.ds(pl.multiple_of(i * chunk, chunk), chunk))
        return carry

    lax.fori_loop(0, rows // chunk, step, 0)


def project_kernel(x_ref, gains_ref, w_ref, init_t_ref, qkv_ref, h1_ref, init_ref):
    i = pl.program_id(0)

    @pl.when(i == 0)
    def _():
        def chunk(rows):
            xhat, _ = norm_parts(x_ref[rows, :].astype(F32))
            h1_ref[rows, :] = (xhat * gains_ref[0:1, :]).astype(BF16)

        row_chunks(x_ref.shape[0], 64, chunk)
        init_ref[...] = init_t_ref[...].T

    acc = dot_nn(h1_ref[...], w_ref[...])
    factor = jnp.where(i < 2, SCALE, 1.0).astype(F32)
    qkv_ref[...] = (acc * factor).astype(BF16)


def project(x, gains, wa):
    rows, width = x.shape
    states = 512
    tile = 512
    return pl.pallas_call(
        project_kernel,
        grid=(3 * width // tile,),
        in_specs=[
            pl.BlockSpec((rows, width), lambda i: (0, 0)),
            pl.BlockSpec((8, width), lambda i: (0, 0)),
            pl.BlockSpec((width, tile), lambda i: (0, i)),
            pl.BlockSpec((width, states), lambda i: (0, 7 * width // states)),
        ],
        out_specs=[
            pl.BlockSpec((rows, tile), lambda i: (0, i)),
            pl.BlockSpec((rows, width), lambda i: (0, 0)),
            pl.BlockSpec((states, width), lambda i: (0, 0)),
        ],
        out_shape=[
            jax.ShapeDtypeStruct((rows, 3 * width), BF16),
            jax.ShapeDtypeStruct((rows, width), BF16),
            jax.ShapeDtypeStruct((states, width), BF16),
        ],
        compiler_params=pltpu.CompilerParams(vmem_limit_bytes=32 * MIB),
        cost_estimate=pl.CostEstimate(flops=2 * rows * width * 3 * width, bytes_accessed=12 * MIB, transcendentals=0),
        name="project",
    )(x, gains, wa, wa)


def advance_kernel(first, flags_ref, gains_ref, c_hbm, wa_hbm, qkv_hbm, *refs):
    if not first:
        refs = refs[6:]
    (new_hbm, cs_hbm, hc_hbm, ckvq_hbm, upd_hbm, z_hbm, lse_hbm) = refs[:7]
    (c_v, w_v, m_v, kv_v, hc_v, ckvq_v, upd_v, z_v, new_v, lse_v, sem) = refs[7:]
    width = c_v.shape[1]

    @pl.when(flags_ref[0] == 1)
    def _():
        c_in = pltpu.make_async_copy(c_hbm, c_v, sem.at[0])
        w_in = pltpu.make_async_copy(wa_hbm.at[:, pl.ds(3 * width, 3 * width)], w_v, sem.at[1])
        kv_in = pltpu.make_async_copy(qkv_hbm.at[:, pl.ds(width, 2 * width)], kv_v, sem.at[2])
        m_in = pltpu.make_async_copy(wa_hbm.at[:, pl.ds(6 * width, width)], m_v, sem.at[3])
        c_in.start()
        w_in.start()
        kv_in.start()
        m_in.start()
        c_in.wait()
        c_out = pltpu.make_async_copy(c_v, cs_hbm, sem.at[0])
        c_out.start()

        def norm_chunk(rows):
            xhat, _ = norm_parts(c_v[rows, :].astype(F32))
            hc_v[rows, :] = (xhat * gains_ref[2:3, :]).astype(BF16)

        row_chunks(c_v.shape[0], 64, norm_chunk)
        hc_out = pltpu.make_async_copy(hc_v, hc_hbm, sem.at[4])
        hc_out.start()
        w_in.wait()

        def column_tile(t, carry):
            cols = pl.ds(pl.multiple_of(t * 512, 512), 512)
            factor = jnp.where(t < 4, 1.0, SCALE).astype(F32)
            ckvq_v[:, cols] = (dot_nn(hc_v[...], w_v[:, cols]) * factor).astype(BF16)
            return carry

        lax.fori_loop(0, 3 * width // 512, column_tile, 0)
        ckvq_out = pltpu.make_async_copy(ckvq_v, ckvq_hbm, sem.at[1])
        ckvq_out.start()
        kv_in.wait()
        nvalid = flags_ref[1]
        keys = kv_v.shape[0]

        def head_step(h, carry):
            off = pl.multiple_of(h * HEAD, HEAD)
            ck = ckvq_v[:, pl.ds(off, HEAD)]
            cvt = ckvq_v[:, pl.ds(off + width, HEAD)].T
            k = kv_v[:, pl.ds(off, HEAD)]
            vt = kv_v[:, pl.ds(off + width, HEAD)].T
            for part in range(2):
                q = ckvq_v[part * 256 : part * 256 + 256, pl.ds(off + 2 * width, HEAD)]
                one = dot_nt(ck, q)
                two = jnp.where(row_iota(keys, 256) < nvalid, dot_nt(k, q), NEG)
                top = jnp.maximum(
                    jnp.max(one, axis=0, keepdims=True), jnp.max(two, axis=0, keepdims=True)
                )
                one = jnp.exp(one - top)
                two = jnp.exp(two - top)
                total = jnp.sum(one, axis=0, keepdims=True) + jnp.sum(two, axis=0, keepdims=True)
                mixed = dot_nn(cvt, one.astype(BF16)) + dot_nn(vt, two.astype(BF16))
                mixed = mixed * (1.0 / total)
                upd_v[part * 256 : part * 256 + 256, pl.ds(off, HEAD)] = mixed.T.astype(BF16)
                lse_v[pl.ds(h, 1), part * 256 : part * 256 + 256] = top + jnp.log(total)
            return carry

        lax.fori_loop(0, HEADS, head_step, 0)
        upd_out = pltpu.make_async_copy(upd_v, upd_hbm, sem.at[2])
        upd_out.start()
        lse_out = pltpu.make_async_copy(lse_v, lse_hbm, sem.at[5])
        lse_out.start()
        m_in.wait()

        def merge_tile(t, carry):
            cols = pl.ds(pl.multiple_of(t * 512, 512), 512)
            z_v[:, cols] = dot_nn(upd_v[...], m_v[:, cols])
            return carry

        lax.fori_loop(0, width // 512, merge_tile, 0)
        z_out = pltpu.make_async_copy(z_v, z_hbm, sem.at[6])
        z_out.start()

        def gate_chunk(rows):
            gate = gains_ref[3:4, :]
            new = gate * c_v[rows, :].astype(F32) + (1.0 - gate) * z_v[rows, :]
            new_v[rows, :] = new.astype(BF16)

        row_chunks(c_v.shape[0], 64, gate_chunk)
        new_out = pltpu.make_async_copy(new_v, new_hbm, sem.at[3])
        new_out.start()
        c_out.wait()
        hc_out.wait()
        ckvq_out.wait()
        upd_out.wait()
        lse_out.wait()
        z_out.wait()
        new_out.wait()


def advance(flags, gains, c, wa, qkv, stash):
    states, width = c.shape
    rows = qkv.shape[0]
    hbm = pl.BlockSpec(memory_space=pl.ANY)
    shapes = [
        jax.ShapeDtypeStruct((states, width), BF16),
        jax.ShapeDtypeStruct((states, width), BF16),
        jax.ShapeDtypeStruct((states, width), BF16),
        jax.ShapeDtypeStruct((states, 3 * width), BF16),
        jax.ShapeDtypeStruct((states, width), BF16),
        jax.ShapeDtypeStruct((states, width), F32),
        jax.ShapeDtypeStruct((HEADS, states), F32),
    ]
    first = stash is None
    extra = () if first else tuple(stash)
    out = pl.pallas_call(
        partial(advance_kernel, first),
        in_specs=[
            pl.BlockSpec(memory_space=pltpu.SMEM),
            pl.BlockSpec(memory_space=pltpu.VMEM),
            hbm,
            hbm,
            hbm,
        ]
        + [hbm] * len(extra),
        out_specs=[hbm] * 7,
        out_shape=shapes,
        scratch_shapes=[
            pltpu.VMEM((states, width), BF16),
            pltpu.VMEM((width, 3 * width), BF16),
            pltpu.VMEM((width, width), BF16),
            pltpu.VMEM((rows, 2 * width), BF16),
            pltpu.VMEM((states, width), BF16),
            pltpu.VMEM((states, 3 * width), BF16),
            pltpu.VMEM((states, width), BF16),
            pltpu.VMEM((states, width), F32),
            pltpu.VMEM((states, width), BF16),
            pltpu.VMEM((HEADS, states), F32),
            pltpu.SemaphoreType.DMA((7,)),
        ],
        input_output_aliases={} if first else {5 + i: 1 + i for i in range(6)},
        compiler_params=pltpu.CompilerParams(vmem_limit_bytes=44 * MIB),
        cost_estimate=pl.CostEstimate(flops=9 << 30, bytes_accessed=24 * MIB, transcendentals=4 * MIB),
        name="advance",
    )(flags, gains, c, wa, qkv, *extra)
    return out[0], out[1:]


def bias_tiles(t_row):
    spread = jnp.broadcast_to(t_row, (128, t_row.shape[1]))
    grid = pltpu.roll(spread, 0, axis=1, stride=1, stride_axis=0)
    lane = lax.broadcasted_iota(jnp.int32, (128, 128), 1)
    sub = lax.broadcasted_iota(jnp.int32, (128, 128), 0)
    tiles = [grid[:, 128 * d : 128 * d + 128] for d in range(4)]
    tiles[0] = jnp.where(lane >= sub, tiles[0], NEG)
    return tiles


def bias_part(tiles, part):
    none = jnp.full((128, 128), NEG, F32)
    rows = []
    for j in range(2 * part + 2):
        row = [tiles[i - j] if i >= j else none for i in (2 * part, 2 * part + 1)]
        rows.append(jnp.concatenate(row, axis=1))
    return jnp.concatenate(rows, axis=0)


def own_scores(k, q, tiles, part, nvalid):
    used = 256 * (part + 1)
    scores = dot_nt(k[:used], q) + bias_part(tiles, part)
    return jnp.where(row_iota(used, 256) < nvalid, scores, NEG)


def token_kernel(flags_ref, t_ref, gains_ref, x_ref, q_ref, k_ref, v_ref, ck_ref, cv_ref, w_ref,
                 o_ref, lse_ref, x1_ref, h2_ref, acc_ref):
    i = pl.program_id(0)
    nvalid = flags_ref[1]
    for sub in range(2):
        cols = slice(sub * HEAD, sub * HEAD + HEAD)
        h = 2 * i + sub
        tiles = bias_tiles(t_ref[pl.ds(h, 1), :])
        k = k_ref[:, cols]
        vt = v_ref[:, cols].T
        ck = ck_ref[:, cols]
        cvt = cv_ref[:, cols].T
        for part in range(2):
            q = q_ref[part * 256 : part * 256 + 256, cols]
            one = dot_nt(ck, q)
            two = own_scores(k, q, tiles, part, nvalid)
            top = jnp.maximum(
                jnp.max(one, axis=0, keepdims=True), jnp.max(two, axis=0, keepdims=True)
            )
            one = jnp.exp(one - top)
            two = jnp.exp(two - top)
            total = jnp.sum(one, axis=0, keepdims=True) + jnp.sum(two, axis=0, keepdims=True)
            used = 256 * (part + 1)
            mixed = dot_nn(cvt, one.astype(BF16)) + dot_nn(vt[:, :used], two.astype(BF16))
            mixed = mixed * (1.0 / total)
            o_ref[part * 256 : part * 256 + 256, cols] = mixed.T.astype(BF16)
            lse_ref[pl.ds(h, 1), part * 256 : part * 256 + 256] = top + jnp.log(total)
    term = dot_nn(o_ref[...], w_ref[...])

    @pl.when(i == 0)
    def _():
        acc_ref[...] = x_ref[...].astype(F32) + term

    @pl.when(i > 0)
    def _():
        acc_ref[...] += term

    @pl.when(i == pl.num_programs(0) - 1)
    def _():
        def chunk(rows):
            x1 = acc_ref[rows, :]
            x1_ref[rows, :] = x1
            xhat, _ = norm_parts(x1)
            h2_ref[rows, :] = (xhat * gains_ref[1:2, :]).astype(BF16)

        row_chunks(acc_ref.shape[0], 64, chunk)


def token_forward(flags, t, gains, x, qkv, ckvq, wb):
    rows, width = x.shape
    states = ckvq.shape[0]
    steps = HEADS // 2
    return pl.pallas_call(
        token_kernel,
        grid=(steps,),
        in_specs=[
            pl.BlockSpec(memory_space=pltpu.SMEM),
            pl.BlockSpec((HEADS, rows), lambda i: (0, 0)),
            pl.BlockSpec((8, width), lambda i: (0, 0)),
            pl.BlockSpec((rows, width), lambda i: (0, 0)),
            pl.BlockSpec((rows, 256), lambda i: (0, i)),
            pl.BlockSpec((rows, 256), lambda i: (0, 4 + i)),
            pl.BlockSpec((rows, 256), lambda i: (0, 8 + i)),
            pl.BlockSpec((states, 256), lambda i: (0, i)),
            pl.BlockSpec((states, 256), lambda i: (0, 4 + i)),
            pl.BlockSpec((256, width), lambda i: (i, 0)),
        ],
        out_specs=[
            pl.BlockSpec((rows, 256), lambda i: (0, i)),
            pl.BlockSpec((HEADS, rows), lambda i: (0, 0)),
            pl.BlockSpec((rows, width), lambda i: (0, 0)),
            pl.BlockSpec((rows, width), lambda i: (0, 0)),
        ],
        out_shape=[
            jax.ShapeDtypeStruct((rows, width), BF16),
            jax.ShapeDtypeStruct((HEADS, rows), F32),
            jax.ShapeDtypeStruct((rows, width), F32),
            jax.ShapeDtypeStruct((rows, width), BF16),
        ],
        scratch_shapes=[pltpu.VMEM((rows, width), F32)],
        compiler_params=pltpu.CompilerParams(vmem_limit_bytes=40 * MIB),
        cost_estimate=pl.CostEstimate(flops=4 << 30, bytes_accessed=12 * MIB, transcendentals=4 * MIB),
        name="token_forward",
    )(flags, t, gains, x, qkv, qkv, qkv, ckvq, ckvq, wb)


def ffn_kernel(gains_ref, h2_ref, g_ref, x1_ref, wu_ref, wd_ref, wo_ref,
               act_ref, dup_ref, out_ref, dx1_ref, da_ref, do_ref, sums_ref, acc_ref, dh_ref):
    i = pl.program_id(0)
    up = dot_nn(h2_ref[...], wu_ref[...])
    dact = dot_nt(g_ref[...], wd_ref[...])
    cubic = 0.7978845608028654
    square = up * up
    th = jnp.tanh(cubic * up * (1.0 + 0.044715 * square))
    half = 0.5 * (1.0 + th)
    act = (up * half).astype(BF16)
    slope = half + (0.5 * cubic) * up * (1.0 - th * th) * (1.0 + (3 * 0.044715) * square)
    dup = (dact * slope).astype(BF16)
    act_ref[...] = act
    dup_ref[...] = dup
    out_term = dot_nn(act, wd_ref[...])
    dh_term = dot_nt(dup, wu_ref[...])

    @pl.when(i == 0)
    def _():
        acc_ref[...] = x1_ref[...] + out_term
        dh_ref[...] = dh_term

    @pl.when(i > 0)
    def _():
        acc_ref[...] += out_term
        dh_ref[...] += dh_term

    @pl.when(i == pl.num_programs(0) - 1)
    def _():
        sums_ref[...] = jnp.zeros_like(sums_ref)

        def chunk(rows):
            out_ref[rows, :] = acc_ref[rows, :].astype(BF16)
            dx, gain_term = norm_back(x1_ref[rows, :], gains_ref[1:2, :], dh_ref[rows, :])
            dx = dx + g_ref[rows, :].astype(F32)
            dx1_ref[rows, :] = dx
            da_ref[rows, :] = dx.astype(BF16)
            sums_ref[0:1, :] += jnp.sum(gain_term, axis=0, keepdims=True)

        row_chunks(acc_ref.shape[0], 64, chunk)
        do_ref[...] = dot_nt(da_ref[...], wo_ref[...]).astype(BF16)


def feed_forward(gains, h2, g, x1, wb):
    rows, width = h2.shape
    hidden = 4 * width
    tile = 512
    whole = lambda i: (0, 0)
    return pl.pallas_call(
        ffn_kernel,
        grid=(hidden // tile,),
        in_specs=[
            pl.BlockSpec((8, width), whole),
            pl.BlockSpec((rows, width), whole),
            pl.BlockSpec((rows, width), whole),
            pl.BlockSpec((rows, width), whole),
            pl.BlockSpec((width, tile), lambda i: (0, 2 + i)),
            pl.BlockSpec((tile, width), lambda i: (i % 2, 5 + i // 2)),
            pl.BlockSpec((width, width), whole),
        ],
        out_specs=[
            pl.BlockSpec((rows, tile), lambda i: (0, i)),
            pl.BlockSpec((rows, tile), lambda i: (0, i)),
            pl.BlockSpec((rows, width), whole),
            pl.BlockSpec((rows, width), whole),
            pl.BlockSpec((rows, width), whole),
            pl.BlockSpec((rows, width), whole),
            pl.BlockSpec((8, width), whole),
        ],
        out_shape=[
            jax.ShapeDtypeStruct((rows, hidden), BF16),
            jax.ShapeDtypeStruct((rows, hidden), BF16),
            jax.ShapeDtypeStruct((rows, width), BF16),
            jax.ShapeDtypeStruct((rows, width), F32),
            jax.ShapeDtypeStruct((rows, width), BF16),
            jax.ShapeDtypeStruct((rows, width), BF16),
            jax.ShapeDtypeStruct((8, width), F32),
        ],
        scratch_shapes=[pltpu.VMEM((rows, width), F32), pltpu.VMEM((rows, width), F32)],
        compiler_params=pltpu.CompilerParams(vmem_limit_bytes=52 * MIB),
        cost_estimate=pl.CostEstimate(flops=18 << 30, bytes_accessed=32 * MIB, transcendentals=2 * MIB),
        name="feed_forward",
    )(gains, h2, g, x1, wb, wb, wb)


def token_back_kernel(flags_ref, t_ref, lse_ref, q_ref, k_ref, v_ref, ck_ref, cv_ref, do_ref,
                      dq_ref, dkv_ref, dst_ref, db_ref):
    h = pl.program_id(0)
    nvalid = flags_ref[1]
    tiles = bias_tiles(t_ref[pl.ds(h, 1), :])
    k, v, ck, cv = k_ref[...], v_ref[...], ck_ref[...], cv_ref[...]
    kt, ckt = k.T, ck.T
    dk, dv, dck, dcv = [], [], [], []
    shear = [jnp.zeros((128, 128), F32) for _ in range(4)]
    for part in range(2):
        span = slice(part * 256, part * 256 + 256)
        used = 256 * (part + 1)
        q, do = q_ref[span, :], do_ref[span, :]
        lse = lse_ref[pl.ds(h, 1), span]
        one = jnp.exp(dot_nt(ck, q) - lse)
        two = jnp.exp(own_scores(k, q, tiles, part, nvalid) - lse)
        done = dot_nt(cv, do)
        dtwo = dot_nt(v[:used], do)
        inner = jnp.sum(one * done, axis=0, keepdims=True) + jnp.sum(
            two * dtwo, axis=0, keepdims=True
        )
        dcv.append(dot_nn(one.astype(BF16), do))
        dv.append(dot_nn(two.astype(BF16), do))
        one = one * (done - inner)
        two = two * (dtwo - inner)
        for j in range(2 * part + 2):
            for i in (0, 1):
                d = 2 * part + i - j
                if d >= 0:
                    shear[d] += two[128 * j : 128 * j + 128, 128 * i : 128 * i + 128]
        one, two = one.astype(BF16), two.astype(BF16)
        dck.append(dot_nn(one, q))
        dk.append(dot_nn(two, q))
        dqt = dot_nn(ckt, one) + dot_nn(kt[:, :used], two)
        dq_ref[span, :] = (dqt.T * SCALE).astype(BF16)
    for slot, pieces in ((0, dk), (1, dv)):
        dkv_ref[slot, :256, :] = (pieces[0] + pieces[1][:256]).astype(BF16)
        dkv_ref[slot, 256:, :] = pieces[1][256:].astype(BF16)
    dst_ref[0] = (dck[0] + dck[1]).astype(BF16)
    dst_ref[1] = (dcv[0] + dcv[1]).astype(BF16)
    grid = jnp.concatenate(shear, axis=1)
    size = grid.shape[1]
    flipped = grid[:8]
    for group in range(1, 16):
        flipped += pltpu.roll(grid[8 * group : 8 * group + 8], size - 8 * group, axis=1)
    for step in (1, 2, 4):
        moved = pltpu.roll(flipped, size - step, axis=1)
        flipped = jnp.where((row_iota(8, size) // step) % 2 == 1, moved, flipped)
    db_ref[pl.ds(h, 1), :] = jnp.sum(flipped, axis=0, keepdims=True)


def token_back(flags, t, lse, qkv, ckvq, do):
    rows = do.shape[0]
    width = do.shape[1]
    states = ckvq.shape[0]
    column = lambda base: (lambda h: (0, base + h))
    return pl.pallas_call(
        token_back_kernel,
        grid=(HEADS,),
        in_specs=[
            pl.BlockSpec(memory_space=pltpu.SMEM),
            pl.BlockSpec((HEADS, rows), lambda h: (0, 0)),
            pl.BlockSpec((HEADS, rows), lambda h: (0, 0)),
            pl.BlockSpec((rows, HEAD), column(0)),
            pl.BlockSpec((rows, HEAD), column(8)),
            pl.BlockSpec((rows, HEAD), column(16)),
            pl.BlockSpec((states, HEAD), column(0)),
            pl.BlockSpec((states, HEAD), column(8)),
            pl.BlockSpec((rows, HEAD), column(0)),
        ],
        out_specs=[
            pl.BlockSpec((rows, HEAD), column(0)),
            pl.BlockSpec((2, rows, HEAD), lambda h: (0, 0, h)),
            pl.BlockSpec((2, states, HEAD), lambda h: (0, 0, h)),
            pl.BlockSpec((HEADS, rows), lambda h: (0, 0)),
        ],
        out_shape=[
            jax.ShapeDtypeStruct((rows, width), BF16),
            jax.ShapeDtypeStruct((2, rows, width), BF16),
            jax.ShapeDtypeStruct((2, states, width), BF16),
            jax.ShapeDtypeStruct((HEADS, rows), F32),
        ],
        compiler_params=pltpu.CompilerParams(vmem_limit_bytes=40 * MIB),
        cost_estimate=pl.CostEstimate(flops=5 << 30, bytes_accessed=12 * MIB, transcendentals=4 * MIB),
        name="token_back",
    )(flags, t, lse, qkv, qkv, qkv, ckvq, ckvq, do)


def retreat_kernel(first, flags_ref, gains_ref, lam_hbm, wa_hbm, qkv_hbm, cs_hbm, ckvq_hbm, z_hbm,
                   lse_hbm, dst_hbm, *refs):
    if not first:
        refs = refs[4:]
    (prev_hbm, dz_hbm, dcs_hbm, dkv_hbm, sums_hbm) = refs[:5]
    (lam_v, w_v, m_v, kv_v, c_v, ckvq_v, z_v, lse_v, dst_v,
     dz_v, du_v, dcs_v, dkv_v, dh_v, prev_v, sums_v, sem) = refs[5:]
    states, width = c_v.shape

    @pl.when(flags_ref[0] == 1)
    def _():
        copies = [
            pltpu.make_async_copy(src, dst, sem.at[n])
            for n, (src, dst) in enumerate(
                (
                    (lam_hbm, lam_v),
                    (cs_hbm, c_v),
                    (z_hbm, z_v),
                    (wa_hbm.at[:, pl.ds(6 * width, width)], m_v),
                    (ckvq_hbm, ckvq_v),
                    (qkv_hbm.at[:, pl.ds(width, 2 * width)], kv_v),
                    (lse_hbm, lse_v),
                    (dst_hbm, dst_v),
                    (wa_hbm.at[:, pl.ds(3 * width, 3 * width)], w_v),
                )
            )
        ]
        for copy in copies:
            copy.start()
        for copy in copies[:3]:
            copy.wait()
        sums_v[...] = jnp.zeros_like(sums_v)

        def gate_chunk(rows):
            lam = lam_v[rows, :].astype(F32)
            dz_v[rows, :] = ((1.0 - gains_ref[3:4, :]) * lam).astype(BF16)
            change = lam * (c_v[rows, :].astype(F32) - z_v[rows, :])
            sums_v[1:2, :] += jnp.sum(change, axis=0, keepdims=True)

        row_chunks(states, 64, gate_chunk)
        dz_out = pltpu.make_async_copy(dz_v, dz_hbm, sem.at[0])
        dz_out.start()
        copies[3].wait()

        def merge_tile(t, carry):
            cols = pl.ds(pl.multiple_of(t * 512, 512), 512)
            du_v[:, cols] = dot_nt(dz_v[...], m_v[cols, :]).astype(BF16)
            return carry

        lax.fori_loop(0, width // 512, merge_tile, 0)
        for copy in copies[4:8]:
            copy.wait()
        nvalid = flags_ref[1]
        keys = kv_v.shape[0]

        def head_step(h, carry):
            off = pl.multiple_of(h * HEAD, HEAD)
            here = pl.ds(off, HEAD)
            there = pl.ds(off + width, HEAD)
            ck, cv = ckvq_v[:, here], ckvq_v[:, there]
            k, v = kv_v[:, here], kv_v[:, there]
            ckt, kt = ck.T, k.T
            total = None
            for part in range(2):
                span = slice(part * 256, part * 256 + 256)
                q = ckvq_v[span, pl.ds(off + 2 * width, HEAD)]
                du = du_v[span, here]
                lse = lse_v[pl.ds(h, 1), span]
                one = jnp.exp(dot_nt(ck, q) - lse)
                two = jnp.where(row_iota(keys, 256) < nvalid, dot_nt(k, q), NEG)
                two = jnp.exp(two - lse)
                done = dot_nt(cv, du)
                dtwo = dot_nt(v, du)
                inner = jnp.sum(one * done, axis=0, keepdims=True) + jnp.sum(
                    two * dtwo, axis=0, keepdims=True
                )
                terms = [dot_nn(one.astype(BF16), du), dot_nn(two.astype(BF16), du)]
                one = (one * (done - inner)).astype(BF16)
                two = (two * (dtwo - inner)).astype(BF16)
                terms += [dot_nn(one, q), dot_nn(two, q)]
                dqt = dot_nn(ckt, one) + dot_nn(kt, two)
                dcs_v[span, pl.ds(off + 2 * width, HEAD)] = (dqt.T * SCALE).astype(BF16)
                total = terms if total is None else [a + b for a, b in zip(total, terms)]
            dcs_v[:, there] = (total[0] + dst_v[1, :, here].astype(F32)).astype(BF16)
            dcs_v[:, here] = (total[2] + dst_v[0, :, here].astype(F32)).astype(BF16)
            dkv_v[:, there] = total[1].astype(BF16)
            dkv_v[:, here] = total[3].astype(BF16)
            return carry

        lax.fori_loop(0, HEADS, head_step, 0)
        dcs_out = pltpu.make_async_copy(dcs_v, dcs_hbm, sem.at[1])
        dcs_out.start()
        dkv_out = pltpu.make_async_copy(dkv_v, dkv_hbm, sem.at[2])
        dkv_out.start()
        copies[8].wait()
        dh_v[...] = dot_nt(dcs_v[:, :512], w_v[:, :512])

        def depth_tile(t, carry):
            cols = pl.ds(pl.multiple_of(t * 512, 512), 512)
            dh_v[...] += dot_nt(dcs_v[:, cols], w_v[:, cols])
            return carry

        lax.fori_loop(1, 3 * width // 512, depth_tile, 0)

        def norm_chunk(rows):
            dx, gain_term = norm_back(
                c_v[rows, :].astype(F32), gains_ref[2:3, :], dh_v[rows, :]
            )
            prev = dx + gains_ref[3:4, :] * lam_v[rows, :].astype(F32)
            prev_v[rows, :] = prev.astype(BF16)
            sums_v[0:1, :] += jnp.sum(gain_term, axis=0, keepdims=True)

        row_chunks(states, 64, norm_chunk)
        prev_out = pltpu.make_async_copy(prev_v, prev_hbm, sem.at[3])
        prev_out.start()
        sums_out = pltpu.make_async_copy(sums_v, sums_hbm, sem.at[4])
        sums_out.start()
        dz_out.wait()
        dcs_out.wait()
        dkv_out.wait()
        prev_out.wait()
        sums_out.wait()


def retreat(flags, gains, lam, wa, qkv, cs, ckvq, z, lse, dst, stash):
    states, width = cs.shape
    rows = qkv.shape[0]
    hbm = pl.BlockSpec(memory_space=pl.ANY)
    shapes = [
        jax.ShapeDtypeStruct((states, width), BF16),
        jax.ShapeDtypeStruct((states, width), BF16),
        jax.ShapeDtypeStruct((states, 3 * width), BF16),
        jax.ShapeDtypeStruct((rows, 2 * width), BF16),
        jax.ShapeDtypeStruct((8, width), F32),
    ]
    first = stash is None
    extra = () if first else tuple(stash)
    out = pl.pallas_call(
        partial(retreat_kernel, first),
        in_specs=[
            pl.BlockSpec(memory_space=pltpu.SMEM),
            pl.BlockSpec(memory_space=pltpu.VMEM),
        ]
        + [hbm] * (8 + len(extra)),
        out_specs=[hbm] * 5,
        out_shape=shapes,
        scratch_shapes=[
            pltpu.VMEM((states, width), lam.dtype),
            pltpu.VMEM((width, 3 * width), BF16),
            pltpu.VMEM((width, width), BF16),
            pltpu.VMEM((rows, 2 * width), BF16),
            pltpu.VMEM((states, width), BF16),
            pltpu.VMEM((states, 3 * width), BF16),
            pltpu.VMEM((states, width), F32),
            pltpu.VMEM((HEADS, states), F32),
            pltpu.VMEM((2, states, width), BF16),
            pltpu.VMEM((states, width), BF16),
            pltpu.VMEM((states, width), BF16),
            pltpu.VMEM((states, 3 * width), BF16),
            pltpu.VMEM((rows, 2 * width), BF16),
            pltpu.VMEM((states, width), F32),
            pltpu.VMEM((states, width), BF16),
            pltpu.VMEM((8, width), F32),
            pltpu.SemaphoreType.DMA((9,)),
        ],
        input_output_aliases={} if first else {10 + i: 1 + i for i in range(4)},
        compiler_params=pltpu.CompilerParams(vmem_limit_bytes=52 * MIB),
        cost_estimate=pl.CostEstimate(flops=13 << 30, bytes_accessed=32 * MIB, transcendentals=4 * MIB),
        name="retreat",
    )(flags, gains, lam, wa, qkv, cs, ckvq, z, lse, dst, *extra)
    return out[0], out[1:]


def input_grad_kernel(gains_ref, x_ref, dx1_ref, d_ref, w_ref, out_ref, sums_ref, acc_ref):
    i = pl.program_id(0)
    term = dot_nt(d_ref[...], w_ref[...])

    @pl.when(i == 0)
    def _():
        acc_ref[...] = term

    @pl.when(i > 0)
    def _():
        acc_ref[...] += term

    @pl.when(i == pl.num_programs(0) - 1)
    def _():
        sums_ref[...] = jnp.zeros_like(sums_ref)

        def chunk(rows):
            dx, gain_term = norm_back(x_ref[rows, :].astype(F32), gains_ref[0:1, :], acc_ref[rows, :])
            out_ref[rows, :] = dx1_ref[rows, :] + dx
            sums_ref[0:1, :] += jnp.sum(gain_term, axis=0, keepdims=True)

        row_chunks(acc_ref.shape[0], 64, chunk)


def input_grad(gains, x, dx1, dqkv, wa):
    rows, width = x.shape
    tile = 512
    whole = lambda i: (0, 0)
    return pl.pallas_call(
        input_grad_kernel,
        grid=(3 * width // tile,),
        in_specs=[
            pl.BlockSpec((8, width), whole),
            pl.BlockSpec((rows, width), whole),
            pl.BlockSpec((rows, width), whole),
            pl.BlockSpec((rows, tile), lambda i: (0, i)),
            pl.BlockSpec((width, tile), lambda i: (0, i)),
        ],
        out_specs=[pl.BlockSpec((rows, width), whole), pl.BlockSpec((8, width), whole)],
        out_shape=[
            jax.ShapeDtypeStruct((rows, width), F32),
            jax.ShapeDtypeStruct((8, width), F32),
        ],
        scratch_shapes=[pltpu.VMEM((rows, width), F32)],
        compiler_params=pltpu.CompilerParams(vmem_limit_bytes=40 * MIB),
        cost_estimate=pl.CostEstimate(flops=3 << 30, bytes_accessed=16 * MIB, transcendentals=0),
        name="input_grad",
    )(gains, x, dx1, dqkv, wa)


def outer_kernel(a_ref, b_ref, o_ref, at_ref):
    @pl.when(pl.program_id(1) == 0)
    def _():
        at_ref[...] = a_ref[...].T

    o_ref[...] = dot_nn(at_ref[...], b_ref[...]).astype(BF16)


def outer_product(a, b):
    rows, width = b.shape[0], 1024
    slabs = a.shape[1] // width
    tile = 512
    tiles = b.shape[1] // tile
    return pl.pallas_call(
        outer_kernel,
        grid=(slabs, tiles),
        in_specs=[
            pl.BlockSpec((rows, width), lambda s, i: (0, s)),
            pl.BlockSpec((rows, tile), lambda s, i: (0, i)),
        ],
        out_specs=pl.BlockSpec((width, tile), lambda s, i: (0, s * tiles + i)),
        out_shape=jax.ShapeDtypeStruct((width, slabs * b.shape[1]), BF16),
        scratch_shapes=[pltpu.VMEM((width, rows), BF16)],
        compiler_params=pltpu.CompilerParams(vmem_limit_bytes=32 * MIB),
        cost_estimate=pl.CostEstimate(
            flops=2 * rows * width * slabs * b.shape[1], bytes_accessed=4 * width * slabs * b.shape[1], transcendentals=0
        ),
        name="weight_grad",
    )(a, b)


def scatter_order(devices):
    bits = [1 << n for n in range(devices.bit_length() - 1)]
    rest = bits[1:]
    if len(rest) < 4:
        return [bits] * 3
    return [
        bits[:1] + rest,
        bits[:1] + rest[1:] + rest[:1],
        bits[:1] + rest[2:] + rest[:2],
    ]


def scatter_sum(value, order, devices):
    me = lax.axis_index(AXES)
    value = value.reshape(devices, value.shape[0] // devices, value.shape[1])
    left = sorted(order)
    for bit in order:
        place = left.index(bit)
        left.remove(bit)
        blocks, rows, cols = value.shape
        low = 1 << place
        view = value.reshape(blocks // (2 * low), 2, low, rows, cols)
        mine = (me // bit) % 2
        keep = lax.dynamic_index_in_dim(view, mine, 1, keepdims=False)
        send = lax.dynamic_index_in_dim(view, 1 - mine, 1, keepdims=False)
        keep = keep.reshape(blocks // 2, rows, cols)
        send = send.reshape(blocks // 2, rows, cols)
        route = [(i, i ^ bit) for i in range(devices)]
        got = lax.ppermute(send, AXES, route)
        value = keep.astype(F32) + got.astype(F32)
        if left:
            value = value.astype(BF16)
    return value[0]


def body(
    layer_input,
    segment_length,
    output_gradient,
    state_cotangent,
    query_key_value_weight,
    state_key_value_weight,
    state_query_weight,
    output_weight,
    merge_weight,
    up_weight,
    down_weight,
    initial_state_learned,
    attention_norm_gain,
    feedforward_norm_gain,
    state_norm_gain,
    state_gate_logits,
    relative_position_bias,
):
    _, rows, width = layer_input.shape
    place = lax.axis_index("seq")
    count = lax.axis_size("seq")
    devices = count * lax.axis_size("dp")
    share = width // devices
    pairs = lax.axis_size("dp")

    bias_local = relative_position_bias.shape[0]
    small = jnp.stack(
        [
            attention_norm_gain,
            feedforward_norm_gain,
            state_norm_gain,
            state_gate_logits,
            jnp.pad(relative_position_bias, (0, share - bias_local)),
        ],
        axis=1,
    )
    small = jnp.pad(small, ((0, 0), (0, 123)))
    wa = jnp.concatenate(
        [
            query_key_value_weight,
            state_key_value_weight,
            state_query_weight,
            merge_weight,
            initial_state_learned.T,
            small,
        ],
        axis=1,
    )
    up_local = up_weight.reshape(share, devices, 4, share).transpose(0, 2, 1, 3)
    down_local = down_weight.reshape(4, share, width).transpose(1, 0, 2)
    wb = jnp.concatenate(
        [output_weight, up_local.reshape(share, 4 * width), down_local.reshape(share, 4 * width)],
        axis=1,
    )
    wa = lax.all_gather(wa, AXES, axis=0, tiled=True)
    wb = lax.all_gather(wb, AXES, axis=0, tiled=True)

    vectors = wa[:, 15 * width // 2 : 15 * width // 2 + 5].astype(F32).T
    gate = jax.nn.sigmoid(vectors[3:4])
    gains = jnp.concatenate([vectors[:3], gate, jnp.zeros((4, width), F32)], axis=0)
    table = vectors[4].reshape(devices, share)[:, :bias_local].reshape(HEADS, BUCKETS)
    onehot = np.eye(BUCKETS, dtype=np.float32)[:, bucket_of(rows)]
    t = jnp.dot(table, jnp.asarray(onehot), precision=lax.Precision.HIGHEST)

    x = layer_input.reshape(rows, width)
    g = output_gradient.reshape(rows, width)
    nvalid = jnp.clip(segment_length[0] - place * rows, 0, rows).astype(jnp.int32)

    def flags(section):
        return jnp.stack([(place == section).astype(jnp.int32), nvalid])

    def hop(value, frm, to):
        route = [(d * count + frm, d * count + to) for d in range(pairs)]
        return lax.ppermute(value, AXES, route)

    qkv, h1, carry = project(x, gains, wa)
    stash = None
    for section in range(count):
        new, stash = advance(flags(section), gains, carry, wa, qkv, stash)
        if section + 1 < count:
            carry = hop(new, section, section + 1)
    cs, hc, ckvq, upd, z, lse_two = stash

    o, lse, x1, h2 = token_forward(flags(0), t, gains, x, qkv, ckvq, wb)
    act, dup, layer_out, dx1, da, do, sums_mlp = feed_forward(gains, h2, g, x1, wb)
    dq, dkv, dst, dbias = token_back(flags(0), t, lse, qkv, ckvq, do)

    back = None
    lam = state_cotangent.reshape(state_cotangent.shape[1:])
    for section in reversed(range(count)):
        prev, back = retreat(
            flags(section), gains, lam, wa, qkv, cs, ckvq, z, lse_two, dst, back
        )
        if section > 0:
            lam = hop(prev, section, section - 1)
    dz, dcs, dkv_two, sums_state = back

    quarter = new.shape[0] // count
    state_out = lax.dynamic_slice_in_dim(new, place * quarter, quarter, 0)
    for to in range(count - 1):
        got = hop(new[to * quarter : (to + 1) * quarter], count - 1, to)
        state_out = jnp.where(place == to, got, state_out)
    state_out = state_out.astype(F32)[None]

    up_grad = outer_product(h2, dup)
    down_grad = outer_product(act, g)
    out_grad = outer_product(o, da)
    early = jnp.concatenate([out_grad, up_grad, down_grad], axis=1)
    early = lax.psum_scatter(early, AXES, scatter_dimension=0, tiled=True).astype(F32)

    dqkv = jnp.concatenate(
        [
            dq,
            (dkv[0].astype(F32) + dkv_two[:, :width].astype(F32)).astype(BF16),
            (dkv[1].astype(F32) + dkv_two[:, width:].astype(F32)).astype(BF16),
        ],
        axis=1,
    )
    merge_grad = outer_product(upd, dz)
    state_grad = outer_product(hc, dcs)
    qkv_grad = outer_product(h1, dqkv)
    x_grad, sums_attn = input_grad(gains, x, dx1, dqkv, wa)
    x_grad = x_grad[None]

    init_grad = jnp.where(place == 0, prev, jnp.zeros_like(prev)).T
    buckets = jnp.asarray(np.ascontiguousarray(onehot.T))
    dtable = jnp.dot(dbias, buckets, precision=lax.Precision.HIGHEST).reshape(devices, bias_local)
    dtable = jnp.pad(dtable, ((0, 0), (0, share - bias_local))).reshape(width)
    gate_grad = sums_state[1] * gate[0] * (1.0 - gate[0])
    vector_grads = jnp.stack([sums_attn[0], sums_mlp[0], sums_state[0], gate_grad, dtable], axis=1)
    vector_grads = jnp.pad(vector_grads, ((0, 0), (0, 123))).astype(BF16)

    orders = scatter_order(devices)
    one = scatter_sum(jnp.concatenate([merge_grad, init_grad, vector_grads], axis=1), orders[0], devices)
    two = scatter_sum(state_grad, orders[1], devices)
    three = scatter_sum(qkv_grad, orders[2], devices)

    up_shard = early[:, width : 5 * width].reshape(share, 4, devices, share)
    up_shard = up_shard.transpose(0, 2, 1, 3).reshape(share, 4 * width)
    down_shard = early[:, 5 * width :].reshape(share, 4, width).transpose(1, 0, 2)
    states = width // 2
    vec = one[:, width + states :]
    return (
        layer_out[None],
        state_out,
        x_grad,
        three,
        two[:, : 2 * width],
        two[:, 2 * width :],
        early[:, :width],
        one[:, :width],
        up_shard,
        down_shard.reshape(4 * share, width),
        one[:, width : width + states].T,
        vec[:, 0],
        vec[:, 1],
        vec[:, 2],
        vec[:, 3],
        vec[:bias_local, 4],
    )


def solution(mesh):
    return jax.shard_map(
        body,
        mesh=mesh,
        in_specs=(
            P("dp", "seq", None),
            P("dp"),
            P("dp", "seq", None),
            P("dp", None, None),
            P(AXES, None),
            P(AXES, None),
            P(AXES, None),
            P(AXES, None),
            P(AXES, None),
            P(AXES, None),
            P(AXES, None),
            P(None, AXES),
            P(AXES),
            P(AXES),
            P(AXES),
            P(AXES),
            P(AXES),
        ),
        out_specs=(
            P("dp", "seq", None),
            P("dp", "seq", None),
            P("dp", "seq", None),
            P(AXES, None),
            P(AXES, None),
            P(AXES, None),
            P(AXES, None),
            P(AXES, None),
            P(AXES, None),
            P(AXES, None),
            P(None, AXES),
            P(AXES),
            P(AXES),
            P(AXES),
            P(AXES),
            P(AXES),
        ),
        check_vma=False,
    )
```

time: 2380 us -> 780 us (0.33)
  waiting for transfers between devices: 1610 us -> 413 us
  matrix products: 288 us -> 1.22 us
  Pallas kernels: 0 us -> 173 us
  blocking collectives: 80.5 us -> 0 us
  local copies, waits for them, and re-layouts: 170 us -> 106 us
  other arithmetic: 98.8 us -> 34.9 us
  loops' own time: 45.3 us -> 0 us
  starting transfers between devices: 56.6 us -> 22.8 us
    reduce_scatter x8 -> x1, waiting for transfers between devices: 1030 us -> 0.01 us  [body(): lax.psum_scatter(early, AXES, scatter_dimension=0, tiled=True).astype(F32)]
    dot_general x55 -> x2, matrix products: 288 us -> 1.22 us  [the longest x1 0.99 us: body(): t = jnp.dot(table, jnp.asarray(onehot), precision=lax.Precision.HIGHEST)]
    pallas_call x0 -> x19, Pallas kernels: none -> 173 us  [the longest x4 34.1 us: retreat(): pl.pallas_call(partial(retreat_kernel, first), in_specs=[pl.BlockSpec(mem...]
    all_gather x8 -> x2, waiting for transfers between devices: 242 us -> 155 us  [the longest x1 109 us: body(): wa = lax.all_gather(wa, AXES, axis=0, tiled=True)]
    unnamed x2 -> x0, blocking collectives: 80.5 us -> none
    ppermute x6 -> x24, waiting for transfers between devices: 332 us -> 258 us  [the longest x9 140 us: hop(): return lax.ppermute(value, AXES, route)]
    another operation x10 -> x0, loops' own time: 45.3 us -> none  [the longest x4 26.6 us: body(): lax.cond(place == section, retreat, partial(hold, back_stash), adjoint)]
    ppermute x6 -> x24, starting transfers between devices: 55.8 us -> 22.7 us  [the longest x15 13 us: scatter_sum(): got = lax.ppermute(send, AXES, route)]
  transfers between devices with their start and end apart: 23 -> 27, of which waited for: 15 -> 15; matrix products, arithmetic and copies ran while one was open for 19% -> 7% of each run, Pallas kernels for 0% -> 14%
where the time goes in v1:
time: 780 us; the launch traced here: 767 us
  waiting for transfers between devices  413 us (53%)
  Pallas kernels  173 us (22%)
  local copies, waits for them, and re-layouts  106 us (14%)
  other arithmetic  34.9 us (4%)
  starting transfers between devices  22.8 us (3%)
  between operations  15.9 us (2%)
    ppermute x9, waiting for transfers between devices, hop(): return lax.ppermute(value, AXES, route)  140 us
    ppermute x15, waiting for transfers between devices, scatter_sum(): got = lax.ppermute(send, AXES, route)  118 us
    all_gather x1, waiting for transfers between devices, body(): wa = lax.all_gather(wa, AXES, axis=0, tiled=True)  109 us
    unnamed x157, local copies, waits for them, and re-layouts  74 us
    all_gather x1, waiting for transfers between devices, body(): wb = lax.all_gather(wb, AXES, axis=0, tiled=True)  46.3 us
    pallas_call x4, Pallas kernels, retreat(): pl.pallas_call(partial(retreat_kernel, first), in_specs=[pl.BlockSpec(mem...  34.1 us
    pallas_call x1, Pallas kernels, feed_forward(): pl.pallas_call(ffn_kernel, grid=(hidden // tile,), in_specs=[pl.BlockSpec...  33.4 us
    pallas_call x6, Pallas kernels, outer_product(): pl.pallas_call(outer_kernel, grid=(slabs, tiles), in_specs=[pl.BlockSpec(...  29.7 us
  transfers between devices with their start and end apart: 27, of which 15 were waited for; matrix products, arithmetic and copies ran while one was open for 7% of the time, Pallas kernels for 14%

profile of v1, /device:TPU:0, one launch (start us, length us, event | category | flops | bytes accessed | tf_op | source)
XLA Modules:
  0.0 767.3 jit_solution(5524170298307715552)
XLA Ops:
  19.1 108.9 %all-gather.3.cloned.1.call-done.w_ref.init_t_ref.wa_hbm = bf16[1024,7808]{1,0:T(8,128)(2,1)} async-done(((bf16[32,7808]{1,0:T(8,128)(2,1)}), bf16[1024,7808]{1,0:T(8,128)(2,1)}) %all-gather.3.cloned.1.call-update) | async-done | bytes 15990800 | tf_op jit(solution)/shard_map/all_gather | solution.py:888
  129.9 5.5 copy-done
  135.4 7.2 project.1
  145.4 21.2 %advance.4 = (bf16[512,1024]{1,0:T(8,128)(2,1)S(1)}, bf16[512,1024]{1,0:T(8,128)(2,1)S(1)}, bf16[512,1024]{1,0:T(8,128)(2,1)S(1)}, bf16[512,3072]{1,0:T(8,128)(2...) custom-call(s32[2]{0:T(128)S(1)} %pad_add_fusion.flags_ref, ...), custom_call_target="tpu_custom_call" | custom-call | flops 9663676416 | bytes 25165824 | tf_op jit(solution)/shard_map/advance/pallas_call | solution.py:227
  207.6 46.3 %all-gather.5.cloned.1.call-done.w_ref.wu_ref.wd_ref.wo_ref = bf16[1024,9216]{1,0:T(8,128)(2,1)} async-done(((bf16[32,9216]{1,0:T(8,128)(2,1)}), bf16[1024,9216]{1,0:T(8,128)(2,1)}) %all-gather.5.cloned.1.call-update) | async-done | bytes 18874384 | tf_op jit(solution)/shard_map/all_gather | solution.py:889
  257.0 14.8 %token_forward.1 = (bf16[512,1024]{1,0:T(8,128)(2,1)S(1)}, f32[8,512]{1,0:T(8,128)S(1)}, f32[512,1024]{1,0:T(8,128)S(1)}, bf16[512,1024]{1,0:T(8,128)(2,1)S(1)}) custom-call(s32[2]{0:T(128)S(1)} %pad_add_fusion.flags_ref, f32[8,512]{1,0:T(8,128)S(1)} %fusion.26.t_ref, f32[8,1024]{1,0:T(8,128)S(1)} %maximum_maximum_fusion.gains_ref, ...), custom_call_target="tpu_custom_call" | custom-call | flops 4294967296 | bytes 12582912 | tf_op jit(solution)/shard_map/token_forward/pallas_call | solution.py:337
  275.1 33.4 %feed_forward.1 = (bf16[512,4096]{1,0:T(8,128)(2,1)}, bf16[512,4096]{1,0:T(8,128)(2,1)}, bf16[512,1024]{1,0:T(8,128)(2,1)}, f32[512,1024]{1,0:T(8,128)}, bf16[51...) custom-call(f32[8,1024]{1,0:T(8,128)S(1)} %maximum_maximum_fusion.gains_ref, ...), custom_call_target="tpu_custom_call" | custom-call | flops 19327352832 | bytes 33554432 | tf_op jit(solution)/shard_map/feed_forward/pallas_call | solution.py:419
  310.7 19.2 %token_back.1 = (bf16[512,1024]{1,0:T(8,128)(2,1)S(1)}, bf16[2,512,1024]{2,1,0:T(8,128)(2,1)S(1)}, bf16[2,512,1024]{2,1,0:T(8,128)(2,1)S(1)}, f32[8,512]{1,0:T(8,128)S(1)}) custom-call(s32[2]{0:T(128)S(1)} %pad_add_fusion.flags_ref, f32[8,512]{1,0:T(8,128)S(1)} %fusion.26.t_ref, f32[8,512]{1,0:T(8,128)S(1)} %get-tuple-element.113.lse_ref, ...), custom_call_target="tpu_custom_call" | custom-call | flops 5368709120 | bytes 12582912 | tf_op jit(solution)/shard_map/token_back/pallas_call | solution.py:512
  335.9 6.9 weight_grad.9
  342.8 8.2 %weight_grad.10 = bf16[1024,4096]{1,0:T(8,128)(2,1)S(1)} custom-call(bf16[512,4096]{1,0:T(8,128)(2,1)S(1)} %copy-done.36, bf16[512,1024]{1,0:T(8,128)(2,1)S(1)} %bitcast.152), custom_call_target="tpu_custom_call" | custom-call | flops 4294967296 | bytes 16777216 | tf_op jit(solution)/shard_map/weight_grad/pallas_call | solution.py:780
  353.1 13.4 %pad_maximum_fusion = bf16[1024,9216]{1,0:T(8,128)(2,1)} fusion(bf16[1024,4096]{1,0:T(8,128)(2,1)S(1)} %weight_grad.10, bf16[1024,4096]{1,0:T(8,128)(2,1)S(1)} %weight_grad.9, bf16[1024,1024]{1,0:T(8,128)(2,1)S(1)} %weight_grad.8), kind=kLoop, calls=%fused_computation | loop fusion | flops 56623104 | bytes 37748736 | tf_op jit(solution)/shard_map/concatenate | solution.py:941
  371.5 133.0 %collective-permute-done.8.lam_hbm = bf16[512,1024]{1,0:T(8,128)(2,1)S(1)} collective-permute-done((bf16[512,1024]{1,0:T(8,128)(2,1)S(1)}, bf16[512,1024]{1,0:T(8,128)(2,1)S(1)}, u32[]{:S(2)}, u32[]{:S(2)}) %collective-permute-start.8) | collective-permute-done | bytes 1048608 | tf_op jit(solution)/shard_map/ppermute | solution.py:907
  505.5 31.6 %retreat.7 = (bf16[512,1024]{1,0:T(8,128)(2,1)S(1)}, bf16[512,1024]{1,0:T(8,128)(2,1)}, bf16[512,3072]{1,0:T(8,128)(2,1)}, bf16[512,2048]{1,0:T(8,128)(2,1)}, f32[8,1024]{1,0:T(8,128)S(1)}) custom-call(s32[2]{0:T(128)S(1)} %pad_add_fusion.flags_ref, ...), custom_call_target="tpu_custom_call", output_to_operand_aliasing={{1}: (10, {}), {2}: (11, {}), {3}: (12, {}), {4}: (13, {})} | custom-call | flops 13958643712 | bytes 33554432 | tf_op jit(solution)/shard_map/retreat/pallas_call | solution.py:681
  545.1 11.7 %input_grad.1 = (f32[512,1024]{1,0:T(8,128)}, f32[8,1024]{1,0:T(8,128)S(1)}) custom-call(f32[8,1024]{1,0:T(8,128)S(1)} %maximum_maximum_fusion.gains_ref, bf16[512,1024]{1,0:T(8,128)(2,1)S(1)} %bitcast.144, f32[512,1024]{1,0:T(8,128)S(1)} %copy-done.12, bf16[512,3072]{1,0:T(8,128)(2,1)S(1)} %pad_maximum_fusion.1.d_ref.b_ref, ...), custom_call_target="tpu_custom_call" | custom-call | flops 3221225472 | bytes 16777216 | tf_op jit(solution)/shard_map/input_grad/pallas_call | solution.py:745
  570.6 5.2 weight_grad.7
  582.7 5.3 weight_grad.6
  593.9 17.0 %collective-permute-done.20 = bf16[8,32,1664]{2,1,0:T(8,128)(2,1)S(1)} collective-permute-done((bf16[8,32,1664]{2,1,0:T(8,128)(2,1)S(1)}, bf16[8,32,1664]{2,1,0:T(8,128)(2,1)S(1)}, u32[]{:S(2)}, u32[]{:S(2)}) %collective-permute-start.20) | collective-permute-done | bytes 852000 | tf_op jit(solution)/shard_map/ppermute | solution.py:826
  614.1 4.6 collective-permute-done.5
  640.8 30.3 %collective-permute-done.15 = bf16[8,32,3072]{2,1,0:T(8,128)(2,1)S(1)} collective-permute-done((bf16[8,32,3072]{2,1,0:T(8,128)(2,1)S(1)}, bf16[8,32,3072]{2,1,0:T(8,128)(2,1)S(1)}, u32[]{:S(2)}, u32[]{:S(2)}) %collective-permute-start.15) | collective-permute-done | bytes 1572896 | tf_op jit(solution)/shard_map/ppermute | solution.py:826
  672.4 11.8 %collective-permute-done.10 = bf16[8,32,3072]{2,1,0:T(8,128)(2,1)S(1)} collective-permute-done((bf16[8,32,3072]{2,1,0:T(8,128)(2,1)S(1)}, bf16[8,32,3072]{2,1,0:T(8,128)(2,1)S(1)}, u32[]{:S(2)}, u32[]{:S(2)}) %collective-permute-start.10) | collective-permute-done | bytes 1572896 | tf_op jit(solution)/shard_map/ppermute | solution.py:826
  687.4 26.4 %collective-permute-done.16 = bf16[4,32,3072]{2,1,0:T(8,128)(2,1)S(1)} collective-permute-done((bf16[4,32,3072]{2,1,0:T(8,128)(2,1)S(1)}, bf16[4,32,3072]{2,1,0:T(8,128)(2,1)S(1)}, u32[]{:S(2)}, u32[]{:S(2)}) %collective-permute-start.16) | collective-permute-done | bytes 786464 | tf_op jit(solution)/shard_map/ppermute | solution.py:826
  714.9 16.7 %collective-permute-done.11 = bf16[4,32,3072]{2,1,0:T(8,128)(2,1)S(1)} collective-permute-done((bf16[4,32,3072]{2,1,0:T(8,128)(2,1)S(1)}, bf16[4,32,3072]{2,1,0:T(8,128)(2,1)S(1)}, u32[]{:S(2)}, u32[]{:S(2)}) %collective-permute-start.11) | collective-permute-done | bytes 786464 | tf_op jit(solution)/shard_map/ppermute | solution.py:826
  731.9 5.9 collective-permute-done.17
  753.0 4.4 reshape.297
  (296 shorter events, 162.4 us)
Async XLA Ops:
  7.2 120.9 %all-gather.3.cloned.1.call-start = ((), (), s32[]{:S(2)}) async-start(), calls=%async_computation.1 | async-start | bytes 16490496 | tf_op jit(solution)/shard_map/all_gather | solution.py:888
  13.9 240.0 %all-gather.5.cloned.1.call-start = ((), (), s32[]{:S(2)}) async-start(), calls=%async_computation.2 | async-start | bytes 19464192 | tf_op jit(solution)/shard_map/all_gather | solution.py:889
  18.2 729.9 %reduce-scatter.2.cloned.1.call-start = ((), (), s32[]{:S(2)}) async-start(), calls=%async_computation.3 | async-start | bytes 19464192 | tf_op jit(solution)/shard_map/reduce_scatter | solution.py:942
  169.8 3.6 collective-permute-start
  333.6 32.9 %collective-permute-start.6 = (bf16[512,1024]{1,0:T(8,128)(2,1)S(1)}, bf16[512,1024]{1,0:T(8,128)(2,1)}, u32[]{:S(2)}, u32[]{:S(2)}) collective-permute-start(bf16[512,1024]{1,0:T(8,128)(2,1)S(1)} %get-tuple-element.121), channel_id=1, source_target_pairs={{3,2},{7,6},{11,10},{15,14},{19,18},{23,22},{27,26},{31,30}} | collective-permute-start | bytes 3145736 | tf_op jit(solution)/shard_map/ppermute | solution.py:907
  369.7 134.7 %collective-permute-start.8 = (bf16[512,1024]{1,0:T(8,128)(2,1)S(1)}, bf16[512,1024]{1,0:T(8,128)(2,1)S(1)}, u32[]{:S(2)}, u32[]{:S(2)}) collective-permute-start(bf16[512,1024]{1,0:T(8,128)(2,1)S(1)} %get-tuple-element.131), channel_id=1, source_target_pairs={{1,0},{5,4},{9,8},{13,12},{17,16},{21,20},{25,24},{29,28}} | collective-permute-start | bytes 3145736 | tf_op jit(solution)/shard_map/ppermute | solution.py:907
  567.5 13.2 %collective-permute-start.19 = (bf16[16,32,1664]{2,1,0:T(8,128)(2,1)}, bf16[16,32,1664]{2,1,0:T(8,128)(2,1)}, u32[]{:S(2)}, u32[]{:S(2)}) collective-permute-start(bf16[16,32,1664]{2,1,0:T(8,128)(2,1)} %dynamic-slice_bitcast_fusion.2), channel_id=1, source_target_pairs={{0,1},{1,0},{2,3},{3,2},{4,5},{5,4},{6,7},{7,6},{8,9},{9,8},{10,11... | collective-permute-start | bytes 5111816 | tf_op jit(solution)/shard_map/ppermute | solution.py:826
  580.2 42.2 %collective-permute-start.14 = (bf16[16,32,3072]{2,1,0:T(8,128)(2,1)}, bf16[16,32,3072]{2,1,0:T(8,128)(2,1)}, u32[]{:S(2)}, u32[]{:S(2)}) collective-permute-start(bf16[16,32,3072]{2,1,0:T(8,128)(2,1)} %dynamic-slice_bitcast_fusion), channel_id=1, source_target_pairs={{0,1},{1,0},{2,3},{3,2},{4,5},{5,4},{6,7},{7,6},{8,9},{9,8},{10,11... | collective-permute-start | bytes 9437192 | tf_op jit(solution)/shard_map/ppermute | solution.py:826
  582.6 28.3 %collective-permute-start.20 = (bf16[8,32,1664]{2,1,0:T(8,128)(2,1)S(1)}, bf16[8,32,1664]{2,1,0:T(8,128)(2,1)S(1)}, u32[]{:S(2)}, u32[]{:S(2)}) collective-permute-start(bf16[8,32,1664]{2,1,0:T(8,128)(2,1)S(1)} %dynamic-slice_bitcast_fusion.3), channel_id=1, source_target_pairs={{0,2},{1,3},{2,0},{3,1},{4,6},{5,7},{6,4},{7,5},{8,10},{9,11},{10,... | collective-permute-start | bytes 2555912 | tf_op jit(solution)/shard_map/ppermute | solution.py:826
  591.5 36.8 %collective-permute-start.9 = (bf16[16,32,3072]{2,1,0:T(8,128)(2,1)}, bf16[16,32,3072]{2,1,0:T(8,128)(2,1)}, u32[]{:S(2)}, u32[]{:S(2)}) collective-permute-start(bf16[16,32,3072]{2,1,0:T(8,128)(2,1)} %dynamic-slice_bitcast_fusion.1), channel_id=1, source_target_pairs={{0,1},{1,0},{2,3},{3,2},{4,5},{5,4},{6,7},{7,6},{8,9},{9,8},{10,11... | collective-permute-start | bytes 9437192 | tf_op jit(solution)/shard_map/ppermute | solution.py:826
  592.6 20.2 %collective-permute-start.3 = (bf16[128,1024]{1,0:T(8,128)(2,1)S(1)}, bf16[128,1024]{1,0:T(8,128)(2,1)S(1)}, u32[]{:S(2)}, u32[]{:S(2)}) collective-permute-start(bf16[128,1024]{1,0:T(8,128)(2,1)S(1)} %get-tuple-element.168), channel_id=1, source_target_pairs={{3,2},{7,6},{11,10},{15,14},{19,18},{23,22},{27,26},{31,30}} | collective-permute-start | bytes 786440 | tf_op jit(solution)/shard_map/ppermute | solution.py:907
  593.3 20.8 %collective-permute-start.4 = (bf16[128,1024]{1,0:T(8,128)(2,1)}, bf16[128,1024]{1,0:T(8,128)(2,1)S(1)}, u32[]{:S(2)}, u32[]{:S(2)}) collective-permute-start(bf16[128,1024]{1,0:T(8,128)(2,1)} %get-tuple-element.167), channel_id=1, source_target_pairs={{3,1},{7,5},{11,9},{15,13},{19,17},{23,21},{27,25},{31,29}} | collective-permute-start | bytes 786440 | tf_op jit(solution)/shard_map/ppermute | solution.py:907
  610.9 7.8 %collective-permute-start.5 = (bf16[128,1024]{1,0:T(8,128)(2,1)S(1)}, bf16[128,1024]{1,0:T(8,128)(2,1)}, u32[]{:S(2)}, u32[]{:S(2)}) collective-permute-start(bf16[128,1024]{1,0:T(8,128)(2,1)S(1)} %get-tuple-element.166), channel_id=1, source_target_pairs={{3,0},{7,4},{11,8},{15,12},{19,16},{23,20},{27,24},{31,28}} | collective-permute-start | bytes 786440 | tf_op jit(solution)/shard_map/ppermute | solution.py:907
  612.8 9.4 %collective-permute-start.21 = (bf16[4,32,1664]{2,1,0:T(8,128)(2,1)S(1)}, bf16[4,32,1664]{2,1,0:T(8,128)(2,1)S(1)}, u32[]{:S(2)}, u32[]{:S(2)}) collective-permute-start(bf16[4,32,1664]{2,1,0:T(8,128)(2,1)S(1)} %dynamic-slice_bitcast_fusion.5), channel_id=1, source_target_pairs={{0,4},{1,5},{2,6},{3,7},{4,0},{5,1},{6,2},{7,3},{8,12},{9,13},{10,... | collective-permute-start | bytes 1277960 | tf_op jit(solution)/shard_map/ppermute | solution.py:826
  622.3 9.1 %collective-permute-start.22 = (bf16[2,32,1664]{2,1,0:T(8,128)(2,1)S(1)}, bf16[2,32,1664]{2,1,0:T(8,128)(2,1)S(1)}, u32[]{:S(2)}, u32[]{:S(2)}) collective-permute-start(bf16[2,32,1664]{2,1,0:T(8,128)(2,1)S(1)} %dynamic-slice_bitcast_fusion.8), channel_id=1, source_target_pairs={{0,8},{1,9},{2,10},{3,11},{4,12},{5,13},{6,14},{7,15},{8,0},{9,1},... | collective-permute-start | bytes 638984 | tf_op jit(solution)/shard_map/ppermute | solution.py:826
  627.0 44.1 %collective-permute-start.15 = (bf16[8,32,3072]{2,1,0:T(8,128)(2,1)S(1)}, bf16[8,32,3072]{2,1,0:T(8,128)(2,1)S(1)}, u32[]{:S(2)}, u32[]{:S(2)}) collective-permute-start(bf16[8,32,3072]{2,1,0:T(8,128)(2,1)S(1)} %bitcast.174), channel_id=1, source_target_pairs={{0,4},{1,5},{2,6},{3,7},{4,0},{5,1},{6,2},{7,3},{8,12},{9,13},{10,... | collective-permute-start | bytes 4718600 | tf_op jit(solution)/shard_map/ppermute | solution.py:826
  631.6 6.4 collective-permute-start.23
  633.3 50.8 %collective-permute-start.10 = (bf16[8,32,3072]{2,1,0:T(8,128)(2,1)S(1)}, bf16[8,32,3072]{2,1,0:T(8,128)(2,1)S(1)}, u32[]{:S(2)}, u32[]{:S(2)}) collective-permute-start(bf16[8,32,3072]{2,1,0:T(8,128)(2,1)S(1)} %bitcast.175), channel_id=1, source_target_pairs={{0,8},{1,9},{2,10},{3,11},{4,12},{5,13},{6,14},{7,15},{8,0},{9,1},... | collective-permute-start | bytes 4718600 | tf_op jit(solution)/shard_map/ppermute | solution.py:826
  671.9 41.9 %collective-permute-start.16 = (bf16[4,32,3072]{2,1,0:T(8,128)(2,1)S(1)}, bf16[4,32,3072]{2,1,0:T(8,128)(2,1)S(1)}, u32[]{:S(2)}, u32[]{:S(2)}) collective-permute-start(bf16[4,32,3072]{2,1,0:T(8,128)(2,1)S(1)} %bitcast.178), channel_id=1, source_target_pairs={{0,8},{1,9},{2,10},{3,11},{4,12},{5,13},{6,14},{7,15},{8,0},{9,1},... | collective-permute-start | bytes 2359304 | tf_op jit(solution)/shard_map/ppermute | solution.py:826
  684.9 46.7 %collective-permute-start.11 = (bf16[4,32,3072]{2,1,0:T(8,128)(2,1)S(1)}, bf16[4,32,3072]{2,1,0:T(8,128)(2,1)S(1)}, u32[]{:S(2)}, u32[]{:S(2)}) collective-permute-start(bf16[4,32,3072]{2,1,0:T(8,128)(2,1)S(1)} %dynamic-slice_bitcast_fusion.4), channel_id=1, source_target_pairs={{0,16},{1,17},{2,18},{3,19},{4,20},{5,21},{6,22},{7,23},{8,24},{9,... | collective-permute-start | bytes 2359304 | tf_op jit(solution)/shard_map/ppermute | solution.py:826
  714.1 23.8 %collective-permute-start.17 = (bf16[2,32,3072]{2,1,0:T(8,128)(2,1)S(1)}, bf16[2,32,3072]{2,1,0:T(8,128)(2,1)S(1)}, u32[]{:S(2)}, u32[]{:S(2)}) collective-permute-start(bf16[2,32,3072]{2,1,0:T(8,128)(2,1)S(1)} %dynamic-slice_bitcast_fusion.6), channel_id=1, source_target_pairs={{0,16},{1,17},{2,18},{3,19},{4,20},{5,21},{6,22},{7,23},{8,24},{9,... | collective-permute-start | bytes 1179656 | tf_op jit(solution)/shard_map/ppermute | solution.py:826
  731.9 8.2 %collective-permute-start.12 = (bf16[2,32,3072]{2,1,0:T(8,128)(2,1)S(1)}, bf16[2,32,3072]{2,1,0:T(8,128)(2,1)S(1)}, u32[]{:S(2)}, u32[]{:S(2)}) collective-permute-start(bf16[2,32,3072]{2,1,0:T(8,128)(2,1)S(1)} %dynamic-slice_bitcast_fusion.7), channel_id=1, source_target_pairs={{0,2},{1,3},{2,0},{3,1},{4,6},{5,7},{6,4},{7,5},{8,10},{9,11},{10,... | collective-permute-start | bytes 1179656 | tf_op jit(solution)/shard_map/ppermute | solution.py:826
  738.0 7.9 %collective-permute-start.18 = (bf16[1,32,3072]{2,1,0:T(8,128)(2,1)S(1)}, bf16[1,32,3072]{2,1,0:T(8,128)(2,1)S(1)}, u32[]{:S(2)}, u32[]{:S(2)}) collective-permute-start(bf16[1,32,3072]{2,1,0:T(8,128)(2,1)S(1)} %constant_dynamic-slice_fusion.1), channel_id=1, source_target_pairs={{0,2},{1,3},{2,0},{3,1},{4,6},{5,7},{6,4},{7,5},{8,10},{9,11},{10,... | collective-permute-start | bytes 589832 | tf_op jit(solution)/shard_map/ppermute | solution.py:826
  740.2 7.1 collective-permute-start.13
  (78 other events, 429.3 us)
Sparse Core Ops, SparseCore 0:
  14.0 113.9 all-gather.2
  130.9 122.8 all-gather.4
  366.6 311.6 reduce-scatter.1

commit v2 on v1

v2 whole, which is shorter than its diff:
```python
from functools import partial

import jax
import jax.numpy as jnp
import numpy as np
from jax import lax
from jax.experimental import pallas as pl
from jax.experimental.pallas import tpu as pltpu
from jax.sharding import PartitionSpec as P

HEADS = 8
HEAD = 128
BUCKETS = 32
MAX_DIST = 128
EPS = 1e-05
NEG = -1e30
SCALE = HEAD ** (-0.5)
AXES = ("dp", "seq")
F32 = jnp.float32
BF16 = jnp.bfloat16
MIB = 1 << 20
VMEM_LIMIT = 60 * MIB
LOG2E = 1.4426950408889634
NO_COST = pl.CostEstimate(flops=0, bytes_accessed=0, transcendentals=0)
Q_SCALE = SCALE * LOG2E


def bucket_of(length):
    dist = np.arange(length)
    exact = BUCKETS // 2
    scaled = np.log(np.maximum(dist, exact) / exact) / np.log(MAX_DIST / exact) * (BUCKETS - exact)
    far = np.minimum(exact + np.floor(scaled).astype(np.int32), BUCKETS - 1)
    return np.where(dist < exact, dist, far).astype(np.int32)


def dot_nn(a, b):
    return jnp.dot(a, b, preferred_element_type=F32)


def dot_nt(a, b):
    return lax.dot_general(a, b, (((1,), (1,)), ((), ())), preferred_element_type=F32)


def norm_parts(x):
    mean = jnp.mean(x, axis=-1, keepdims=True)
    centered = x - mean
    spread = jnp.mean(centered * centered, axis=-1, keepdims=True)
    rstd = lax.rsqrt(spread + EPS)
    return centered * rstd, rstd


def norm_back(x, gain, dy):
    xhat, rstd = norm_parts(x)
    dyg = dy * gain
    mean_one = jnp.mean(dyg, axis=-1, keepdims=True)
    mean_two = jnp.mean(dyg * xhat, axis=-1, keepdims=True)
    return rstd * (dyg - mean_one - xhat * mean_two), dy * xhat


def row_iota(rows, cols):
    return lax.broadcasted_iota(jnp.int32, (rows, cols), 0)


def columns(start, size):
    return slice(start, start + size)


def pipeline(count, first, second, third):
    one, two = {}, {}
    for i in range(count + 2):
        if i < count:
            one[i] = first(i)
        if i >= 2:
            third(i - 2, two.pop(i - 2))
        if 1 <= i <= count:
            two[i - 1] = second(i - 1, one.pop(i - 1))


def start_all(pairs, sem, base=0):
    copies = [pltpu.make_async_copy(src, dst, sem.at[base + n]) for n, (src, dst) in enumerate(pairs)]
    for copy in copies:
        copy.start()
    return copies


def wait_all(copies):
    for copy in copies:
        copy.wait()


def soft_forward(one, two):
    top = jnp.maximum(jnp.max(one, axis=0, keepdims=True), jnp.max(two, axis=0, keepdims=True))
    one = jnp.exp2(one - top)
    two = jnp.exp2(two - top)
    total = jnp.sum(one, axis=0, keepdims=True) + jnp.sum(two, axis=0, keepdims=True)
    return one.astype(BF16), two.astype(BF16), 1.0 / total, top + jnp.log2(total)


def soft_backward(one, two, done, dtwo, lse):
    one = jnp.exp2(one - lse)
    two = jnp.exp2(two - lse)
    inner = jnp.sum(one * done, axis=0, keepdims=True) + jnp.sum(two * dtwo, axis=0, keepdims=True)
    return one.astype(BF16), two.astype(BF16), one * (done - inner), two * (dtwo - inner)


def row_chunks(rows, chunk, body):
    def step(i, carry):
        body(pl.ds(pl.multiple_of(i * chunk, chunk), chunk))
        return carry

    lax.fori_loop(0, rows // chunk, step, 0)


HBM = pl.BlockSpec(memory_space=pltpu.HBM)
SMEM = pl.BlockSpec(memory_space=pltpu.SMEM)
VMEM = pl.BlockSpec(memory_space=pltpu.VMEM)
CHUNK = 128
A_KV, A_STATE, A_MERGE, A_INIT, A_VEC, A_END = 0, 2048, 5120, 6144, 6656, 6784
B_Q, B_OUT, B_UP, B_DOWN, B_END = 0, 1024, 2048, 6144, 10240


def shape(dims, kind):
    return jax.ShapeDtypeStruct(dims, kind)


def advance_kernel(first, flags_ref, gains_ref, c_hbm, wa_hbm, kv_hbm, *refs):
    if first:
        x_hbm = c_hbm
        (kv_out, h1_out) = refs[:2]
        refs = refs[2:]
    else:
        refs = refs[6:]
    (new_hbm, cs_hbm, hc_hbm, ckvq_hbm, upd_hbm, z_hbm, lse_hbm) = refs[:7]
    refs = refs[7:]
    (c_v, w_v, m_v, kv_v, hc_v, ckvq_v, upd_v, z_v, new_v, lse_v, sem) = refs[:11]
    states, width = c_v.shape
    w_src = wa_hbm.at[:, pl.ds(A_STATE, 3 * width)]
    m_src = wa_hbm.at[:, pl.ds(A_MERGE, width)]
    if first:
        x_v, wkv_v, h1_v, init_v = refs[11:]
        begun = start_all(
            (
                (x_hbm, x_v),
                (wa_hbm.at[:, pl.ds(A_KV, 2 * width)], wkv_v),
                (wa_hbm.at[:, pl.ds(A_INIT, states)], init_v),
                (w_src, w_v),
                (m_src, m_v),
            ),
            sem,
            8,
        )
        begun[0].wait()

        def token_chunk(rows):
            xhat, _ = norm_parts(x_v[rows, :].astype(F32))
            h1_v[rows, :] = (xhat * gains_ref[0:1, :]).astype(BF16)

        row_chunks(x_v.shape[0], CHUNK, token_chunk)
        begun[1].wait()
        for t in range(4):
            cols = columns(512 * t, 512)
            kv_v[:, cols] = dot_nn(h1_v[...], wkv_v[:, cols]).astype(BF16)
        sent = start_all(((kv_v, kv_out), (h1_v, h1_out)), sem, 13)
        wait_all(begun[2:])

    @pl.when(flags_ref[0] == 1)
    def _():
        if first:
            c_v[...] = init_v[...].T
            begun_here = []
        else:
            begun_here = start_all(
                ((c_hbm, c_v), (w_src, w_v), (kv_hbm, kv_v), (m_src, m_v)), sem, 8
            )
            begun_here[0].wait()
        outs = start_all(((c_v, cs_hbm),), sem)

        def norm_chunk(rows):
            xhat, _ = norm_parts(c_v[rows, :].astype(F32))
            hc_v[rows, :] = (xhat * gains_ref[2:3, :]).astype(BF16)

        row_chunks(states, CHUNK, norm_chunk)
        outs += start_all(((hc_v, hc_hbm),), sem, 1)
        for copy in begun_here[1:2]:
            copy.wait()
        for t in range(6):
            cols = columns(512 * t, 512)
            product = dot_nn(hc_v[...], w_v[:, cols])
            ckvq_v[:, cols] = (product if t < 4 else product * Q_SCALE).astype(BF16)
        outs += start_all(((ckvq_v, ckvq_hbm),), sem, 2)
        wait_all(begun_here[2:])
        nvalid = flags_ref[1]
        allowed = row_iota(kv_v.shape[0], states) < nvalid

        def scores(h):
            q = ckvq_v[:, columns(2 * width + h * HEAD, HEAD)]
            return (
                dot_nt(ckvq_v[:, columns(h * HEAD, HEAD)], q),
                dot_nt(kv_v[:, columns(h * HEAD, HEAD)], q),
            )

        def soft(h, pair):
            return soft_forward(pair[0], jnp.where(allowed, pair[1], NEG))

        def mix(h, parts):
            one, two, factor, lse = parts
            mixed = dot_nn(ckvq_v[:, columns(width + h * HEAD, HEAD)].T, one)
            mixed += dot_nn(kv_v[:, columns(width + h * HEAD, HEAD)].T, two)
            upd_v[:, columns(h * HEAD, HEAD)] = (mixed * factor).T.astype(BF16)
            lse_v[h : h + 1, :] = lse

        pipeline(HEADS, scores, soft, mix)
        outs += start_all(((upd_v, upd_hbm), (lse_v, lse_hbm)), sem, 3)
        z_v[...] = dot_nn(upd_v[...], m_v[...])
        outs += start_all(((z_v, z_hbm),), sem, 5)

        def gate_chunk(rows):
            gate = gains_ref[3:4, :]
            new = gate * c_v[rows, :].astype(F32) + (1.0 - gate) * z_v[rows, :]
            new_v[rows, :] = new.astype(BF16)

        row_chunks(states, CHUNK, gate_chunk)
        outs += start_all(((new_v, new_hbm),), sem, 6)
        wait_all(outs)

    if first:
        wait_all(sent)


def advance(flags, gains, c, wa, kv, stash):
    states, width = c.shape
    rows = states if kv is None else kv.shape[0]
    first = stash is None
    extra = () if first else tuple(stash)
    shapes = [
        shape((states, width), BF16),
        shape((states, width), BF16),
        shape((states, width), BF16),
        shape((states, 3 * width), BF16),
        shape((states, width), BF16),
        shape((states, width), F32),
        shape((HEADS, states), F32),
    ]
    scratch = [
        pltpu.VMEM((states, width), BF16),
        pltpu.VMEM((width, 3 * width), BF16),
        pltpu.VMEM((width, width), BF16),
        pltpu.VMEM((rows, 2 * width), BF16),
        pltpu.VMEM((states, width), BF16),
        pltpu.VMEM((states, 3 * width), BF16),
        pltpu.VMEM((states, width), BF16),
        pltpu.VMEM((states, width), F32),
        pltpu.VMEM((states, width), BF16),
        pltpu.VMEM((HEADS, states), F32),
        pltpu.SemaphoreType.DMA((15,)),
    ]
    if first:
        kernel = lambda f, g, x, w, *refs: advance_kernel(True, f, g, x, w, None, *refs)
        shapes = [shape((rows, 2 * width), BF16), shape((rows, width), BF16)] + shapes
        scratch += [
            pltpu.VMEM((rows, width), BF16),
            pltpu.VMEM((width, 2 * width), BF16),
            pltpu.VMEM((rows, width), BF16),
            pltpu.VMEM((width, states), BF16),
        ]
        args = (flags, gains, c, wa)
    else:
        kernel = partial(advance_kernel, False)
        args = (flags, gains, c, wa, kv) + extra
    return pl.pallas_call(
        kernel,
        in_specs=[SMEM, VMEM] + [HBM] * (len(args) - 2),
        out_specs=[HBM] * len(shapes),
        out_shape=shapes,
        scratch_shapes=scratch,
        input_output_aliases={} if first else {5 + i: 1 + i for i in range(6)},
        compiler_params=pltpu.CompilerParams(vmem_limit_bytes=VMEM_LIMIT),
        cost_estimate=pl.CostEstimate(flops=9 << 30, bytes_accessed=24 * MIB, transcendentals=4 * MIB),
        name="advance",
    )(*args)


def bias_tiles(t_row):
    spread = jnp.broadcast_to(t_row, (128, t_row.shape[1]))
    grid = pltpu.roll(spread, 0, axis=1, stride=1, stride_axis=0)
    lane = lax.broadcasted_iota(jnp.int32, (128, 128), 1)
    sub = lax.broadcasted_iota(jnp.int32, (128, 128), 0)
    tiles = [grid[:, 128 * d : 128 * d + 128] for d in range(4)]
    tiles[0] = jnp.where(lane >= sub, tiles[0], NEG)
    return tiles


def bias_part(tiles, part):
    none = jnp.full((128, 128), NEG, F32)
    rows = []
    for j in range(2 * part + 2):
        row = [tiles[i - j] if i >= j else none for i in (2 * part, 2 * part + 1)]
        rows.append(jnp.concatenate(row, axis=1))
    return jnp.concatenate(rows, axis=0)


def block_kernel(flags_ref, t_ref, gains_ref, x_hbm, g_hbm, h1_hbm, kv_hbm, ckvq_hbm, wb_hbm,
                 o_hbm, x1_hbm, h2_hbm, act_hbm, dup_hbm, dx1_hbm, da_hbm, dq_hbm, dkv_hbm, dst_hbm,
                 db_ref, sums_ref,
                 x_v, g_v, q_v, kv_v, ckv_v, wo_v, wu_v, wd_v, o_v, x1_v, h2_v, act_v, dup_v,
                 dh_v, do_v, dq_v, dkv_v, dst_v, lse_v, wq_v, sem):
    rows, width = x_v.shape
    half = HEADS // 2 * HEAD
    loads = []
    for s in range(2):
        here, there = pl.ds(s * half, half), pl.ds(width + s * half, half)
        loads += [
            (wb_hbm.at[:, pl.ds(B_Q + s * half, half)], wq_v.at[:, here]),
            (ckvq_hbm.at[:, here], ckv_v.at[:, here]),
            (kv_hbm.at[:, here], kv_v.at[:, here]),
            (ckvq_hbm.at[:, there], ckv_v.at[:, there]),
            (kv_hbm.at[:, there], kv_v.at[:, there]),
        ]
    loads += [
        (wb_hbm.at[:, pl.ds(B_OUT, width)], wo_v),
        (x_hbm, x_v),
        (g_hbm, g_v),
        (wb_hbm.at[:, pl.ds(B_UP, 4 * width)], wu_v),
        (wb_hbm.at[:, pl.ds(B_DOWN, 4 * width)], wd_v),
    ]
    h1_in = start_all([(h1_hbm, do_v)], sem, 26)
    begun = start_all(loads, sem)
    wait_all(h1_in)
    nvalid = flags_ref[1]
    units = [(h, part) for h in range(HEADS) for part in range(2)]
    tile_cache = {}

    def tiles_of(h, key):
        if (h, key) not in tile_cache:
            tile_cache.clear()
            tile_cache[(h, key)] = bias_tiles(t_ref[h : h + 1, :])
        return tile_cache[(h, key)]

    def pick(n):
        h, part = units[n]
        return h, part, columns(256 * part, 256), 256 * (part + 1), columns(h * HEAD, HEAD), columns(width + h * HEAD, HEAD)

    def masked(scores, h, part, key):
        scores = scores + bias_part(tiles_of(h, key), part)
        return jnp.where(row_iota(scores.shape[0], 256) < nvalid, scores, NEG)

    def scores(n):
        h, part, span, used, here, there = pick(n)
        if part == 0 and h in (0, HEADS // 2):
            s = h // (HEADS // 2)
            wait_all(begun[5 * s :][:5])
            cols = columns(s * half, half)
            q_v[:, cols] = (dot_nn(do_v[...], wq_v[:, cols]) * Q_SCALE).astype(BF16)
        q = q_v[span, here]
        return dot_nt(ckv_v[:, here], q), dot_nt(kv_v[:used, here], q)

    def soft(n, pair):
        h, part, span, used, here, there = pick(n)
        return soft_forward(pair[0], masked(pair[1], h, part, 0))

    def mix(n, parts):
        h, part, span, used, here, there = pick(n)
        one, two, factor, lse = parts
        mixed = dot_nn(ckv_v[:, there].T, one) + dot_nn(kv_v[:used, there].T, two)
        o_v[span, here] = (mixed * factor).T.astype(BF16)
        lse_v[h : h + 1, span] = lse

    pipeline(len(units), scores, soft, mix)
    wait_all(begun[10:12])
    x1_v[...] = x_v[...].astype(F32) + dot_nn(o_v[...], wo_v[...])

    def norm_chunk(span):
        xhat, _ = norm_parts(x1_v[span, :])
        h2_v[span, :] = (xhat * gains_ref[1:2, :]).astype(BF16)

    row_chunks(rows, CHUNK, norm_chunk)
    outs = start_all(((o_v, o_hbm), (x1_v, x1_hbm), (h2_v, h2_hbm)), sem, 16)
    wait_all(begun[12:15])

    tile = 512

    def hidden(i):
        slab = wd_v[columns(tile * (i % 2), tile), columns(width * (i // 2), width)]
        return dot_nn(h2_v[...], wu_v[:, columns(tile * i, tile)]), dot_nt(g_v[...], slab)

    def activate(i, pair):
        up, dact = pair
        root = 0.7978845608028654
        square = up * up
        th = jnp.tanh(up * (root + (root * 0.044715) * square))
        part = 0.5 + 0.5 * th
        slope = part + up * (part - part * part) * (2 * root + (6 * root * 0.044715) * square)
        act_v[:, columns(tile * i, tile)] = (up * part).astype(BF16)
        dup_v[:, columns(tile * i, tile)] = (dact * slope).astype(BF16)

    pipeline(4 * width // tile, hidden, activate, lambda i, nothing: None)
    outs += start_all(((act_v, act_hbm), (dup_v, dup_hbm)), sem, 19)
    dh_v[...] = dot_nt(dup_v[...], wu_v[...])
    sums_ref[...] = jnp.zeros_like(sums_ref)

    def back_chunk(span):
        dx, gain_term = norm_back(x1_v[span, :], gains_ref[1:2, :], dh_v[span, :])
        dx = dx + g_v[span, :].astype(F32)
        dh_v[span, :] = dx
        x_v[span, :] = dx.astype(BF16)
        sums_ref[0:1, :] += jnp.sum(gain_term, axis=0, keepdims=True)

    row_chunks(rows, CHUNK, back_chunk)
    outs += start_all(((dh_v, dx1_hbm), (x_v, da_hbm)), sem, 21)
    do_v[...] = dot_nt(x_v[...], wo_v[...]).astype(BF16)

    held = {}

    def back_scores(n):
        h, part, span, used, here, there = pick(n)
        q, do = q_v[span, here], do_v[span, here]
        return (
            dot_nt(ckv_v[:, here], q),
            dot_nt(kv_v[:used, here], q),
            dot_nt(ckv_v[:, there], do),
            dot_nt(kv_v[:used, there], do),
        )

    def back_soft(n, parts):
        h, part, span, used, here, there = pick(n)
        lse = lse_v[h : h + 1, span]
        p1, p2, d1, d2 = soft_backward(
            parts[0], masked(parts[1], h, part, 1), parts[2], parts[3], lse
        )
        shear = held.setdefault(("shear", h), [0.0] * 4)
        for j in range(2 * part + 2):
            for i in (0, 1):
                d = 2 * part + i - j
                if d >= 0:
                    shear[d] = shear[d] + d2[128 * j : 128 * j + 128, 128 * i : 128 * i + 128]
        if part == 1:
            grid = jnp.concatenate(held.pop(("shear", h)), axis=1)
            size = grid.shape[1]
            flipped = grid[:8]
            for group in range(1, 16):
                flipped += pltpu.roll(grid[8 * group : 8 * group + 8], size - 8 * group, axis=1)
            for step in (1, 2, 4):
                moved = pltpu.roll(flipped, size - step, axis=1)
                flipped = jnp.where((row_iota(8, size) // step) % 2 == 1, moved, flipped)
            db_ref[h : h + 1, :] = jnp.sum(flipped, axis=0, keepdims=True)
        return p1, p2, d1.astype(BF16), d2.astype(BF16)

    def back_mix(n, parts):
        h, part, span, used, here, there = pick(n)
        p1, p2, d1, d2 = parts
        q, do = q_v[span, here], do_v[span, here]
        terms = [dot_nn(d1, q), dot_nn(p1, do), dot_nn(d2, q), dot_nn(p2, do)]
        dqt = dot_nn(ckv_v[:, here].T, d1) + dot_nn(kv_v[:used, here].T, d2)
        dq_v[span, here] = (dqt.T * SCALE).astype(BF16)
        if part == 0:
            held[("terms", h)] = terms
            return
        before = held.pop(("terms", h))
        dst_v[:, here] = ((before[0] + terms[0]) * (1.0 / LOG2E)).astype(BF16)
        dst_v[:, there] = (before[1] + terms[1]).astype(BF16)
        dkv_v[:256, here] = ((before[2] + terms[2][:256]) * (1.0 / LOG2E)).astype(BF16)
        dkv_v[256:, here] = (terms[2][256:] * (1.0 / LOG2E)).astype(BF16)
        dkv_v[:256, there] = (before[3] + terms[3][:256]).astype(BF16)
        dkv_v[256:, there] = terms[3][256:].astype(BF16)

    pipeline(len(units), back_scores, back_soft, back_mix)
    outs += start_all(((dq_v, dq_hbm), (dkv_v, dkv_hbm), (dst_v, dst_hbm)), sem, 23)
    wait_all(outs)


def block_part(flags, t, gains, x, g, h1, kv, ckvq, wb):
    rows, width = x.shape
    states = ckvq.shape[0]
    hidden = 4 * width
    narrow, wide = shape((rows, width), BF16), shape((rows, width), F32)
    return pl.pallas_call(
        block_kernel,
        in_specs=[SMEM, VMEM, VMEM] + [HBM] * 6,
        out_specs=[HBM] * 10 + [VMEM] * 2,
        out_shape=[
            narrow,
            wide,
            narrow,
            shape((rows, hidden), BF16),
            shape((rows, hidden), BF16),
            wide,
            narrow,
            narrow,
            shape((rows, 2 * width), BF16),
            shape((states, 2 * width), BF16),
            shape((HEADS, rows), F32),
            shape((8, width), F32),
        ],
        scratch_shapes=[
            pltpu.VMEM((rows, width), BF16),
            pltpu.VMEM((rows, width), BF16),
            pltpu.VMEM((rows, width), BF16),
            pltpu.VMEM((rows, 2 * width), BF16),
            pltpu.VMEM((states, 2 * width), BF16),
            pltpu.VMEM((width, width), BF16),
            pltpu.VMEM((width, hidden), BF16),
            pltpu.VMEM((width, hidden), BF16),
            pltpu.VMEM((rows, width), BF16),
            pltpu.VMEM((rows, width), F32),
            pltpu.VMEM((rows, width), BF16),
            pltpu.VMEM((rows, hidden), BF16),
            pltpu.VMEM((rows, hidden), BF16),
            pltpu.VMEM((rows, width), F32),
            pltpu.VMEM((rows, width), BF16),
            pltpu.VMEM((rows, width), BF16),
            pltpu.VMEM((rows, 2 * width), BF16),
            pltpu.VMEM((states, 2 * width), BF16),
            pltpu.VMEM((HEADS, rows), F32),
            pltpu.VMEM((width, width), BF16),
            pltpu.SemaphoreType.DMA((27,)),
        ],
        compiler_params=pltpu.CompilerParams(vmem_limit_bytes=VMEM_LIMIT),
        cost_estimate=pl.CostEstimate(flops=25 << 30, bytes_accessed=40 * MIB, transcendentals=10 * MIB),
        name="block_part",
    )(flags, t, gains, x, g, h1, kv, ckvq, wb)


def retreat_kernel(first, looped, flags_ref, gains_ref, lam_hbm, wa_hbm, kv_hbm, cs_hbm, ckvq_hbm, z_hbm,
                   lse_hbm, dst_hbm, *refs):
    if not first:
        refs = refs[4:]
    (prev_hbm, dz_hbm, dcs_hbm, dkv_hbm, sums_hbm) = refs[:5]
    (lam_v, w_v, m_v, kv_v, c_v, ckvq_v, z_v, lse_v, dst_v,
     dz_v, du_v, dcs_v, dkv_v, dh_v, prev_v, sums_v, sem) = refs[5:]
    states, width = c_v.shape

    @pl.when(flags_ref[0] == 1)
    def _():
        begun = start_all(
            (
                (lam_hbm, lam_v),
                (cs_hbm, c_v),
                (z_hbm, z_v),
                (wa_hbm.at[:, pl.ds(A_MERGE, width)], m_v),
                (ckvq_hbm, ckvq_v),
                (kv_hbm, kv_v),
                (lse_hbm, lse_v),
                (dst_hbm, dst_v),
                (wa_hbm.at[:, pl.ds(A_STATE, 3 * width)], w_v),
            ),
            sem,
        )
        wait_all(begun[:3])
        sums_v[...] = jnp.zeros_like(sums_v)

        def gate_chunk(rows):
            lam = lam_v[rows, :].astype(F32)
            dz_v[rows, :] = ((1.0 - gains_ref[3:4, :]) * lam).astype(BF16)
            change = lam * (c_v[rows, :].astype(F32) - z_v[rows, :])
            sums_v[1:2, :] += jnp.sum(change, axis=0, keepdims=True)

        row_chunks(states, CHUNK, gate_chunk)
        outs = start_all(((dz_v, dz_hbm),), sem, 9)
        begun[3].wait()
        du_v[...] = dot_nt(dz_v[...], m_v[...]).astype(BF16)
        wait_all(begun[4:8])
        allowed = row_iota(kv_v.shape[0], states) < flags_ref[1]

        def pick(h):
            starts = [base + h * HEAD for base in (0, width, 2 * width)]
            return [pl.ds(pl.multiple_of(n, HEAD) if looped else n, HEAD) for n in starts]

        def scores(h):
            here, there, third = pick(h)
            q, du = ckvq_v[:, third], du_v[:, here]
            return (
                dot_nt(ckvq_v[:, here], q),
                dot_nt(kv_v[:, here], q),
                dot_nt(ckvq_v[:, there], du),
                dot_nt(kv_v[:, there], du),
            )

        def soft(h, parts):
            one, two, done, dtwo = parts
            two = jnp.where(allowed, two, NEG)
            p1, p2, d1, d2 = soft_backward(one, two, done, dtwo, lse_v[pl.ds(h, 1), :])
            return p1, p2, d1.astype(BF16), d2.astype(BF16)

        def mix(h, parts):
            here, there, third = pick(h)
            p1, p2, d1, d2 = parts
            q, du = ckvq_v[:, third], du_v[:, here]
            ln2 = 1.0 / LOG2E
            dcs_v[:, here] = (dot_nn(d1, q) * ln2 + dst_v[:, here].astype(F32)).astype(BF16)
            dcs_v[:, there] = (dot_nn(p1, du) + dst_v[:, there].astype(F32)).astype(BF16)
            dkv_v[:, here] = (dot_nn(d2, q) * ln2).astype(BF16)
            dkv_v[:, there] = dot_nn(p2, du).astype(BF16)
            dqt = dot_nn(ckvq_v[:, here].T, d1) + dot_nn(kv_v[:, here].T, d2)
            dcs_v[:, third] = (dqt.T * SCALE).astype(BF16)

        def some(block, carry):
            base = 2 * block
            pipeline(2, lambda h: scores(base + h), lambda h, p: soft(base + h, p), lambda h, p: mix(base + h, p))
            return carry

        if looped:
            lax.fori_loop(0, HEADS // 2, some, 0)
        else:
            pipeline(HEADS, scores, soft, mix)
        outs += start_all(((dcs_v, dcs_hbm), (dkv_v, dkv_hbm)), sem, 10)
        begun[8].wait()
        dh_v[...] = dot_nt(dcs_v[...], w_v[...])

        def norm_chunk(rows):
            dx, gain_term = norm_back(c_v[rows, :].astype(F32), gains_ref[2:3, :], dh_v[rows, :])
            prev = dx + gains_ref[3:4, :] * lam_v[rows, :].astype(F32)
            prev_v[rows, :] = prev.astype(BF16)
            sums_v[0:1, :] += jnp.sum(gain_term, axis=0, keepdims=True)

        row_chunks(states, CHUNK, norm_chunk)
        outs += start_all(((prev_v, prev_hbm), (sums_v, sums_hbm)), sem, 12)
        wait_all(outs)


def retreat(flags, gains, lam, wa, kv, cs, ckvq, z, lse, dst, stash, looped):
    states, width = cs.shape
    rows = kv.shape[0]
    first = stash is None
    extra = () if first else tuple(stash)
    out = pl.pallas_call(
        partial(retreat_kernel, first, looped),
        in_specs=[SMEM, VMEM] + [HBM] * (8 + len(extra)),
        out_specs=[HBM] * 5,
        out_shape=[
            shape((states, width), BF16),
            shape((states, width), BF16),
            shape((states, 3 * width), BF16),
            shape((rows, 2 * width), BF16),
            shape((8, width), F32),
        ],
        scratch_shapes=[
            pltpu.VMEM((states, width), lam.dtype),
            pltpu.VMEM((width, 3 * width), BF16),
            pltpu.VMEM((width, width), BF16),
            pltpu.VMEM((rows, 2 * width), BF16),
            pltpu.VMEM((states, width), BF16),
            pltpu.VMEM((states, 3 * width), BF16),
            pltpu.VMEM((states, width), F32),
            pltpu.VMEM((HEADS, states), F32),
            pltpu.VMEM((states, 2 * width), BF16),
            pltpu.VMEM((states, width), BF16),
            pltpu.VMEM((states, width), BF16),
            pltpu.VMEM((states, 3 * width), BF16),
            pltpu.VMEM((rows, 2 * width), BF16),
            pltpu.VMEM((states, width), F32),
            pltpu.VMEM((states, width), BF16),
            pltpu.VMEM((8, width), F32),
            pltpu.SemaphoreType.DMA((14,)),
        ],
        input_output_aliases={} if first else {10 + i: 1 + i for i in range(4)},
        compiler_params=pltpu.CompilerParams(vmem_limit_bytes=VMEM_LIMIT),
        cost_estimate=pl.CostEstimate(flops=13 << 30, bytes_accessed=32 * MIB, transcendentals=4 * MIB),
        name="retreat",
    )(flags, gains, lam, wa, kv, cs, ckvq, z, lse, dst, *extra)
    return out[0], list(out[1:])


def input_grad_kernel(gains_ref, x_hbm, dx1_hbm, dq_hbm, one_hbm, two_hbm, wa_hbm, wb_hbm, out_hbm, sums_ref,
                      x_v, dx_v, dq_v, one_v, two_v, wkv_v, wq_v, dh_v, sem):
    rows, width = x_v.shape
    begun = start_all(
        (
            (one_hbm, one_v),
            (two_hbm, two_v),
            (wa_hbm.at[:, pl.ds(A_KV, 2 * width)], wkv_v),
            (dq_hbm, dq_v),
            (wb_hbm.at[:, pl.ds(B_Q, width)], wq_v),
            (x_hbm, x_v),
            (dx1_hbm, dx_v),
        ),
        sem,
    )
    wait_all(begun[:2])
    one_v[...] = (one_v[...].astype(F32) + two_v[...].astype(F32)).astype(BF16)
    begun[2].wait()
    dh_v[...] = dot_nt(one_v[...], wkv_v[...])
    wait_all(begun[3:5])
    dh_v[...] += dot_nt(dq_v[...], wq_v[...])
    wait_all(begun[5:])
    sums_ref[...] = jnp.zeros_like(sums_ref)

    def chunk(span):
        dx, gain_term = norm_back(x_v[span, :].astype(F32), gains_ref[0:1, :], dh_v[span, :])
        dx_v[span, :] += dx
        sums_ref[0:1, :] += jnp.sum(gain_term, axis=0, keepdims=True)

    row_chunks(rows, CHUNK, chunk)
    pltpu.sync_copy(dx_v, out_hbm)


def input_grad(gains, x, dx1, dq, one, two, wa, wb):
    rows, width = x.shape
    return pl.pallas_call(
        input_grad_kernel,
        in_specs=[VMEM] + [HBM] * 7,
        out_specs=[HBM, VMEM],
        out_shape=[shape((rows, width), F32), shape((8, width), F32)],
        scratch_shapes=[
            pltpu.VMEM((rows, width), BF16),
            pltpu.VMEM((rows, width), F32),
            pltpu.VMEM((rows, width), BF16),
            pltpu.VMEM((rows, 2 * width), BF16),
            pltpu.VMEM((rows, 2 * width), BF16),
            pltpu.VMEM((width, 2 * width), BF16),
            pltpu.VMEM((width, width), BF16),
            pltpu.VMEM((rows, width), F32),
            pltpu.SemaphoreType.DMA((7,)),
        ],
        compiler_params=pltpu.CompilerParams(vmem_limit_bytes=VMEM_LIMIT),
        cost_estimate=NO_COST,
        name="input_grad",
    )(gains, x, dx1, dq, one, two, wa, wb)


def dot_tn(a, b):
    return lax.dot_general(a, b, (((0,), (0,)), ((), ())), preferred_element_type=F32)


def early_kernel(share, fresh, flags_ref, o_hbm, da_hbm, h1_hbm, dq_hbm, h2_hbm, dup_hbm, act_hbm, g_hbm, *refs):
    outs = refs[:-11] if fresh else refs[(len(refs) - 11) // 2 : -11]
    (o_v, da_v, h1_v, dq_v, h2_v, g_v, dup_v, act_v, tile_v, sem, out_sem) = refs[-11:]
    width = h2_v.shape[1]
    tile = tile_v.shape[-1]
    cut = B_END // 2
    mine = flags_ref[2]

    @pl.when(flags_ref[0] == 1)
    def _():
        begun = start_all(
            ((act_hbm, act_v), (g_hbm, g_v), (o_hbm, o_v), (da_hbm, da_v), (h1_hbm, h1_v), (dq_hbm, dq_v),
             (h2_hbm, h2_v), (dup_hbm, dup_v)), sem)

        def outgoing(slot, base, n):
            here = pl.multiple_of(base % cut + n * tile, tile)
            if share % 32:
                there = pl.ds(pl.multiple_of(base + n * tile, tile), tile)
                pairs = [(tile_v.at[slot], outs[0].at[:, there])]
            else:
                send, keep = outs[2 * (base // cut) : 2 * (base // cut) + 2]
                pairs = [
                    (tile_v.at[slot, :, 1 - mine], send.at[:, :, pl.ds(here, tile)]),
                    (tile_v.at[slot, :, mine], keep.at[:, :, pl.ds(here, tile)]),
                ]
            return [pltpu.make_async_copy(src, dst, out_sem.at[slot, m]) for m, (src, dst) in enumerate(pairs)]

        def emit(count, base, product, done):
            def step(n, carry):
                slot = n % 2
                copies = outgoing(slot, base, n)
                value = product(n).astype(BF16)

                @pl.when(n + done >= 2)
                def _():
                    wait_all(copies)

                tile_v[slot] = value.reshape(tile_v.shape[1:])
                for copy in copies:
                    copy.start()
                return carry

            lax.fori_loop(0, count, step, 0)

        def at(n):
            return pl.ds(pl.multiple_of(n * tile, tile), tile)

        def down(n):
            slab = pl.ds(pl.multiple_of((n // 2) * width, width), width)
            return dot_tn(act_v[:, slab], g_v[:, at(n % 2)])

        first = (cut - B_UP) // tile
        wait_all(begun[:2])
        emit(8, B_DOWN, down, 0)
        wait_all(begun[2:4])
        emit(2, B_OUT, lambda n: dot_tn(o_v[...], da_v[:, at(n)]), 8)
        wait_all(begun[4:6])
        emit(2, B_Q, lambda n: dot_tn(h1_v[...], dq_v[:, at(n)]), 10)
        wait_all(begun[6:8])
        emit(first, B_UP, lambda n: dot_tn(h2_v[...], dup_v[:, at(n)]), 12)
        emit(8 - first, cut, lambda n: dot_tn(h2_v[...], dup_v[:, at(n + first)]), 12 + first)
        for slot in range(2):
            wait_all(outgoing(slot, 0, 0))


def early_grads(flags, share, before, o, da, h1, dq, h2, dup, act, g):
    rows, width = o.shape
    pairs = width // (2 * share)
    if share % 32:
        outs = [shape((width, B_END), BF16)]
        tiles = pltpu.VMEM((2, width, 512), BF16)
    else:
        outs = [shape((pairs, share, B_END // 2), BF16)] * 4
        tiles = pltpu.VMEM((2, pairs, 2, share, 512), BF16)
    narrow = pltpu.VMEM((rows, width), BF16)
    wide = pltpu.VMEM((rows, 4 * width), BF16)
    return pl.pallas_call(
        partial(early_kernel, share, not before),
        in_specs=[SMEM] + [HBM] * (8 + len(before)),
        out_specs=[HBM] * len(outs),
        out_shape=outs,
        scratch_shapes=[narrow] * 6 + [wide] * 2 + [tiles, pltpu.SemaphoreType.DMA((8,)), pltpu.SemaphoreType.DMA((2, 2))],
        input_output_aliases={9 + n: n for n in range(len(before))},
        compiler_params=pltpu.CompilerParams(vmem_limit_bytes=VMEM_LIMIT),
        cost_estimate=pl.CostEstimate(flops=11 << 30, bytes_accessed=34 * MIB, transcendentals=0),
        name="early_grads",
    )(flags, o, da, h1, dq, h2, dup, act, g, *before)


def layer_out_kernel(x1_ref, act_ref, wd_ref, out_ref, acc_ref):
    i = pl.program_id(0)
    term = dot_nn(act_ref[...], wd_ref[...])

    @pl.when(i == 0)
    def _():
        acc_ref[...] = x1_ref[...] + term

    @pl.when(i > 0)
    def _():
        acc_ref[...] += term

    @pl.when(i == pl.num_programs(0) - 1)
    def _():
        out_ref[...] = acc_ref[...].astype(BF16)


def layer_output(x1, act, wb):
    rows, width = x1.shape
    return pl.pallas_call(
        layer_out_kernel,
        grid=(4,),
        in_specs=[
            pl.BlockSpec((rows, width), lambda i: (0, 0)),
            pl.BlockSpec((rows, width), lambda i: (0, i)),
            pl.BlockSpec((width, width), lambda i: (0, B_DOWN // width + i)),
        ],
        out_specs=pl.BlockSpec((rows, width), lambda i: (0, 0)),
        out_shape=shape((rows, width), BF16),
        scratch_shapes=[pltpu.VMEM((rows, width), F32)],
        compiler_params=pltpu.CompilerParams(vmem_limit_bytes=VMEM_LIMIT),
        cost_estimate=pl.CostEstimate(flops=4 << 30, bytes_accessed=15 * MIB, transcendentals=0),
        name="layer_output",
    )(x1, act, wb)


def late_kernel(plan, share, flags_ref, *refs):
    count = len(refs) - 2
    send_ref, keep_ref = refs[count:]
    mine = flags_ref[2] == 0
    tile = 512
    for n, (kind, a, b) in enumerate(plan):
        if kind == "product":
            value = dot_tn(refs[a][...], refs[b[0]][:, columns(b[1], tile)])
        elif kind == "sum":
            total = sum(refs[m][:, columns(b[1], tile)].astype(F32) for m in b[0])
            value = dot_tn(refs[a][...], total.astype(BF16))
        else:
            value = jnp.where(flags_ref[3] == 0, refs[a][...].T.astype(F32), 0.0)
        value = value.astype(BF16)
        cols = columns(n * tile, tile)
        for m in range(value.shape[0] // (2 * share)):
            low = value[2 * share * m : 2 * share * m + share]
            high = value[2 * share * m + share : 2 * share * (m + 1)]
            rows = columns(share * m, share)
            send_ref[rows, cols] = jnp.where(mine, high, low)
            keep_ref[rows, cols] = jnp.where(mine, low, high)


def late_whole_kernel(plan, flags_ref, *refs):
    tile = 512
    for n, (kind, a, b) in enumerate(plan):
        if kind == "product":
            value = dot_tn(refs[a][...], refs[b[0]][:, columns(b[1], tile)])
        elif kind == "sum":
            total = sum(refs[m][:, columns(b[1], tile)].astype(F32) for m in b[0])
            value = dot_tn(refs[a][...], total.astype(BF16))
        else:
            value = jnp.where(flags_ref[3] == 0, refs[a][...].T.astype(F32), 0.0)
        refs[-1][:, columns(n * tile, tile)] = value.astype(BF16)


def late_grads(flags, share, plan, *arrays):
    width = arrays[0].shape[1]
    cols = 512 * len(plan)
    params = dict(
        in_specs=[SMEM] + [VMEM] * len(arrays),
        compiler_params=pltpu.CompilerParams(vmem_limit_bytes=VMEM_LIMIT),
        cost_estimate=NO_COST,
        name="late_grads",
    )
    if share % 32:
        whole = pl.pallas_call(
            partial(late_whole_kernel, plan), out_specs=VMEM, out_shape=shape((width, cols), BF16), **params
        )(flags, *arrays)
        blocks = whole.reshape(width // (2 * share), 2, share, cols)
        keep = lax.dynamic_index_in_dim(blocks, flags[2], 1, keepdims=False)
        send = lax.dynamic_index_in_dim(blocks, 1 - flags[2], 1, keepdims=False)
        return send, keep
    half = shape((width // 2, cols), BF16)
    send, keep = pl.pallas_call(
        partial(late_kernel, plan, share), out_specs=[VMEM] * 2, out_shape=[half, half], **params
    )(flags, *arrays)
    dims = (width // (2 * share), share, cols)
    return send.reshape(dims), keep.reshape(dims)


def settle_kernel(devices, in_ref, q_ref, out_ref, up_ref, down_ref):
    share = in_ref.shape[0]
    width = share * devices
    q_ref[...] = in_ref[:, columns(B_Q, width)].astype(F32)
    out_ref[...] = in_ref[:, columns(B_OUT, width)].astype(F32)
    for d in range(devices):
        pieces = [in_ref[:, columns(B_UP + s * width + d * share, share)] for s in range(4)]
        up_ref[:, columns(4 * share * d, 4 * share)] = jnp.concatenate(pieces, axis=1).astype(F32)
    for s in range(4):
        down_ref[columns(s * share, share), :] = in_ref[:, columns(B_DOWN + s * width, width)].astype(F32)


def settle(early, devices):
    share = early.shape[0]
    width = share * devices
    return pl.pallas_call(
        partial(settle_kernel, devices),
        in_specs=[VMEM],
        out_specs=[VMEM] * 4,
        out_shape=[
            shape((share, width), F32),
            shape((share, width), F32),
            shape((share, 4 * width), F32),
            shape((4 * share, width), F32),
        ],
        compiler_params=pltpu.CompilerParams(vmem_limit_bytes=VMEM_LIMIT),
        name="settle",
    )(early)


def orders_of(devices):
    bits = [1 << n for n in range(devices.bit_length() - 1)]
    if devices != 32:
        return [bits] * 2, [bits] * 2
    core, x, y, z, far = bits
    return [[core, y, z, x, far], [core, z, y, x, far]], [[core, y, x, z, far], [core, z, y, x, far]]


def exchange(value, bit, devices):
    return lax.ppermute(value, AXES, [(i, i ^ bit) for i in range(devices)])


def split_blocks(term, place, which):
    blocks, rows, cols = term.shape
    low = 1 << place
    view = term.reshape(blocks // (2 * low), 2, low, rows, cols)
    return lax.dynamic_index_in_dim(view, which, 1, keepdims=False).reshape(blocks // 2, rows, cols)


def half_kernel(count, which_ref, *refs):
    pairs, outs = refs[: 2 * count], refs[2 * count : 3 * count]
    scratch, (sem, out_sem) = refs[3 * count : 5 * count], refs[5 * count :]
    loads, stores = [], []
    for n in range(count):
        which = which_ref[n]
        loads.append(
            start_all(
                [(pairs[2 * n + m].at[:, which], scratch[2 * n + m]) for m in range(2)], sem, 2 * n
            )
        )
    for n in range(count):
        wait_all(loads[n])
        one, two = scratch[2 * n], scratch[2 * n + 1]
        high, low = one.shape[:2]

        def add(i, carry, one=one, two=two, low=low):
            one[i // low, i % low] = (
                one[i // low, i % low].astype(F32) + two[i // low, i % low].astype(F32)
            ).astype(BF16)
            return carry

        lax.fori_loop(0, high * low, add, 0)
        stores += start_all([(one, outs[n])], out_sem, n)
    wait_all(stores)


def half_sums(terms, places, which):
    share = terms[0][0].shape[1]
    if share % 32:
        return [
            sum(split_blocks(t, place, w).astype(F32) for t in pair).astype(BF16)
            for pair, place, w in zip(terms, places, which)
        ]
    args, outs, scratch = [], [], []
    for pair, place in zip(terms, places):
        blocks, rows, cols = pair[0].shape
        low = 1 << place
        high = blocks // (2 * low)
        args += [t.reshape(high, 2, low, rows, cols) for t in pair]
        outs.append(shape((high, low, rows, cols), BF16))
        scratch += [pltpu.VMEM((high, low, rows, cols), BF16)] * 2
    count = len(terms)
    results = pl.pallas_call(
        partial(half_kernel, count),
        in_specs=[SMEM] + [HBM] * (2 * count),
        out_specs=[HBM] * count,
        out_shape=outs,
        scratch_shapes=scratch + [pltpu.SemaphoreType.DMA((2 * count,)), pltpu.SemaphoreType.DMA((count,))],
        compiler_params=pltpu.CompilerParams(vmem_limit_bytes=VMEM_LIMIT),
        cost_estimate=NO_COST,
        name="half_sums",
    )(jnp.stack(which), *args)
    return [r.reshape(-1, *r.shape[2:]) for r in results]


class Stream:
    def __init__(self, send, keep, order, devices):
        self.devices, self.order, self.left = devices, list(order), sorted(order)
        self.keep, self.send, self.got = keep, send, None
        self.bit = self.order.pop(0)
        self.left.remove(self.bit)

    def move(self):
        self.got = exchange(self.send, self.bit, self.devices)
        self.send = None

    def result(self):
        return (self.keep.astype(F32) + self.got.astype(F32))[0]


class Few:
    def __init__(self, value, order, devices):
        self.devices, self.order, self.left, self.total = devices, list(order), sorted(order), value.astype(F32)
        self.pick()

    def pick(self):
        me = lax.axis_index(AXES)
        bits, self.order = self.order[:2], self.order[2:]
        masks = [0]
        for bit in bits:
            masks += [mask | bit for mask in masks]
        parts = []
        for mask in masks:
            value, left = self.total, list(self.left)
            for bit in bits:
                value = split_blocks(value, left.index(bit), ((me ^ mask) // bit) % 2)
                left.remove(bit)
            parts.append(value)
        self.left = [bit for bit in self.left if bit not in bits]
        self.keep, self.send, self.masks = parts[0], [part.astype(BF16) for part in parts[1:]], masks[1:]

    def move(self):
        self.got = [exchange(send, mask, self.devices) for send, mask in zip(self.send, self.masks)]
        self.send = None

    def split(self):
        self.total = self.keep + sum(got.astype(F32) for got in self.got)
        self.pick()

    def result(self):
        return (self.keep + sum(got.astype(F32) for got in self.got))[0]


class Step:
    def __init__(self, streams):
        self.streams, self.terms, self.places, self.mine = streams, [], [], []
        for stream in streams:
            stream.bit = stream.order.pop(0)
            self.places.append(stream.left.index(stream.bit))
            stream.left.remove(stream.bit)
            self.mine.append((lax.axis_index(AXES) // stream.bit) % 2)
            self.terms.append((stream.keep, stream.got))
        sends = half_sums(self.terms, self.places, [1 - m for m in self.mine])
        for stream, send in zip(streams, sends):
            stream.send = send

    def keep(self, after):
        after, self.terms = lax.optimization_barrier((after, self.terms))
        keeps = half_sums(self.terms, self.places, self.mine)
        for stream, keep in zip(self.streams, keeps):
            stream.keep = keep
        return after


def split(streams):
    step = Step(streams)
    sends = step.keep([stream.send for stream in streams])
    for stream, send in zip(streams, sends):
        stream.send = send


def body(
    layer_input,
    segment_length,
    output_gradient,
    state_cotangent,
    query_key_value_weight,
    state_key_value_weight,
    state_query_weight,
    output_weight,
    merge_weight,
    up_weight,
    down_weight,
    initial_state_learned,
    attention_norm_gain,
    feedforward_norm_gain,
    state_norm_gain,
    state_gate_logits,
    relative_position_bias,
):
    _, rows, width = layer_input.shape
    place = lax.axis_index("seq")
    count = lax.axis_size("seq")
    devices = count * lax.axis_size("dp")
    share = width // devices
    pairs = lax.axis_size("dp")

    bias_local = relative_position_bias.shape[0]
    small = jnp.stack(
        [
            attention_norm_gain,
            feedforward_norm_gain,
            state_norm_gain,
            state_gate_logits,
            jnp.pad(relative_position_bias, (0, share - bias_local)),
        ],
        axis=1,
    )
    small = jnp.pad(small, ((0, 0), (0, A_END - A_VEC - 5)))
    wa = jnp.concatenate(
        [
            query_key_value_weight[:, width:],
            state_key_value_weight,
            state_query_weight,
            merge_weight,
            initial_state_learned.T,
            small,
        ],
        axis=1,
    )
    up_local = up_weight.reshape(share, devices, 4, share).transpose(0, 2, 1, 3)
    down_local = down_weight.reshape(4, share, width).transpose(1, 0, 2)
    wb = jnp.concatenate(
        [
            query_key_value_weight[:, :width],
            output_weight,
            up_local.reshape(share, 4 * width),
            down_local.reshape(share, 4 * width),
        ],
        axis=1,
    )
    wa = lax.all_gather(wa, AXES, axis=0, tiled=True)
    wb = lax.all_gather(wb, AXES, axis=0, tiled=True)

    vectors = wa[:, A_VEC : A_VEC + 5].astype(F32).T
    gate = jax.nn.sigmoid(vectors[3:4])
    gains = jnp.concatenate([vectors[:3], gate, jnp.zeros((4, width), F32)], axis=0)
    table = vectors[4].reshape(devices, share)[:, :bias_local].reshape(HEADS, BUCKETS)
    onehot = np.eye(BUCKETS, dtype=np.float32)[:, bucket_of(rows)]
    t = jnp.dot(table * LOG2E, jnp.asarray(onehot), precision=lax.Precision.HIGHEST)

    x = layer_input.reshape(rows, width)
    g = output_gradient.reshape(rows, width)
    nvalid = jnp.clip(segment_length[0] - place * rows, 0, rows).astype(jnp.int32)

    def flags(section):
        core = lax.axis_index(AXES) % 2
        parts = [(place == section).astype(jnp.int32), nvalid, core, place]
        return jnp.stack([part.astype(jnp.int32) for part in parts])

    def hop(value, frm, to):
        route = [(d * count + frm, d * count + to) for d in range(pairs)]
        return lax.ppermute(value, AXES, route)

    kv, h1, new, *stash = advance(flags(0), gains, x, wa, None, None)
    for section in range(1, count):
        carry = hop(new, section - 1, section)
        new, *stash = advance(flags(section), gains, carry, wa, kv, stash)
    cs, hc, ckvq, upd, z, lse_two = stash

    quarter = new.shape[0] // count
    state_out = lax.dynamic_slice_in_dim(new, place * quarter, quarter, 0)
    for to in range(count - 1):
        got = hop(new[to * quarter : (to + 1) * quarter], count - 1, to)
        state_out = jnp.where(place == to, got, state_out)
    wb, state_out = lax.optimization_barrier((wb, state_out))
    state_out = state_out.astype(F32)[None]

    o, x1, h2, act, dup, dx1, da, dq, dkv, dst, dbias, sums_mlp = block_part(
        flags(0), t, gains, x, g, h1, kv, ckvq, wb
    )

    early_args = (o, da, h1, dq, h2, dup, act, g)

    def only(active):
        parts = [active, nvalid, lax.axis_index(AXES) % 2]
        return jnp.stack([part.astype(jnp.int32) for part in parts])

    halves = early_grads(only(place < count - 1), share, (), *early_args)

    tie = lax.optimization_barrier
    early_orders, late_orders = orders_of(devices)
    back = None
    lam = state_cotangent.reshape(state_cotangent.shape[1:])
    lam, halves = tie((lam, halves))
    for section in reversed(range(count)):
        prev, back = retreat(flags(section), gains, lam, wa, kv, cs, ckvq, z, lse_two, dst, back, section > 0)
        if section == 0:
            break
        if section == count - 1:
            prev, halves = tie((prev, halves))
            lam = hop(prev, section, section - 1)
            halves = early_grads(only(place == count - 1), share, tuple(halves), *early_args)
            lam, halves = tie((lam, halves))
            if share % 32:
                whole = halves[0].reshape(devices, share, B_END)
                mine = lax.axis_index(AXES) % 2
                halves = [split_blocks(whole, 0, 1 - mine), split_blocks(whole, 0, mine)]
                cut = B_END // 2
                halves = [half[:, :, c : c + cut] for c in (0, cut) for half in halves]
        elif section == count - 2:
            prev, halves, x1 = tie((prev, halves, x1))
            early = [Stream(*halves[2 * n : 2 * n + 2], early_orders[n], devices) for n in range(2)]
            lam = hop(prev, section, section - 1)
            for stream in early:
                stream.move()
            layer_out = layer_output(x1, act, wb)
            layer_out, gots = tie((layer_out, [stream.got for stream in early]))
            for stream, got in zip(early, gots):
                stream.got = got
            step = Step(early)
            lam, sends = tie((lam, [stream.send for stream in early]))
            for stream, send in zip(early, sends):
                stream.send = send
                stream.move()
        else:
            prev = step.keep(prev)
            lam = hop(prev, section, section - 1)
            lam, keeps = tie((lam, [stream.keep for stream in early]))
            for stream, keep in zip(early, keeps):
                stream.keep = keep
    dz, dcs, dkv_two, sums_state = back

    tiles = [512 * n for n in range(4)]
    late_one = [("product", 0, (1, 512 * n)) for n in range(6)] + [("flip", 2, None)]
    late_two = [("sum", 0, ((1, 2), c)) for c in tiles] + [("product", 3, (4, c)) for c in tiles[:2]]
    def arrived(streams, others):
        gots, keeps, others = tie(([s.got for s in streams], [s.keep for s in streams], others))
        for stream, got, keep in zip(streams, gots, keeps):
            stream.got, stream.keep = got, keep
        return others

    def together(streams, other=None):
        sends = tie([stream.send for stream in streams])
        for stream, send in zip(streams, sends):
            stream.send = send
        result = other(jnp.minimum(jnp.abs(sends[0][0, 0, 0].astype(F32)), 0.0)) if other else ()
        for stream in streams:
            stream.move()
        return arrived(streams, result)

    prev, gots = tie((prev, [stream.got for stream in early]))
    for stream, got in zip(early, gots):
        stream.got = got
    split(early)
    switches = flags(0)
    switches, sends = tie((switches, [stream.send for stream in early]))
    for stream, send in zip(early, sends):
        stream.send = send
        stream.move()
    late = [
        late_grads(switches, share, late_one, hc, dcs, prev),
        late_grads(switches, share, late_two, h1, dkv, dkv_two, upd, dz),
    ]
    late = [Stream(*halves, order, devices) for halves, order in zip(arrived(early, late), late_orders)]
    for stream in late:
        stream.move()
    split(early)
    gots, sends, keeps = tie(
        ([s.got for s in late], [s.send for s in early], [s.keep for s in early])
    )
    for stream, got in zip(late, gots):
        stream.got = got
    for stream, send, keep in zip(early, sends, keeps):
        stream.send, stream.keep = send, keep
    split(late)
    x_grad, sums_attn = together(
        late + early, lambda zero: input_grad(gains + zero, x, dx1, dq, dkv, dkv_two, wa, wb)
    )

    buckets = jnp.asarray(np.ascontiguousarray(onehot.T))
    dtable = jnp.dot(dbias, buckets, precision=lax.Precision.HIGHEST).reshape(devices, bias_local)
    dtable = jnp.pad(dtable, ((0, 0), (0, share - bias_local))).reshape(width)
    gate_grad = sums_state[1] * gate[0] * (1.0 - gate[0])
    vectors = jnp.stack([sums_attn[0], sums_mlp[0], sums_state[0], gate_grad, dtable], axis=1)
    vectors = jnp.pad(vectors, ((0, 0), (0, 123))).reshape(devices, share, 128)
    small = Few(vectors, sorted(late_orders[0]), devices)
    while late[0].order or small.order or small.send:
        running = [stream for stream in late + early if stream.order]
        if running:
            split(running)
        if small.send is None and small.order:
            small.split()
        together(running + ([small] if small.send else []))
    early = jnp.concatenate([stream.result() for stream in early], axis=1)
    one, two = [stream.result() for stream in late]
    vec = small.result()

    q_shard, out_shard, up_shard, down_shard = settle(early, devices)
    return (
        layer_out[None],
        state_out,
        x_grad[None],
        jnp.concatenate([q_shard, two[:, : 2 * width]], axis=1),
        one[:, : 2 * width],
        one[:, 2 * width : 3 * width],
        out_shard,
        two[:, 2 * width :],
        up_shard,
        down_shard,
        one[:, 3 * width :].T,
        vec[:, 0],
        vec[:, 1],
        vec[:, 2],
        vec[:, 3],
        vec[:bias_local, 4],
    )


def solution(mesh):
    return jax.shard_map(
        body,
        mesh=mesh,
        in_specs=(
            P("dp", "seq", None),
            P("dp"),
            P("dp", "seq", None),
            P("dp", None, None),
            P(AXES, None),
            P(AXES, None),
            P(AXES, None),
            P(AXES, None),
            P(AXES, None),
            P(AXES, None),
            P(AXES, None),
            P(None, AXES),
            P(AXES),
            P(AXES),
            P(AXES),
            P(AXES),
            P(AXES),
        ),
        out_specs=(
            P("dp", "seq", None),
            P("dp", "seq", None),
            P("dp", "seq", None),
            P(AXES, None),
            P(AXES, None),
            P(AXES, None),
            P(AXES, None),
            P(AXES, None),
            P(AXES, None),
            P(AXES, None),
            P(None, AXES),
            P(AXES),
            P(AXES),
            P(AXES),
            P(AXES),
            P(AXES),
        ),
        check_vma=False,
    )
```

time: 780 us -> 646 us (0.83)
  waiting for transfers between devices: 413 us -> 289 us
  local copies, waits for them, and re-layouts: 106 us -> 32.7 us
  Pallas kernels: 173 us -> 228 us
  starting transfers between devices: 22.8 us -> 55.3 us
  other arithmetic: 34.9 us -> 17.5 us
    ppermute x15 -> x27, waiting for transfers between devices: 118 us -> 53.9 us  [exchange(): return lax.ppermute(value, AXES, [(i, i ^ bit) for i in range(devices)])]
    unnamed x157 -> x75, local copies, waits for them, and re-layouts: 74 us -> 17.7 us
    pallas_call x19 -> x30, Pallas kernels: 173 us -> 228 us  [the longest x14 60.4 us: half_sums(): pl.pallas_call(partial(half_kernel, count), in_specs=[SMEM] + [HBM] * (2...]
    ppermute x15 -> x27, starting transfers between devices: 13 us -> 44.7 us  [exchange(): return lax.ppermute(value, AXES, [(i, i ^ bit) for i in range(devices)])]
    all_gather x1, waiting for transfers between devices: 46.3 us -> 20 us  [body(): wb = lax.all_gather(wb, AXES, axis=0, tiled=True)]
    ppermute x9, waiting for transfers between devices: 140 us -> 116 us  [hop(): return lax.ppermute(value, AXES, route)]
    convert_element_type x13 -> x0, other arithmetic: 14.2 us -> none  [the longest x12 11.6 us: scatter_sum(): value = value.astype(BF16)]
    concatenate x4 -> x3, other arithmetic: 14.8 us -> 2.82 us  [the longest x1 1.15 us: body(): early = jnp.concatenate([stream.result() for stream in early], axis=1)]
  transfers between devices with their start and end apart: 27 -> 38, of which waited for: 15 -> 16; matrix products, arithmetic and copies ran while one was open for 7% -> 4% of each run, Pallas kernels for 14% -> 22%
where the time goes in v2:
time: 646 us; the launch traced here: 640 us
  waiting for transfers between devices  289 us (45%)
  Pallas kernels  228 us (35%)
  starting transfers between devices  55.3 us (9%)
  local copies, waits for them, and re-layouts  32.7 us (5%)
  other arithmetic  17.5 us (3%)
  between operations  16.6 us (3%)
    ppermute x9, waiting for transfers between devices, hop(): return lax.ppermute(value, AXES, route)  116 us
    all_gather x1, waiting for transfers between devices, body(): wa = lax.all_gather(wa, AXES, axis=0, tiled=True)  98.9 us
    pallas_call x14, Pallas kernels, half_sums(): pl.pallas_call(partial(half_kernel, count), in_specs=[SMEM] + [HBM] * (2...  60.4 us
    ppermute x27, waiting for transfers between devices, exchange(): return lax.ppermute(value, AXES, [(i, i ^ bit) for i in range(devices)])  53.9 us
    pallas_call x1, Pallas kernels, block_part(): pl.pallas_call(block_kernel, in_specs=[SMEM, VMEM, VMEM] + [HBM] * 6, out...  46.2 us
    ppermute x27, starting transfers between devices, exchange(): return lax.ppermute(value, AXES, [(i, i ^ bit) for i in range(devices)])  44.7 us
    pallas_call x4, Pallas kernels, advance(): pl.pallas_call(kernel, in_specs=[SMEM, VMEM] + [HBM] * (len(args) - 2), o...  28.1 us
    pallas_call x4, Pallas kernels, retreat(): pl.pallas_call(partial(retreat_kernel, first, looped), in_specs=[SMEM, VM...  28.1 us
  transfers between devices with their start and end apart: 38, of which 16 were waited for; matrix products, arithmetic and copies ran while one was open for 4% of the time, Pallas kernels for 22%

profile of v2, /device:TPU:0, one launch (start us, length us, event | category | flops | bytes accessed | tf_op | source)
XLA Modules:
  0.0 640.3 jit_solution(16806825827493246647)
XLA Ops:
  19.6 98.9 %all-gather.3.cloned.1.call-done.w.wa_hbm = bf16[1024,6784]{1,0:T(8,128)(2,1)} async-done(((bf16[32,6784]{1,0:T(8,128)(2,1)}), bf16[1024,6784]{1,0:T(8,128)(2,1)}) %all-gather.3.cloned.1.call-update) | async-done | bytes 13893648 | tf_op jit(solution)/shard_map/all_gather | solution.py:1151
  121.1 19.1 %advance.4 = (bf16[512,2048]{1,0:T(8,128)(2,1)}, bf16[512,1024]{1,0:T(8,128)(2,1)}, bf16[512,1024]{1,0:T(8,128)(2,1)}, bf16[512,1024]{1,0:T(8,128)(2,1)}, bf16[5...) custom-call(s32[4]{0:T(128)} %add_add_fusion.5.f.flags_ref, ...), custom_call_target="tpu_custom_call" | custom-call | flops 9663676416 | bytes 25165824 | tf_op jit(solution)/shard_map/advance/pallas_call | solution.py:270
  166.4 71.5 %collective-permute-done.5 = bf16[128,1024]{1,0:T(8,128)(2,1)S(1)} collective-permute-done((bf16[128,1024]{1,0:T(8,128)(2,1)S(1)}, bf16[128,1024]{1,0:T(8,128)(2,1)S(1)}, u32[]{:S(2)}, u32[]{:S(2)}) %collective-permute-start.5) | collective-permute-done | bytes 262176 | tf_op jit(solution)/shard_map/ppermute | solution.py:1172
  239.7 20.0 %all-gather.5.cloned.1.call-done.wb_hbm.wd_ref = bf16[1024,10240]{1,0:T(8,128)(2,1)} async-done(((bf16[32,10240]{1,0:T(8,128)(2,1)}), bf16[1024,10240]{1,0:T(8,128)(2,1)}) %all-gather.5.cloned.1.call-update) | async-done | bytes 20971536 | tf_op jit(solution)/shard_map/all_gather | solution.py:1152
  259.8 46.2 %block_part.1 = (bf16[512,1024]{1,0:T(8,128)(2,1)}, f32[512,1024]{1,0:T(8,128)}, bf16[512,1024]{1,0:T(8,128)(2,1)}, bf16[512,4096]{1,0:T(8,128)(2,1)}, bf16[512,...) custom-call(s32[4]{0:T(128)} %add_add_fusion.5.f.flags_ref, ...), custom_call_target="tpu_custom_call" | custom-call | flops 26843545600 | bytes 41943040 | tf_op jit(solution)/shard_map/block_part/pallas_call | solution.py:476
  306.0 21.4 %early_grads.2 = (bf16[16,32,5120]{2,1,0:T(8,128)(2,1)}, bf16[16,32,5120]{2,1,0:T(8,128)(2,1)}, bf16[16,32,5120]{2,1,0:T(8,128)(2,1)}, bf16[16,32,5120]{2,1,0:T(8,128)(2,1)}) custom-call(s32[3]{0:T(128)} %get-tuple-element.565.flags_ref, bf16[512,1024]{1,0:T(8,128)(2,1)} %get-tuple-element.308.o_hbm, bf16[512,1024]{1,0:T(8,128)(2,1)} %get-tuple-element.309.da_hbm, ...), custom_call_target="tpu_custom_call" | custom-call | flops 11811160064 | bytes 35651584 | tf_op jit(solution)/shard_map/early_grads/pallas_call | solution.py:800
  334.2 10.1 %layer_output.1 = bf16[512,1024]{1,0:T(8,128)(2,1)} custom-call(f32[512,1024]{1,0:T(8,128)} %get-tuple-element.348.x1_ref, bf16[512,4096]{1,0:T(8,128)(2,1)} %get-tuple-element.313.act_hbm.act_ref, bf16[1024,10240]{1,0:T(8,128)(2,1)} %all-gather.5.cloned.1.call-done.wb_hbm.wd_ref), custom_call_target="tpu_custom_call" | custom-call | flops 4294967296 | bytes 15728640 | tf_op jit(solution)/shard_map/layer_output/pallas_call | solution.py:832
  348.7 6.9 %half_sums.14 = (bf16[4,2,32,5120]{3,2,1,0:T(8,128)(2,1)}, bf16[2,4,32,5120]{3,2,1,0:T(8,128)(2,1)}) custom-call(s32[2]{0:T(128)} %get-tuple-element.567.which_ref, bf16[4,2,2,32,5120]{4,3,2,1,0:T(8,128)(2,1)} %bitcast.232, bf16[4,2,2,32,5120]{4,3,2,1,0:T(8,128)(2,1)} %bitcast.27.refs_1_, bf16[2,2,4,32,5120]{4,3,2,1,0:T(8,128)(2,1)} %bitcast.234, ...), custom_call_target="tpu_custom_call" | custom-call | tf_op jit(solution)/shard_map/half_sums/pallas_call | solution.py:1002
  360.4 6.9 %half_sums.15 = (bf16[4,2,32,5120]{3,2,1,0:T(8,128)(2,1)}, bf16[2,4,32,5120]{3,2,1,0:T(8,128)(2,1)}) custom-call(s32[2]{0:T(128)} %get-tuple-element.569.which_ref, bf16[4,2,2,32,5120]{4,3,2,1,0:T(8,128)(2,1)} %bitcast.233, bf16[4,2,2,32,5120]{4,3,2,1,0:T(8,128)(2,1)} %bitcast.35.refs_1_, bf16[2,2,4,32,5120]{4,3,2,1,0:T(8,128)(2,1)} %bitcast.235, ...), custom_call_target="tpu_custom_call" | custom-call | tf_op jit(solution)/shard_map/half_sums/pallas_call | solution.py:1002
  367.3 43.0 %collective-permute-done.10.lam_hbm = bf16[512,1024]{1,0:T(8,128)(2,1)S(1)} collective-permute-done((bf16[512,1024]{1,0:T(8,128)(2,1)}, bf16[512,1024]{1,0:T(8,128)(2,1)S(1)}, u32[]{:S(2)}, u32[]{:S(2)}) %collective-permute-start.10) | collective-permute-done | bytes 1048608 | tf_op jit(solution)/shard_map/ppermute | solution.py:1172
  411.3 25.2 %retreat.7 = (bf16[512,1024]{1,0:T(8,128)(2,1)}, bf16[512,1024]{1,0:T(8,128)(2,1)}, bf16[512,3072]{1,0:T(8,128)(2,1)}, bf16[512,2048]{1,0:T(8,128)(2,1)}, f32[8,1024]{1,0:T(8,128)}) custom-call(s32[4]{0:T(128)} %add_add_fusion.5.f.flags_ref, ...), custom_call_target="tpu_custom_call", output_to_operand_aliasing={{1}: (10, {}), {2}: (11, {}), {3}: (12, {}), {4}: (13, {})} | custom-call | flops 13958643712 | bytes 33554432 | tf_op jit(solution)/shard_map/retreat/pallas_call | solution.py:625
  438.0 4.6 half_sums.16
  445.2 9.0 %late_grads.2 = (bf16[512,3584]{1,0:T(8,128)(2,1)}, bf16[512,3584]{1,0:T(8,128)(2,1)}) custom-call(s32[4]{0:T(128)} %add_add_fusion.5.f.flags_ref, bf16[512,1024]{1,0:T(8,128)(2,1)} %get-tuple-element.398.refs_0_, bf16[512,3072]{1,0:T(8,128)(2,1)} %get-tuple-element.399.refs_1_, bf16[512,1024]{1,0:T(8,128)(2,1)} %get-tuple-element.400.refs_2_), custom_call_target="tpu_custom_call" | custom-call | tf_op jit(solution)/shard_map/late_grads/pallas_call | solution.py:903
  454.3 9.2 %late_grads.3 = (bf16[512,3072]{1,0:T(8,128)(2,1)}, bf16[512,3072]{1,0:T(8,128)(2,1)}) custom-call(s32[4]{0:T(128)} %add_add_fusion.5.f.flags_ref, bf16[512,1024]{1,0:T(8,128)(2,1)} %get-tuple-element.282.h1_hbm.refs_0_, bf16[512,2048]{1,0:T(8,128)(2,1)} %get-tuple-element.403.refs_1_.one_hbm, bf16[512,2048]{1,0:T(8,128)(2,1)} %get-tuple-element.404.refs_2_.two_hbm, ...), custom_call_target="tpu_custom_call" | custom-call | tf_op jit(solution)/shard_map/late_grads/pallas_call | solution.py:903
  482.0 5.5 half_sums.20
  490.8 15.6 %collective-permute-start.19 = (bf16[2,32,5120]{2,1,0:T(8,128)(2,1)}, bf16[2,32,5120]{2,1,0:T(8,128)(2,1)S(1)}, u32[]{:S(2)}, u32[]{:S(2)}) collective-permute-start(bf16[2,32,5120]{2,1,0:T(8,128)(2,1)} %bitcast.329), channel_id=1, source_target_pairs={{0,2},{1,3},{2,0},{3,1},{4,6},{5,7},{6,4},{7,5},{8,10},{9,11},{10,... | collective-permute-start | bytes 1966088 | tf_op jit(solution)/shard_map/ppermute | solution.py:949
  509.7 5.6 half_sums.21
  516.1 11.4 %input_grad.1 = (f32[512,1024]{1,0:T(8,128)}, f32[8,1024]{1,0:T(8,128)}) custom-call(f32[8,1024]{1,0:T(8,128)} %broadcast_add_fusion.gains_ref, bf16[512,1024]{1,0:T(8,128)(2,1)} %bitcast.291, f32[512,1024]{1,0:T(8,128)} %get-tuple-element.447.dx1_hbm, bf16[512,1024]{1,0:T(8,128)(2,1)} %get-tuple-element.310.dq_hbm, ...), custom_call_target="tpu_custom_call" | custom-call | tf_op jit(solution)/shard_map/input_grad/pallas_call | solution.py:698
  527.6 7.9 %collective-permute-done.20 = bf16[2,32,5120]{2,1,0:T(8,128)(2,1)} collective-permute-done((bf16[2,32,5120]{2,1,0:T(8,128)(2,1)}, bf16[2,32,5120]{2,1,0:T(8,128)(2,1)}, u32[]{:S(2)}, u32[]{:S(2)}) %collective-permute-start.20) | collective-permute-done | bytes 655392 | tf_op jit(solution)/shard_map/ppermute | solution.py:949
  542.0 9.8 %collective-permute-start.21 = (bf16[4,32,3584]{2,1,0:T(8,128)(2,1)}, bf16[4,32,3584]{2,1,0:T(8,128)(2,1)S(1)}, u32[]{:S(2)}, u32[]{:S(2)}) collective-permute-start(bf16[4,32,3584]{2,1,0:T(8,128)(2,1)} %bitcast.97), channel_id=1, source_target_pairs={{0,2},{1,3},{2,0},{3,1},{4,6},{5,7},{6,4},{7,5},{8,10},{9,11},{10,... | collective-permute-start | bytes 2752520 | tf_op jit(solution)/shard_map/ppermute | solution.py:949
  561.5 11.9 %collective-permute-done.26 = bf16[8,32,128]{2,1,0:T(8,128)(2,1)S(1)} collective-permute-done((bf16[8,32,128]{2,1,0:T(8,128)(2,1)S(1)}, bf16[8,32,128]{2,1,0:T(8,128)(2,1)S(1)}, u32[]{:S(2)}, u32[]{:S(2)}) %collective-permute-start.26) | collective-permute-done | bytes 65568 | tf_op jit(solution)/shard_map/ppermute | solution.py:949
  578.2 6.1 collective-permute-done.24
  595.9 5.3 collective-permute-done.31
  617.2 9.1 %collective-permute-done.35 = bf16[1,32,128]{2,1,0:T(8,128)(2,1)S(1)} collective-permute-done((bf16[1,32,128]{2,1,0:T(8,128)(2,1)S(1)}, bf16[1,32,128]{2,1,0:T(8,128)(2,1)S(1)}, u32[]{:S(2)}, u32[]{:S(2)}) %collective-permute-start.35) | collective-permute-done | bytes 8224 | tf_op jit(solution)/shard_map/ppermute | solution.py:949
  (238 shorter events, 143.3 us)
Async XLA Ops:
  7.2 111.3 %all-gather.3.cloned.1.call-start = ((), (), s32[]{:S(2)}) async-start(), calls=%async_computation | async-start | bytes 14327808 | tf_op jit(solution)/shard_map/all_gather | solution.py:1151
  13.9 245.9 %all-gather.5.cloned.1.call-start = ((), (), s32[]{:S(2)}) async-start(), calls=%async_computation.1 | async-start | bytes 21626880 | tf_op jit(solution)/shard_map/all_gather | solution.py:1152
  161.9 76.0 %collective-permute-start.5 = (bf16[128,1024]{1,0:T(8,128)(2,1)S(1)}, bf16[128,1024]{1,0:T(8,128)(2,1)S(1)}, u32[]{:S(2)}, u32[]{:S(2)}) collective-permute-start(bf16[128,1024]{1,0:T(8,128)(2,1)S(1)} %get-tuple-element.552), channel_id=1, source_target_pairs={{3,0},{7,4},{11,8},{15,12},{19,16},{23,20},{27,24},{31,28}} | collective-permute-start | bytes 786440 | tf_op jit(solution)/shard_map/ppermute | solution.py:1172
  332.5 16.3 %collective-permute-start.8 = (bf16[16,32,5120]{2,1,0:T(8,128)(2,1)}, bf16[16,32,5120]{2,1,0:T(8,128)(2,1)}, u32[]{:S(2)}, u32[]{:S(2)}) collective-permute-start(bf16[16,32,5120]{2,1,0:T(8,128)(2,1)} %get-tuple-element.350), channel_id=1, source_target_pairs={{0,1},{1,0},{2,3},{3,2},{4,5},{5,4},{6,7},{7,6},{8,9},{9,8},{10,11... | collective-permute-start | bytes 15728648 | tf_op jit(solution)/shard_map/ppermute | solution.py:949
  332.8 22.9 %collective-permute-start.9 = (bf16[512,1024]{1,0:T(8,128)(2,1)}, bf16[512,1024]{1,0:T(8,128)(2,1)S(1)}, u32[]{:S(2)}, u32[]{:S(2)}) collective-permute-start(bf16[512,1024]{1,0:T(8,128)(2,1)} %get-tuple-element.353), channel_id=1, source_target_pairs={{2,1},{6,5},{10,9},{14,13},{18,17},{22,21},{26,25},{30,29}} | collective-permute-start | bytes 3145736 | tf_op jit(solution)/shard_map/ppermute | solution.py:1172
  355.7 80.8 %collective-permute-start.11 = (bf16[8,32,5120]{2,1,0:T(8,128)(2,1)}, bf16[8,32,5120]{2,1,0:T(8,128)(2,1)S(1)}, u32[]{:S(2)}, u32[]{:S(2)}) collective-permute-start(bf16[8,32,5120]{2,1,0:T(8,128)(2,1)} %bitcast.317), channel_id=1, source_target_pairs={{0,4},{1,5},{2,6},{3,7},{4,0},{5,1},{6,2},{7,3},{8,12},{9,13},{10,... | collective-permute-start | bytes 7864328 | tf_op jit(solution)/shard_map/ppermute | solution.py:949
  357.2 79.4 %collective-permute-start.12 = (bf16[8,32,5120]{2,1,0:T(8,128)(2,1)}, bf16[8,32,5120]{2,1,0:T(8,128)(2,1)}, u32[]{:S(2)}, u32[]{:S(2)}) collective-permute-start(bf16[8,32,5120]{2,1,0:T(8,128)(2,1)} %bitcast.316), channel_id=1, source_target_pairs={{0,8},{1,9},{2,10},{3,11},{4,12},{5,13},{6,14},{7,15},{8,0},{9,1},... | collective-permute-start | bytes 7864328 | tf_op jit(solution)/shard_map/ppermute | solution.py:949
  358.5 51.8 %collective-permute-start.10 = (bf16[512,1024]{1,0:T(8,128)(2,1)}, bf16[512,1024]{1,0:T(8,128)(2,1)S(1)}, u32[]{:S(2)}, u32[]{:S(2)}) collective-permute-start(bf16[512,1024]{1,0:T(8,128)(2,1)} %get-tuple-element.366), channel_id=1, source_target_pairs={{1,0},{5,4},{9,8},{13,12},{17,16},{21,20},{25,24},{29,28}} | collective-permute-start | bytes 3145736 | tf_op jit(solution)/shard_map/ppermute | solution.py:1172
  442.6 25.4 %collective-permute-start.13 = (bf16[4,32,5120]{2,1,0:T(8,128)(2,1)}, bf16[4,32,5120]{2,1,0:T(8,128)(2,1)S(1)}, u32[]{:S(2)}, u32[]{:S(2)}) collective-permute-start(bf16[4,32,5120]{2,1,0:T(8,128)(2,1)} %bitcast.324), channel_id=1, source_target_pairs={{0,8},{1,9},{2,10},{3,11},{4,12},{5,13},{6,14},{7,15},{8,0},{9,1},... | collective-permute-start | bytes 3932168 | tf_op jit(solution)/shard_map/ppermute | solution.py:949
  443.8 24.3 %collective-permute-start.14 = (bf16[4,32,5120]{2,1,0:T(8,128)(2,1)}, bf16[4,32,5120]{2,1,0:T(8,128)(2,1)S(1)}, u32[]{:S(2)}, u32[]{:S(2)}) collective-permute-start(bf16[4,32,5120]{2,1,0:T(8,128)(2,1)} %bitcast.323), channel_id=1, source_target_pairs={{0,4},{1,5},{2,6},{3,7},{4,0},{5,1},{6,2},{7,3},{8,12},{9,13},{10,... | collective-permute-start | bytes 3932168 | tf_op jit(solution)/shard_map/ppermute | solution.py:949
  487.4 48.0 %collective-permute-start.17 = (bf16[8,32,3584]{2,1,0:T(8,128)(2,1)}, bf16[8,32,3584]{2,1,0:T(8,128)(2,1)S(1)}, u32[]{:S(2)}, u32[]{:S(2)}) collective-permute-start(bf16[8,32,3584]{2,1,0:T(8,128)(2,1)} %bitcast.320), channel_id=1, source_target_pairs={{0,4},{1,5},{2,6},{3,7},{4,0},{5,1},{6,2},{7,3},{8,12},{9,13},{10,... | collective-permute-start | bytes 5505032 | tf_op jit(solution)/shard_map/ppermute | solution.py:949
  488.1 47.3 %collective-permute-start.18 = (bf16[8,32,3072]{2,1,0:T(8,128)(2,1)}, bf16[8,32,3072]{2,1,0:T(8,128)(2,1)}, u32[]{:S(2)}, u32[]{:S(2)}) collective-permute-start(bf16[8,32,3072]{2,1,0:T(8,128)(2,1)} %bitcast.322), channel_id=1, source_target_pairs={{0,8},{1,9},{2,10},{3,11},{4,12},{5,13},{6,14},{7,15},{8,0},{9,1},... | collective-permute-start | bytes 4718600 | tf_op jit(solution)/shard_map/ppermute | solution.py:949
  490.8 36.7 %collective-permute-start.19 = (bf16[2,32,5120]{2,1,0:T(8,128)(2,1)}, bf16[2,32,5120]{2,1,0:T(8,128)(2,1)S(1)}, u32[]{:S(2)}, u32[]{:S(2)}) collective-permute-start(bf16[2,32,5120]{2,1,0:T(8,128)(2,1)} %bitcast.329), channel_id=1, source_target_pairs={{0,2},{1,3},{2,0},{3,1},{4,6},{5,7},{6,4},{7,5},{8,10},{9,11},{10,... | collective-permute-start | bytes 1966088 | tf_op jit(solution)/shard_map/ppermute | solution.py:949
  506.4 29.1 %collective-permute-start.20 = (bf16[2,32,5120]{2,1,0:T(8,128)(2,1)}, bf16[2,32,5120]{2,1,0:T(8,128)(2,1)}, u32[]{:S(2)}, u32[]{:S(2)}) collective-permute-start(bf16[2,32,5120]{2,1,0:T(8,128)(2,1)} %bitcast.328), channel_id=1, source_target_pairs={{0,2},{1,3},{2,0},{3,1},{4,6},{5,7},{6,4},{7,5},{8,10},{9,11},{10,... | collective-permute-start | bytes 1966088 | tf_op jit(solution)/shard_map/ppermute | solution.py:949
  542.0 42.4 %collective-permute-start.21 = (bf16[4,32,3584]{2,1,0:T(8,128)(2,1)}, bf16[4,32,3584]{2,1,0:T(8,128)(2,1)S(1)}, u32[]{:S(2)}, u32[]{:S(2)}) collective-permute-start(bf16[4,32,3584]{2,1,0:T(8,128)(2,1)} %bitcast.97), channel_id=1, source_target_pairs={{0,2},{1,3},{2,0},{3,1},{4,6},{5,7},{6,4},{7,5},{8,10},{9,11},{10,... | collective-permute-start | bytes 2752520 | tf_op jit(solution)/shard_map/ppermute | solution.py:949
  551.7 32.6 %collective-permute-start.22 = (bf16[4,32,3072]{2,1,0:T(8,128)(2,1)}, bf16[4,32,3072]{2,1,0:T(8,128)(2,1)S(1)}, u32[]{:S(2)}, u32[]{:S(2)}) collective-permute-start(bf16[4,32,3072]{2,1,0:T(8,128)(2,1)} %bitcast.98), channel_id=1, source_target_pairs={{0,4},{1,5},{2,6},{3,7},{4,0},{5,1},{6,2},{7,3},{8,12},{9,13},{10,... | collective-permute-start | bytes 2359304 | tf_op jit(solution)/shard_map/ppermute | solution.py:949
  553.5 24.7 %collective-permute-start.23 = (bf16[1,32,5120]{2,1,0:T(8,128)(2,1)}, bf16[1,32,5120]{2,1,0:T(8,128)(2,1)S(1)}, u32[]{:S(2)}, u32[]{:S(2)}) collective-permute-start(bf16[1,32,5120]{2,1,0:T(8,128)(2,1)} %bitcast.99), channel_id=1, source_target_pairs={{0,16},{1,17},{2,18},{3,19},{4,20},{5,21},{6,22},{7,23},{8,24},{9,... | collective-permute-start | bytes 983048 | tf_op jit(solution)/shard_map/ppermute | solution.py:949
  555.0 29.3 %collective-permute-start.24 = (bf16[1,32,5120]{2,1,0:T(8,128)(2,1)}, bf16[1,32,5120]{2,1,0:T(8,128)(2,1)S(1)}, u32[]{:S(2)}, u32[]{:S(2)}) collective-permute-start(bf16[1,32,5120]{2,1,0:T(8,128)(2,1)} %bitcast.332), channel_id=1, source_target_pairs={{0,16},{1,17},{2,18},{3,19},{4,20},{5,21},{6,22},{7,23},{8,24},{9,... | collective-permute-start | bytes 983048 | tf_op jit(solution)/shard_map/ppermute | solution.py:949
  561.3 12.1 %collective-permute-start.26 = (bf16[8,32,128]{2,1,0:T(8,128)(2,1)S(1)}, bf16[8,32,128]{2,1,0:T(8,128)(2,1)S(1)}, u32[]{:S(2)}, u32[]{:S(2)}) collective-permute-start(bf16[8,32,128]{2,1,0:T(8,128)(2,1)S(1)} %fusion.5), channel_id=1, source_target_pairs={{0,2},{1,3},{2,0},{3,1},{4,6},{5,7},{6,4},{7,5},{8,10},{9,11},{10,... | collective-permute-start | bytes 196616 | tf_op jit(solution)/shard_map/ppermute | solution.py:949
  588.7 13.5 %collective-permute-start.28 = (bf16[2,32,3584]{2,1,0:T(8,128)(2,1)}, bf16[2,32,3584]{2,1,0:T(8,128)(2,1)S(1)}, u32[]{:S(2)}, u32[]{:S(2)}) collective-permute-start(bf16[2,32,3584]{2,1,0:T(8,128)(2,1)} %bitcast.330), channel_id=1, source_target_pairs={{0,8},{1,9},{2,10},{3,11},{4,12},{5,13},{6,14},{7,15},{8,0},{9,1},... | collective-permute-start | bytes 1376264 | tf_op jit(solution)/shard_map/ppermute | solution.py:949
  588.8 13.4 %collective-permute-start.29 = (bf16[2,32,3072]{2,1,0:T(8,128)(2,1)}, bf16[2,32,3072]{2,1,0:T(8,128)(2,1)S(1)}, u32[]{:S(2)}, u32[]{:S(2)}) collective-permute-start(bf16[2,32,3072]{2,1,0:T(8,128)(2,1)} %bitcast.331), channel_id=1, source_target_pairs={{0,2},{1,3},{2,0},{3,1},{4,6},{5,7},{6,4},{7,5},{8,10},{9,11},{10,... | collective-permute-start | bytes 1179656 | tf_op jit(solution)/shard_map/ppermute | solution.py:949
  605.9 20.5 %collective-permute-start.33 = (bf16[1,32,3584]{2,1,0:T(8,128)(2,1)}, bf16[1,32,3584]{2,1,0:T(8,128)(2,1)S(1)}, u32[]{:S(2)}, u32[]{:S(2)}) collective-permute-start(bf16[1,32,3584]{2,1,0:T(8,128)(2,1)} %bitcast.333), channel_id=1, source_target_pairs={{0,16},{1,17},{2,18},{3,19},{4,20},{5,21},{6,22},{7,23},{8,24},{9,... | collective-permute-start | bytes 688136 | tf_op jit(solution)/shard_map/ppermute | solution.py:949
  607.7 18.7 %collective-permute-start.34 = (bf16[1,32,3072]{2,1,0:T(8,128)(2,1)}, bf16[1,32,3072]{2,1,0:T(8,128)(2,1)S(1)}, u32[]{:S(2)}, u32[]{:S(2)}) collective-permute-start(bf16[1,32,3072]{2,1,0:T(8,128)(2,1)} %bitcast.334), channel_id=1, source_target_pairs={{0,16},{1,17},{2,18},{3,19},{4,20},{5,21},{6,22},{7,23},{8,24},{9,... | collective-permute-start | bytes 589832 | tf_op jit(solution)/shard_map/ppermute | solution.py:949
  612.8 13.5 %collective-permute-start.35 = (bf16[1,32,128]{2,1,0:T(8,128)(2,1)S(1)}, bf16[1,32,128]{2,1,0:T(8,128)(2,1)S(1)}, u32[]{:S(2)}, u32[]{:S(2)}) collective-permute-start(bf16[1,32,128]{2,1,0:T(8,128)(2,1)S(1)} %dynamic-slice_convert_fusion.3), channel_id=1, source_target_pairs={{0,16},{1,17},{2,18},{3,19},{4,20},{5,21},{6,22},{7,23},{8,24},{9,... | collective-permute-start | bytes 24584 | tf_op jit(solution)/shard_map/ppermute | solution.py:949
  (49 other events, 424.4 us)
Sparse Core Ops, SparseCore 0:
  14.0 104.5 all-gather.2
  121.4 138.3 all-gather.4

commit v3 on v2

--- a/solution.py
+++ b/solution.py
@@ -115,7 +115,8 @@
 SMEM = pl.BlockSpec(memory_space=pltpu.SMEM)
 VMEM = pl.BlockSpec(memory_space=pltpu.VMEM)
 CHUNK = 128
-A_KV, A_STATE, A_MERGE, A_INIT, A_VEC, A_END = 0, 2048, 5120, 6144, 6656, 6784
+A_KV, A_STATE, A_MERGE, A_INIT, A_Q, A_VEC, A_END = 0, 2048, 5120, 6144, 6656, 7680, 7808
+W_OUT, W_UP, W_DOWN = 0, 1024, 5120
 B_Q, B_OUT, B_UP, B_DOWN, B_END = 0, 1024, 2048, 6144, 10240
 
 
@@ -299,33 +300,22 @@
     return jnp.concatenate(rows, axis=0)
 
 
-def block_kernel(flags_ref, t_ref, gains_ref, x_hbm, g_hbm, h1_hbm, kv_hbm, ckvq_hbm, wb_hbm,
-                 o_hbm, x1_hbm, h2_hbm, act_hbm, dup_hbm, dx1_hbm, da_hbm, dq_hbm, dkv_hbm, dst_hbm,
-                 db_ref, sums_ref,
-                 x_v, g_v, q_v, kv_v, ckv_v, wo_v, wu_v, wd_v, o_v, x1_v, h2_v, act_v, dup_v,
-                 dh_v, do_v, dq_v, dkv_v, dst_v, lse_v, wq_v, sem):
-    rows, width = x_v.shape
+def token_kernel(flags_ref, t_ref, h1_hbm, kv_hbm, ckvq_hbm, wa_hbm, o_hbm, q_hbm, lse_hbm,
+                 h1_v, q_v, kv_v, ckv_v, wq_v, o_v, lse_v, sem):
+    width = h1_v.shape[1]
     half = HEADS // 2 * HEAD
-    loads = []
+    loads = [(h1_hbm, h1_v)]
     for s in range(2):
         here, there = pl.ds(s * half, half), pl.ds(width + s * half, half)
         loads += [
-            (wb_hbm.at[:, pl.ds(B_Q + s * half, half)], wq_v.at[:, here]),
+            (wa_hbm.at[:, pl.ds(A_Q + s * half, half)], wq_v.at[:, here]),
             (ckvq_hbm.at[:, here], ckv_v.at[:, here]),
             (kv_hbm.at[:, here], kv_v.at[:, here]),
             (ckvq_hbm.at[:, there], ckv_v.at[:, there]),
             (kv_hbm.at[:, there], kv_v.at[:, there]),
         ]
-    loads += [
-        (wb_hbm.at[:, pl.ds(B_OUT, width)], wo_v),
-        (x_hbm, x_v),
-        (g_hbm, g_v),
-        (wb_hbm.at[:, pl.ds(B_UP, 4 * width)], wu_v),
-        (wb_hbm.at[:, pl.ds(B_DOWN, 4 * width)], wd_v),
-    ]
-    h1_in = start_all([(h1_hbm, do_v)], sem, 26)
     begun = start_all(loads, sem)
-    wait_all(h1_in)
+    begun.pop(0).wait()
     nvalid = flags_ref[1]
     units = [(h, part) for h in range(HEADS) for part in range(2)]
     tile_cache = {}
@@ -350,7 +340,7 @@
             s = h // (HEADS // 2)
             wait_all(begun[5 * s :][:5])
             cols = columns(s * half, half)
-            q_v[:, cols] = (dot_nn(do_v[...], wq_v[:, cols]) * Q_SCALE).astype(BF16)
+            q_v[:, cols] = (dot_nn(h1_v[...], wq_v[:, cols]) * Q_SCALE).astype(BF16)
         q = q_v[span, here]
         return dot_nt(ckv_v[:, here], q), dot_nt(kv_v[:used, here], q)
 
@@ -366,7 +356,76 @@
         lse_v[h : h + 1, span] = lse
 
     pipeline(len(units), scores, soft, mix)
-    wait_all(begun[10:12])
+    wait_all(start_all(((o_v, o_hbm), (q_v, q_hbm), (lse_v, lse_hbm)), sem, 11))
+
+
+def token_forward(flags, t, h1, kv, ckvq, wa):
+    rows, width = h1.shape
+    states = ckvq.shape[0]
+    narrow = shape((rows, width), BF16)
+    return pl.pallas_call(
+        token_kernel,
+        in_specs=[SMEM, VMEM] + [HBM] * 4,
+        out_specs=[HBM] * 3,
+        out_shape=[narrow, narrow, shape((HEADS, rows), F32)],
+        scratch_shapes=[
+            pltpu.VMEM((rows, width), BF16),
+            pltpu.VMEM((rows, width), BF16),
+            pltpu.VMEM((rows, 2 * width), BF16),
+            pltpu.VMEM((states, 2 * width), BF16),
+            pltpu.VMEM((width, width), BF16),
+            pltpu.VMEM((rows, width), BF16),
+            pltpu.VMEM((HEADS, rows), F32),
+            pltpu.SemaphoreType.DMA((14,)),
+        ],
+        compiler_params=pltpu.CompilerParams(vmem_limit_bytes=VMEM_LIMIT),
+        cost_estimate=pl.CostEstimate(flops=4 << 30, bytes_accessed=10 * MIB, transcendentals=4 * MIB),
+        name="token_forward",
+    )(flags, t, h1, kv, ckvq, wa)
+
+
+def block_kernel(flags_ref, t_ref, gains_ref, x_hbm, g_hbm, o_hbm, q_hbm, lse_hbm, kv_hbm, ckvq_hbm, wb_hbm,
+                 x1_hbm, h2_hbm, act_hbm, dup_hbm, dx1_hbm, da_hbm, dq_hbm, dkv_hbm, dst_hbm,
+                 db_ref, sums_ref,
+                 x_v, g_v, q_v, kv_v, ckv_v, wo_v, wu_v, wd_v, o_v, x1_v, h2_v, act_v, dup_v,
+                 dh_v, do_v, dq_v, dkv_v, dst_v, lse_v, sem):
+    rows, width = x_v.shape
+    half = HEADS // 2 * HEAD
+    loads = [
+        (o_hbm, o_v),
+        (wb_hbm.at[:, pl.ds(W_OUT, width)], wo_v),
+        (x_hbm, x_v),
+        (g_hbm, g_v),
+        *[
+            (wb_hbm.at[:, pl.ds(base + s * width, width)], ref.at[:, pl.ds(s * width, width)])
+            for s in range(4)
+            for base, ref in ((W_UP, wu_v), (W_DOWN, wd_v))
+        ],
+        (q_hbm, q_v),
+        (ckvq_hbm.at[:, pl.ds(0, 2 * width)], ckv_v),
+        (kv_hbm, kv_v),
+        (lse_hbm, lse_v),
+    ]
+    begun = start_all(loads, sem)
+    nvalid = flags_ref[1]
+    units = [(h, part) for h in range(HEADS) for part in range(2)]
+    tile_cache = {}
+
+    def tiles_of(h, key):
+        if (h, key) not in tile_cache:
+            tile_cache.clear()
+            tile_cache[(h, key)] = bias_tiles(t_ref[h : h + 1, :])
+        return tile_cache[(h, key)]
+
+    def pick(n):
+        h, part = units[n]
+        return h, part, columns(256 * part, 256), 256 * (part + 1), columns(h * HEAD, HEAD), columns(width + h * HEAD, HEAD)
+
+    def masked(scores, h, part, key):
+        scores = scores + bias_part(tiles_of(h, key), part)
+        return jnp.where(row_iota(scores.shape[0], 256) < nvalid, scores, NEG)
+
+    wait_all(begun[:3])
     x1_v[...] = x_v[...].astype(F32) + dot_nn(o_v[...], wo_v[...])
 
     def norm_chunk(span):
@@ -374,12 +433,14 @@
         h2_v[span, :] = (xhat * gains_ref[1:2, :]).astype(BF16)
 
     row_chunks(rows, CHUNK, norm_chunk)
-    outs = start_all(((o_v, o_hbm), (x1_v, x1_hbm), (h2_v, h2_hbm)), sem, 16)
-    wait_all(begun[12:15])
+    outs = start_all(((x1_v, x1_hbm), (h2_v, h2_hbm)), sem, 20)
+    begun[3].wait()
 
     tile = 512
 
     def hidden(i):
+        if i % 2 == 0:
+            wait_all(begun[4 + i : 6 + i])
         slab = wd_v[columns(tile * (i % 2), tile), columns(width * (i // 2), width)]
         return dot_nn(h2_v[...], wu_v[:, columns(tile * i, tile)]), dot_nt(g_v[...], slab)
 
@@ -394,7 +455,7 @@
         dup_v[:, columns(tile * i, tile)] = (dact * slope).astype(BF16)
 
     pipeline(4 * width // tile, hidden, activate, lambda i, nothing: None)
-    outs += start_all(((act_v, act_hbm), (dup_v, dup_hbm)), sem, 19)
+    outs += start_all(((act_v, act_hbm), (dup_v, dup_hbm)), sem, 23)
     dh_v[...] = dot_nt(dup_v[...], wu_v[...])
     sums_ref[...] = jnp.zeros_like(sums_ref)
 
@@ -406,9 +467,10 @@
         sums_ref[0:1, :] += jnp.sum(gain_term, axis=0, keepdims=True)
 
     row_chunks(rows, CHUNK, back_chunk)
-    outs += start_all(((dh_v, dx1_hbm), (x_v, da_hbm)), sem, 21)
+    outs += start_all(((dh_v, dx1_hbm), (x_v, da_hbm)), sem, 25)
     do_v[...] = dot_nt(x_v[...], wo_v[...]).astype(BF16)
 
+    wait_all(begun[12:])
     held = {}
 
     def back_scores(n):
@@ -464,21 +526,20 @@
         dkv_v[256:, there] = terms[3][256:].astype(BF16)
 
     pipeline(len(units), back_scores, back_soft, back_mix)
-    outs += start_all(((dq_v, dq_hbm), (dkv_v, dkv_hbm), (dst_v, dst_hbm)), sem, 23)
+    outs += start_all(((dq_v, dq_hbm), (dkv_v, dkv_hbm), (dst_v, dst_hbm)), sem, 27)
     wait_all(outs)
 
 
-def block_part(flags, t, gains, x, g, h1, kv, ckvq, wb):
+def block_part(flags, t, gains, x, g, o, q, lse, kv, ckvq, wb):
     rows, width = x.shape
     states = ckvq.shape[0]
     hidden = 4 * width
     narrow, wide = shape((rows, width), BF16), shape((rows, width), F32)
     return pl.pallas_call(
         block_kernel,
-        in_specs=[SMEM, VMEM, VMEM] + [HBM] * 6,
-        out_specs=[HBM] * 10 + [VMEM] * 2,
+        in_specs=[SMEM, VMEM, VMEM] + [HBM] * 8,
+        out_specs=[HBM] * 9 + [VMEM] * 2,
         out_shape=[
-            narrow,
             wide,
             narrow,
             shape((rows, hidden), BF16),
@@ -511,13 +572,12 @@
             pltpu.VMEM((rows, 2 * width), BF16),
             pltpu.VMEM((states, 2 * width), BF16),
             pltpu.VMEM((HEADS, rows), F32),
-            pltpu.VMEM((width, width), BF16),
-            pltpu.SemaphoreType.DMA((27,)),
+            pltpu.SemaphoreType.DMA((31,)),
         ],
         compiler_params=pltpu.CompilerParams(vmem_limit_bytes=VMEM_LIMIT),
         cost_estimate=pl.CostEstimate(flops=25 << 30, bytes_accessed=40 * MIB, transcendentals=10 * MIB),
         name="block_part",
-    )(flags, t, gains, x, g, h1, kv, ckvq, wb)
+    )(flags, t, gains, x, g, o, q, lse, kv, ckvq, wb)
 
 
 def retreat_kernel(first, looped, flags_ref, gains_ref, lam_hbm, wa_hbm, kv_hbm, cs_hbm, ckvq_hbm, z_hbm,
@@ -660,7 +720,7 @@
     return out[0], list(out[1:])
 
 
-def input_grad_kernel(gains_ref, x_hbm, dx1_hbm, dq_hbm, one_hbm, two_hbm, wa_hbm, wb_hbm, out_hbm, sums_ref,
+def input_grad_kernel(gains_ref, x_hbm, dx1_hbm, dq_hbm, one_hbm, two_hbm, wa_hbm, out_hbm, sums_ref,
                       x_v, dx_v, dq_v, one_v, two_v, wkv_v, wq_v, dh_v, sem):
     rows, width = x_v.shape
     begun = start_all(
@@ -669,7 +729,7 @@
             (two_hbm, two_v),
             (wa_hbm.at[:, pl.ds(A_KV, 2 * width)], wkv_v),
             (dq_hbm, dq_v),
-            (wb_hbm.at[:, pl.ds(B_Q, width)], wq_v),
+            (wa_hbm.at[:, pl.ds(A_Q, width)], wq_v),
             (x_hbm, x_v),
             (dx1_hbm, dx_v),
         ),
@@ -693,11 +753,11 @@
     pltpu.sync_copy(dx_v, out_hbm)
 
 
-def input_grad(gains, x, dx1, dq, one, two, wa, wb):
+def input_grad(gains, x, dx1, dq, one, two, wa):
     rows, width = x.shape
     return pl.pallas_call(
         input_grad_kernel,
-        in_specs=[VMEM] + [HBM] * 7,
+        in_specs=[VMEM] + [HBM] * 6,
         out_specs=[HBM, VMEM],
         out_shape=[shape((rows, width), F32), shape((8, width), F32)],
         scratch_shapes=[
@@ -714,7 +774,7 @@
         compiler_params=pltpu.CompilerParams(vmem_limit_bytes=VMEM_LIMIT),
         cost_estimate=NO_COST,
         name="input_grad",
-    )(gains, x, dx1, dq, one, two, wa, wb)
+    )(gains, x, dx1, dq, one, two, wa)
 
 
 def dot_tn(a, b):
@@ -835,7 +895,7 @@
         in_specs=[
             pl.BlockSpec((rows, width), lambda i: (0, 0)),
             pl.BlockSpec((rows, width), lambda i: (0, i)),
-            pl.BlockSpec((width, width), lambda i: (0, B_DOWN // width + i)),
+            pl.BlockSpec((width, width), lambda i: (0, W_DOWN // width + i)),
         ],
         out_specs=pl.BlockSpec((rows, width), lambda i: (0, 0)),
         out_shape=shape((rows, width), BF16),
@@ -1133,6 +1193,7 @@
             state_query_weight,
             merge_weight,
             initial_state_learned.T,
+            query_key_value_weight[:, :width],
             small,
         ],
         axis=1,
@@ -1141,7 +1202,6 @@
     down_local = down_weight.reshape(4, share, width).transpose(1, 0, 2)
     wb = jnp.concatenate(
         [
-            query_key_value_weight[:, :width],
             output_weight,
             up_local.reshape(share, 4 * width),
             down_local.reshape(share, 4 * width),
@@ -1182,11 +1242,12 @@
     for to in range(count - 1):
         got = hop(new[to * quarter : (to + 1) * quarter], count - 1, to)
         state_out = jnp.where(place == to, got, state_out)
-    wb, state_out = lax.optimization_barrier((wb, state_out))
+    o, q, lse = token_forward(flags(0), t, h1, kv, ckvq, wa)
+    wb, state_out, o = lax.optimization_barrier((wb, state_out, o))
     state_out = state_out.astype(F32)[None]
 
-    o, x1, h2, act, dup, dx1, da, dq, dkv, dst, dbias, sums_mlp = block_part(
-        flags(0), t, gains, x, g, h1, kv, ckvq, wb
+    x1, h2, act, dup, dx1, da, dq, dkv, dst, dbias, sums_mlp = block_part(
+        flags(0), t, gains, x, g, o, q, lse, kv, ckvq, wb
     )
 
     early_args = (o, da, h1, dq, h2, dup, act, g)
@@ -1284,7 +1345,7 @@
         stream.send, stream.keep = send, keep
     split(late)
     x_grad, sums_attn = together(
-        late + early, lambda zero: input_grad(gains + zero, x, dx1, dq, dkv, dkv_two, wa, wb)
+        late + early, lambda zero: input_grad(gains + zero, x, dx1, dq, dkv, dkv_two, wa)
     )
 
     buckets = jnp.asarray(np.ascontiguousarray(onehot.T))

time: 646 us -> 639 us (0.989)
  waiting for transfers between devices: 289 us -> 277 us
    ppermute x9, waiting for transfers between devices: 116 us -> 99.7 us  [hop(): return lax.ppermute(value, AXES, route)]
    all_gather x1, waiting for transfers between devices: 98.9 us -> 108 us  [body(): wa = lax.all_gather(wa, AXES, axis=0, tiled=True)]
    pallas_call x2 -> x3, Pallas kernels: 57.7 us -> 62.9 us  [the longest x1 39.9 us: block_part(): pl.pallas_call(block_kernel, in_specs=[SMEM, VMEM, VMEM] + [HBM] * 8, out...]
    unnamed x75 -> x76, local copies, waits for them, and re-layouts: 17.7 us -> 18.5 us
  transfers between devices with their start and end apart: 38 -> 38, of which waited for: 16 -> 16; matrix products, arithmetic and copies ran while one was open for 4% -> 4% of each run, Pallas kernels for 22% -> 24%
where the time goes in v3:
time: 639 us; the launch traced here: 633 us
  waiting for transfers between devices  277 us (43%)
  Pallas kernels  232 us (36%)
  starting transfers between devices  55.4 us (9%)
  local copies, waits for them, and re-layouts  33.5 us (5%)
  other arithmetic  17.6 us (3%)
  between operations  16.6 us (3%)
    all_gather x1, waiting for transfers between devices, body(): wa = lax.all_gather(wa, AXES, axis=0, tiled=True)  108 us
    ppermute x9, waiting for transfers between devices, hop(): return lax.ppermute(value, AXES, route)  99.7 us
    pallas_call x14, Pallas kernels, half_sums(): pl.pallas_call(partial(half_kernel, count), in_specs=[SMEM] + [HBM] * (2...  60.2 us
    ppermute x27, waiting for transfers between devices, exchange(): return lax.ppermute(value, AXES, [(i, i ^ bit) for i in range(devices)])  54.1 us
    ppermute x27, starting transfers between devices, exchange(): return lax.ppermute(value, AXES, [(i, i ^ bit) for i in range(devices)])  44.7 us
    pallas_call x1, Pallas kernels, block_part(): pl.pallas_call(block_kernel, in_specs=[SMEM, VMEM, VMEM] + [HBM] * 8, out...  39.9 us
    pallas_call x4, Pallas kernels, retreat(): pl.pallas_call(partial(retreat_kernel, first, looped), in_specs=[SMEM, VM...  28.1 us
    pallas_call x4, Pallas kernels, advance(): pl.pallas_call(kernel, in_specs=[SMEM, VMEM] + [HBM] * (len(args) - 2), o...  27.3 us
  transfers between devices with their start and end apart: 38, of which 16 were waited for; matrix products, arithmetic and copies ran while one was open for 4% of the time, Pallas kernels for 24%

profile of v3, /device:TPU:0, one launch (start us, length us, event | category | flops | bytes accessed | tf_op | source)
XLA Modules:
  0.0 632.9 jit_solution(16428116528538223761)
XLA Ops:
  20.4 108.4 %all-gather.3.cloned.1.call-done.w.wa_hbm = bf16[1024,7808]{1,0:T(8,128)(2,1)} async-done(((bf16[32,7808]{1,0:T(8,128)(2,1)}), bf16[1024,7808]{1,0:T(8,128)(2,1)}) %all-gather.3.cloned.1.call-update) | async-done | bytes 15990800 | tf_op jit(solution)/shard_map/all_gather | solution.py:1211
  131.5 19.1 %advance.4 = (bf16[512,2048]{1,0:T(8,128)(2,1)}, bf16[512,1024]{1,0:T(8,128)(2,1)}, bf16[512,1024]{1,0:T(8,128)(2,1)}, bf16[512,1024]{1,0:T(8,128)(2,1)}, bf16[5...) custom-call(s32[4]{0:T(128)} %add_add_fusion.6.f.flags_ref, ...), custom_call_target="tpu_custom_call" | custom-call | flops 9663676416 | bytes 25165824 | tf_op jit(solution)/shard_map/advance/pallas_call | solution.py:271
  176.0 11.6 %token_forward.1 = (bf16[512,1024]{1,0:T(8,128)(2,1)}, bf16[512,1024]{1,0:T(8,128)(2,1)}, f32[8,512]{1,0:T(8,128)}) custom-call(s32[4]{0:T(128)} %add_add_fusion.6.f.flags_ref, f32[8,512]{1,0:T(8,128)} %fusion.11.t_ref, bf16[512,1024]{1,0:T(8,128)(2,1)} %get-tuple-element.308.h1_hbm.refs_0_, bf16[512,2048]{1,0:T(8,128)(2,1)} %get-tuple-element.286.kv_hbm, ...), custom_call_target="tpu_custom_call" | custom-call | flops 4294967296 | bytes 10485760 | tf_op jit(solution)/shard_map/token_forward/pallas_call | solution.py:366
  187.6 52.9 %collective-permute-done.5 = bf16[128,1024]{1,0:T(8,128)(2,1)S(1)} collective-permute-done((bf16[128,1024]{1,0:T(8,128)(2,1)S(1)}, bf16[128,1024]{1,0:T(8,128)(2,1)S(1)}, u32[]{:S(2)}, u32[]{:S(2)}) %collective-permute-start.5) | collective-permute-done | bytes 262176 | tf_op jit(solution)/shard_map/ppermute | solution.py:1232
  242.4 14.4 %all-gather.5.cloned.1.call-done.wb_hbm.wd_ref = bf16[1024,9216]{1,0:T(8,128)(2,1)} async-done(((bf16[32,9216]{1,0:T(8,128)(2,1)}), bf16[1024,9216]{1,0:T(8,128)(2,1)}) %all-gather.5.cloned.1.call-update) | async-done | bytes 18874384 | tf_op jit(solution)/shard_map/all_gather | solution.py:1212
  256.8 39.9 %block_part.1 = (f32[512,1024]{1,0:T(8,128)}, bf16[512,1024]{1,0:T(8,128)(2,1)}, bf16[512,4096]{1,0:T(8,128)(2,1)}, bf16[512,4096]{1,0:T(8,128)(2,1)}, f32[512,1...) custom-call(s32[4]{0:T(128)} %add_add_fusion.6.f.flags_ref, ...), custom_call_target="tpu_custom_call" | custom-call | flops 26843545600 | bytes 41943040 | tf_op jit(solution)/shard_map/block_part/pallas_call | solution.py:538
  296.6 21.4 %early_grads.2 = (bf16[16,32,5120]{2,1,0:T(8,128)(2,1)}, bf16[16,32,5120]{2,1,0:T(8,128)(2,1)}, bf16[16,32,5120]{2,1,0:T(8,128)(2,1)}, bf16[16,32,5120]{2,1,0:T(8,128)(2,1)}) custom-call(s32[3]{0:T(128)} %get-tuple-element.571.flags_ref, bf16[512,1024]{1,0:T(8,128)(2,1)} %get-tuple-element.311.o_hbm, bf16[512,1024]{1,0:T(8,128)(2,1)} %get-tuple-element.315.da_hbm, ...), custom_call_target="tpu_custom_call" | custom-call | flops 11811160064 | bytes 35651584 | tf_op jit(solution)/shard_map/early_grads/pallas_call | solution.py:860
  324.8 10.1 %layer_output.1 = bf16[512,1024]{1,0:T(8,128)(2,1)} custom-call(f32[512,1024]{1,0:T(8,128)} %get-tuple-element.354.x1_ref, bf16[512,4096]{1,0:T(8,128)(2,1)} %get-tuple-element.319.act_hbm.act_ref, bf16[1024,9216]{1,0:T(8,128)(2,1)} %all-gather.5.cloned.1.call-done.wb_hbm.wd_ref), custom_call_target="tpu_custom_call" | custom-call | flops 4294967296 | bytes 15728640 | tf_op jit(solution)/shard_map/layer_output/pallas_call | solution.py:892
  339.4 6.9 %half_sums.14 = (bf16[4,2,32,5120]{3,2,1,0:T(8,128)(2,1)}, bf16[2,4,32,5120]{3,2,1,0:T(8,128)(2,1)}) custom-call(s32[2]{0:T(128)} %get-tuple-element.573.which_ref, bf16[4,2,2,32,5120]{4,3,2,1,0:T(8,128)(2,1)} %bitcast.232, bf16[4,2,2,32,5120]{4,3,2,1,0:T(8,128)(2,1)} %bitcast.27.refs_1_, bf16[2,2,4,32,5120]{4,3,2,1,0:T(8,128)(2,1)} %bitcast.234, ...), custom_call_target="tpu_custom_call" | custom-call | tf_op jit(solution)/shard_map/half_sums/pallas_call | solution.py:1062
  351.0 6.9 %half_sums.15 = (bf16[4,2,32,5120]{3,2,1,0:T(8,128)(2,1)}, bf16[2,4,32,5120]{3,2,1,0:T(8,128)(2,1)}) custom-call(s32[2]{0:T(128)} %get-tuple-element.575.which_ref, bf16[4,2,2,32,5120]{4,3,2,1,0:T(8,128)(2,1)} %bitcast.233, bf16[4,2,2,32,5120]{4,3,2,1,0:T(8,128)(2,1)} %bitcast.35.refs_1_, bf16[2,2,4,32,5120]{4,3,2,1,0:T(8,128)(2,1)} %bitcast.235, ...), custom_call_target="tpu_custom_call" | custom-call | tf_op jit(solution)/shard_map/half_sums/pallas_call | solution.py:1062
  358.0 45.0 %collective-permute-done.10.lam_hbm = bf16[512,1024]{1,0:T(8,128)(2,1)S(1)} collective-permute-done((bf16[512,1024]{1,0:T(8,128)(2,1)}, bf16[512,1024]{1,0:T(8,128)(2,1)S(1)}, u32[]{:S(2)}, u32[]{:S(2)}) %collective-permute-start.10) | collective-permute-done | bytes 1048608 | tf_op jit(solution)/shard_map/ppermute | solution.py:1232
  403.9 25.2 %retreat.7 = (bf16[512,1024]{1,0:T(8,128)(2,1)}, bf16[512,1024]{1,0:T(8,128)(2,1)}, bf16[512,3072]{1,0:T(8,128)(2,1)}, bf16[512,2048]{1,0:T(8,128)(2,1)}, f32[8,1024]{1,0:T(8,128)}) custom-call(s32[4]{0:T(128)} %add_add_fusion.6.f.flags_ref, ...), custom_call_target="tpu_custom_call", output_to_operand_aliasing={{1}: (10, {}), {2}: (11, {}), {3}: (12, {}), {4}: (13, {})} | custom-call | flops 13958643712 | bytes 33554432 | tf_op jit(solution)/shard_map/retreat/pallas_call | solution.py:685
  437.9 9.0 %late_grads.2 = (bf16[512,3584]{1,0:T(8,128)(2,1)}, bf16[512,3584]{1,0:T(8,128)(2,1)}) custom-call(s32[4]{0:T(128)} %add_add_fusion.6.f.flags_ref, bf16[512,1024]{1,0:T(8,128)(2,1)} %get-tuple-element.404.refs_0_, bf16[512,3072]{1,0:T(8,128)(2,1)} %get-tuple-element.405.refs_1_, bf16[512,1024]{1,0:T(8,128)(2,1)} %get-tuple-element.406.refs_2_), custom_call_target="tpu_custom_call" | custom-call | tf_op jit(solution)/shard_map/late_grads/pallas_call | solution.py:963
  446.9 9.3 %late_grads.3 = (bf16[512,3072]{1,0:T(8,128)(2,1)}, bf16[512,3072]{1,0:T(8,128)(2,1)}) custom-call(s32[4]{0:T(128)} %add_add_fusion.6.f.flags_ref, bf16[512,1024]{1,0:T(8,128)(2,1)} %get-tuple-element.308.h1_hbm.refs_0_, bf16[512,2048]{1,0:T(8,128)(2,1)} %get-tuple-element.409.refs_1_.one_hbm, bf16[512,2048]{1,0:T(8,128)(2,1)} %get-tuple-element.410.refs_2_.two_hbm, ...), custom_call_target="tpu_custom_call" | custom-call | tf_op jit(solution)/shard_map/late_grads/pallas_call | solution.py:963
  474.8 5.5 half_sums.20
  483.6 15.5 %collective-permute-start.19 = (bf16[2,32,5120]{2,1,0:T(8,128)(2,1)}, bf16[2,32,5120]{2,1,0:T(8,128)(2,1)S(1)}, u32[]{:S(2)}, u32[]{:S(2)}) collective-permute-start(bf16[2,32,5120]{2,1,0:T(8,128)(2,1)} %bitcast.329), channel_id=1, source_target_pairs={{0,2},{1,3},{2,0},{3,1},{4,6},{5,7},{6,4},{7,5},{8,10},{9,11},{10,... | collective-permute-start | bytes 1966088 | tf_op jit(solution)/shard_map/ppermute | solution.py:1009
  502.4 5.5 half_sums.21
  508.6 11.4 %input_grad.1 = (f32[512,1024]{1,0:T(8,128)}, f32[8,1024]{1,0:T(8,128)}) custom-call(f32[8,1024]{1,0:T(8,128)} %broadcast_add_fusion.gains_ref, bf16[512,1024]{1,0:T(8,128)(2,1)} %bitcast.290, f32[512,1024]{1,0:T(8,128)} %get-tuple-element.453.dx1_hbm, bf16[512,1024]{1,0:T(8,128)(2,1)} %get-tuple-element.316.dq_hbm, ...), custom_call_target="tpu_custom_call" | custom-call | tf_op jit(solution)/shard_map/input_grad/pallas_call | solution.py:758
  520.1 8.0 %collective-permute-done.20 = bf16[2,32,5120]{2,1,0:T(8,128)(2,1)} collective-permute-done((bf16[2,32,5120]{2,1,0:T(8,128)(2,1)}, bf16[2,32,5120]{2,1,0:T(8,128)(2,1)}, u32[]{:S(2)}, u32[]{:S(2)}) %collective-permute-start.20) | collective-permute-done | bytes 655392 | tf_op jit(solution)/shard_map/ppermute | solution.py:1009
  534.6 9.8 %collective-permute-start.21 = (bf16[4,32,3584]{2,1,0:T(8,128)(2,1)}, bf16[4,32,3584]{2,1,0:T(8,128)(2,1)S(1)}, u32[]{:S(2)}, u32[]{:S(2)}) collective-permute-start(bf16[4,32,3584]{2,1,0:T(8,128)(2,1)} %bitcast.97), channel_id=1, source_target_pairs={{0,2},{1,3},{2,0},{3,1},{4,6},{5,7},{6,4},{7,5},{8,10},{9,11},{10,... | collective-permute-start | bytes 2752520 | tf_op jit(solution)/shard_map/ppermute | solution.py:1009
  554.1 11.9 %collective-permute-done.26 = bf16[8,32,128]{2,1,0:T(8,128)(2,1)S(1)} collective-permute-done((bf16[8,32,128]{2,1,0:T(8,128)(2,1)S(1)}, bf16[8,32,128]{2,1,0:T(8,128)(2,1)S(1)}, u32[]{:S(2)}, u32[]{:S(2)}) %collective-permute-start.26) | collective-permute-done | bytes 65568 | tf_op jit(solution)/shard_map/ppermute | solution.py:1009
  570.9 6.1 collective-permute-done.24
  588.5 5.3 collective-permute-done.31
  609.9 9.1 %collective-permute-done.35 = bf16[1,32,128]{2,1,0:T(8,128)(2,1)S(1)} collective-permute-done((bf16[1,32,128]{2,1,0:T(8,128)(2,1)S(1)}, bf16[1,32,128]{2,1,0:T(8,128)(2,1)S(1)}, u32[]{:S(2)}, u32[]{:S(2)}) %collective-permute-start.35) | collective-permute-done | bytes 8224 | tf_op jit(solution)/shard_map/ppermute | solution.py:1009
  (238 shorter events, 148.2 us)
Async XLA Ops:
  7.2 121.7 %all-gather.3.cloned.1.call-start = ((), (), s32[]{:S(2)}) async-start(), calls=%async_computation | async-start | bytes 16490496 | tf_op jit(solution)/shard_map/all_gather | solution.py:1211
  14.7 242.1 %all-gather.5.cloned.1.call-start = ((), (), s32[]{:S(2)}) async-start(), calls=%async_computation.1 | async-start | bytes 19464192 | tf_op jit(solution)/shard_map/all_gather | solution.py:1212
  170.9 16.7 %collective-permute-start.3 = (bf16[128,1024]{1,0:T(8,128)(2,1)S(1)}, bf16[128,1024]{1,0:T(8,128)(2,1)S(1)}, u32[]{:S(2)}, u32[]{:S(2)}) collective-permute-start(bf16[128,1024]{1,0:T(8,128)(2,1)S(1)} %get-tuple-element.560), channel_id=1, source_target_pairs={{3,2},{7,6},{11,10},{15,14},{19,18},{23,22},{27,26},{31,30}} | collective-permute-start | bytes 786440 | tf_op jit(solution)/shard_map/ppermute | solution.py:1232
  171.6 16.0 %collective-permute-start.4 = (bf16[128,1024]{1,0:T(8,128)(2,1)S(1)}, bf16[128,1024]{1,0:T(8,128)(2,1)S(1)}, u32[]{:S(2)}, u32[]{:S(2)}) collective-permute-start(bf16[128,1024]{1,0:T(8,128)(2,1)S(1)} %get-tuple-element.559), channel_id=1, source_target_pairs={{3,1},{7,5},{11,9},{15,13},{19,17},{23,21},{27,25},{31,29}} | collective-permute-start | bytes 786440 | tf_op jit(solution)/shard_map/ppermute | solution.py:1232
  172.3 68.3 %collective-permute-start.5 = (bf16[128,1024]{1,0:T(8,128)(2,1)S(1)}, bf16[128,1024]{1,0:T(8,128)(2,1)S(1)}, u32[]{:S(2)}, u32[]{:S(2)}) collective-permute-start(bf16[128,1024]{1,0:T(8,128)(2,1)S(1)} %get-tuple-element.558), channel_id=1, source_target_pairs={{3,0},{7,4},{11,8},{15,12},{19,16},{23,20},{27,24},{31,28}} | collective-permute-start | bytes 786440 | tf_op jit(solution)/shard_map/ppermute | solution.py:1232
  323.1 16.2 %collective-permute-start.8 = (bf16[16,32,5120]{2,1,0:T(8,128)(2,1)}, bf16[16,32,5120]{2,1,0:T(8,128)(2,1)}, u32[]{:S(2)}, u32[]{:S(2)}) collective-permute-start(bf16[16,32,5120]{2,1,0:T(8,128)(2,1)} %get-tuple-element.356), channel_id=1, source_target_pairs={{0,1},{1,0},{2,3},{3,2},{4,5},{5,4},{6,7},{7,6},{8,9},{9,8},{10,11... | collective-permute-start | bytes 15728648 | tf_op jit(solution)/shard_map/ppermute | solution.py:1009
  323.4 22.9 %collective-permute-start.9 = (bf16[512,1024]{1,0:T(8,128)(2,1)}, bf16[512,1024]{1,0:T(8,128)(2,1)S(1)}, u32[]{:S(2)}, u32[]{:S(2)}) collective-permute-start(bf16[512,1024]{1,0:T(8,128)(2,1)} %get-tuple-element.359), channel_id=1, source_target_pairs={{2,1},{6,5},{10,9},{14,13},{18,17},{22,21},{26,25},{30,29}} | collective-permute-start | bytes 3145736 | tf_op jit(solution)/shard_map/ppermute | solution.py:1232
  346.3 82.9 %collective-permute-start.11 = (bf16[8,32,5120]{2,1,0:T(8,128)(2,1)}, bf16[8,32,5120]{2,1,0:T(8,128)(2,1)S(1)}, u32[]{:S(2)}, u32[]{:S(2)}) collective-permute-start(bf16[8,32,5120]{2,1,0:T(8,128)(2,1)} %bitcast.317), channel_id=1, source_target_pairs={{0,4},{1,5},{2,6},{3,7},{4,0},{5,1},{6,2},{7,3},{8,12},{9,13},{10,... | collective-permute-start | bytes 7864328 | tf_op jit(solution)/shard_map/ppermute | solution.py:1009
  347.8 81.4 %collective-permute-start.12 = (bf16[8,32,5120]{2,1,0:T(8,128)(2,1)}, bf16[8,32,5120]{2,1,0:T(8,128)(2,1)}, u32[]{:S(2)}, u32[]{:S(2)}) collective-permute-start(bf16[8,32,5120]{2,1,0:T(8,128)(2,1)} %bitcast.316), channel_id=1, source_target_pairs={{0,8},{1,9},{2,10},{3,11},{4,12},{5,13},{6,14},{7,15},{8,0},{9,1},... | collective-permute-start | bytes 7864328 | tf_op jit(solution)/shard_map/ppermute | solution.py:1009
  349.1 53.9 %collective-permute-start.10 = (bf16[512,1024]{1,0:T(8,128)(2,1)}, bf16[512,1024]{1,0:T(8,128)(2,1)S(1)}, u32[]{:S(2)}, u32[]{:S(2)}) collective-permute-start(bf16[512,1024]{1,0:T(8,128)(2,1)} %get-tuple-element.372), channel_id=1, source_target_pairs={{1,0},{5,4},{9,8},{13,12},{17,16},{21,20},{25,24},{29,28}} | collective-permute-start | bytes 3145736 | tf_op jit(solution)/shard_map/ppermute | solution.py:1232
  435.3 25.5 %collective-permute-start.13 = (bf16[4,32,5120]{2,1,0:T(8,128)(2,1)}, bf16[4,32,5120]{2,1,0:T(8,128)(2,1)S(1)}, u32[]{:S(2)}, u32[]{:S(2)}) collective-permute-start(bf16[4,32,5120]{2,1,0:T(8,128)(2,1)} %bitcast.324), channel_id=1, source_target_pairs={{0,8},{1,9},{2,10},{3,11},{4,12},{5,13},{6,14},{7,15},{8,0},{9,1},... | collective-permute-start | bytes 3932168 | tf_op jit(solution)/shard_map/ppermute | solution.py:1009
  436.5 24.4 %collective-permute-start.14 = (bf16[4,32,5120]{2,1,0:T(8,128)(2,1)}, bf16[4,32,5120]{2,1,0:T(8,128)(2,1)S(1)}, u32[]{:S(2)}, u32[]{:S(2)}) collective-permute-start(bf16[4,32,5120]{2,1,0:T(8,128)(2,1)} %bitcast.323), channel_id=1, source_target_pairs={{0,4},{1,5},{2,6},{3,7},{4,0},{5,1},{6,2},{7,3},{8,12},{9,13},{10,... | collective-permute-start | bytes 3932168 | tf_op jit(solution)/shard_map/ppermute | solution.py:1009
  480.2 47.9 %collective-permute-start.17 = (bf16[8,32,3584]{2,1,0:T(8,128)(2,1)}, bf16[8,32,3584]{2,1,0:T(8,128)(2,1)S(1)}, u32[]{:S(2)}, u32[]{:S(2)}) collective-permute-start(bf16[8,32,3584]{2,1,0:T(8,128)(2,1)} %bitcast.320), channel_id=1, source_target_pairs={{0,4},{1,5},{2,6},{3,7},{4,0},{5,1},{6,2},{7,3},{8,12},{9,13},{10,... | collective-permute-start | bytes 5505032 | tf_op jit(solution)/shard_map/ppermute | solution.py:1009
  480.9 47.2 %collective-permute-start.18 = (bf16[8,32,3072]{2,1,0:T(8,128)(2,1)}, bf16[8,32,3072]{2,1,0:T(8,128)(2,1)}, u32[]{:S(2)}, u32[]{:S(2)}) collective-permute-start(bf16[8,32,3072]{2,1,0:T(8,128)(2,1)} %bitcast.322), channel_id=1, source_target_pairs={{0,8},{1,9},{2,10},{3,11},{4,12},{5,13},{6,14},{7,15},{8,0},{9,1},... | collective-permute-start | bytes 4718600 | tf_op jit(solution)/shard_map/ppermute | solution.py:1009
  483.6 36.5 %collective-permute-start.19 = (bf16[2,32,5120]{2,1,0:T(8,128)(2,1)}, bf16[2,32,5120]{2,1,0:T(8,128)(2,1)S(1)}, u32[]{:S(2)}, u32[]{:S(2)}) collective-permute-start(bf16[2,32,5120]{2,1,0:T(8,128)(2,1)} %bitcast.329), channel_id=1, source_target_pairs={{0,2},{1,3},{2,0},{3,1},{4,6},{5,7},{6,4},{7,5},{8,10},{9,11},{10,... | collective-permute-start | bytes 1966088 | tf_op jit(solution)/shard_map/ppermute | solution.py:1009
  499.1 29.1 %collective-permute-start.20 = (bf16[2,32,5120]{2,1,0:T(8,128)(2,1)}, bf16[2,32,5120]{2,1,0:T(8,128)(2,1)}, u32[]{:S(2)}, u32[]{:S(2)}) collective-permute-start(bf16[2,32,5120]{2,1,0:T(8,128)(2,1)} %bitcast.328), channel_id=1, source_target_pairs={{0,2},{1,3},{2,0},{3,1},{4,6},{5,7},{6,4},{7,5},{8,10},{9,11},{10,... | collective-permute-start | bytes 1966088 | tf_op jit(solution)/shard_map/ppermute | solution.py:1009
  534.6 42.4 %collective-permute-start.21 = (bf16[4,32,3584]{2,1,0:T(8,128)(2,1)}, bf16[4,32,3584]{2,1,0:T(8,128)(2,1)S(1)}, u32[]{:S(2)}, u32[]{:S(2)}) collective-permute-start(bf16[4,32,3584]{2,1,0:T(8,128)(2,1)} %bitcast.97), channel_id=1, source_target_pairs={{0,2},{1,3},{2,0},{3,1},{4,6},{5,7},{6,4},{7,5},{8,10},{9,11},{10,... | collective-permute-start | bytes 2752520 | tf_op jit(solution)/shard_map/ppermute | solution.py:1009
  544.4 32.6 %collective-permute-start.22 = (bf16[4,32,3072]{2,1,0:T(8,128)(2,1)}, bf16[4,32,3072]{2,1,0:T(8,128)(2,1)S(1)}, u32[]{:S(2)}, u32[]{:S(2)}) collective-permute-start(bf16[4,32,3072]{2,1,0:T(8,128)(2,1)} %bitcast.98), channel_id=1, source_target_pairs={{0,4},{1,5},{2,6},{3,7},{4,0},{5,1},{6,2},{7,3},{8,12},{9,13},{10,... | collective-permute-start | bytes 2359304 | tf_op jit(solution)/shard_map/ppermute | solution.py:1009
  546.2 24.7 %collective-permute-start.23 = (bf16[1,32,5120]{2,1,0:T(8,128)(2,1)}, bf16[1,32,5120]{2,1,0:T(8,128)(2,1)S(1)}, u32[]{:S(2)}, u32[]{:S(2)}) collective-permute-start(bf16[1,32,5120]{2,1,0:T(8,128)(2,1)} %bitcast.99), channel_id=1, source_target_pairs={{0,16},{1,17},{2,18},{3,19},{4,20},{5,21},{6,22},{7,23},{8,24},{9,... | collective-permute-start | bytes 983048 | tf_op jit(solution)/shard_map/ppermute | solution.py:1009
  547.7 29.3 %collective-permute-start.24 = (bf16[1,32,5120]{2,1,0:T(8,128)(2,1)}, bf16[1,32,5120]{2,1,0:T(8,128)(2,1)S(1)}, u32[]{:S(2)}, u32[]{:S(2)}) collective-permute-start(bf16[1,32,5120]{2,1,0:T(8,128)(2,1)} %bitcast.332), channel_id=1, source_target_pairs={{0,16},{1,17},{2,18},{3,19},{4,20},{5,21},{6,22},{7,23},{8,24},{9,... | collective-permute-start | bytes 983048 | tf_op jit(solution)/shard_map/ppermute | solution.py:1009
  581.4 13.4 %collective-permute-start.28 = (bf16[2,32,3584]{2,1,0:T(8,128)(2,1)}, bf16[2,32,3584]{2,1,0:T(8,128)(2,1)S(1)}, u32[]{:S(2)}, u32[]{:S(2)}) collective-permute-start(bf16[2,32,3584]{2,1,0:T(8,128)(2,1)} %bitcast.330), channel_id=1, source_target_pairs={{0,8},{1,9},{2,10},{3,11},{4,12},{5,13},{6,14},{7,15},{8,0},{9,1},... | collective-permute-start | bytes 1376264 | tf_op jit(solution)/shard_map/ppermute | solution.py:1009
  598.4 20.5 %collective-permute-start.33 = (bf16[1,32,3584]{2,1,0:T(8,128)(2,1)}, bf16[1,32,3584]{2,1,0:T(8,128)(2,1)S(1)}, u32[]{:S(2)}, u32[]{:S(2)}) collective-permute-start(bf16[1,32,3584]{2,1,0:T(8,128)(2,1)} %bitcast.333), channel_id=1, source_target_pairs={{0,16},{1,17},{2,18},{3,19},{4,20},{5,21},{6,22},{7,23},{8,24},{9,... | collective-permute-start | bytes 688136 | tf_op jit(solution)/shard_map/ppermute | solution.py:1009
  600.3 18.7 %collective-permute-start.34 = (bf16[1,32,3072]{2,1,0:T(8,128)(2,1)}, bf16[1,32,3072]{2,1,0:T(8,128)(2,1)S(1)}, u32[]{:S(2)}, u32[]{:S(2)}) collective-permute-start(bf16[1,32,3072]{2,1,0:T(8,128)(2,1)} %bitcast.334), channel_id=1, source_target_pairs={{0,16},{1,17},{2,18},{3,19},{4,20},{5,21},{6,22},{7,23},{8,24},{9,... | collective-permute-start | bytes 589832 | tf_op jit(solution)/shard_map/ppermute | solution.py:1009
  605.4 13.6 %collective-permute-start.35 = (bf16[1,32,128]{2,1,0:T(8,128)(2,1)S(1)}, bf16[1,32,128]{2,1,0:T(8,128)(2,1)S(1)}, u32[]{:S(2)}, u32[]{:S(2)}) collective-permute-start(bf16[1,32,128]{2,1,0:T(8,128)(2,1)S(1)} %dynamic-slice_convert_fusion.3), channel_id=1, source_target_pairs={{0,16},{1,17},{2,18},{3,19},{4,20},{5,21},{6,22},{7,23},{8,24},{9,... | collective-permute-start | bytes 24584 | tf_op jit(solution)/shard_map/ppermute | solution.py:1009
  (48 other events, 443.8 us)
Sparse Core Ops, SparseCore 0:
  14.8 113.9 all-gather.2
  131.8 124.9 all-gather.4
